TPU v7x, 256 devices: a whole 4x4x8 slice. The times are simulated.
256 devices in a mesh: chan: 8 (over z_hi, x), depth: 32 (over z_lo, y, core).
Axes of the slice: x: 4, y: 4, z: 8 (z_hi: 2, z_lo: 4; z = z_hi * 4 + z_lo), core: 2. Of those that a mesh axis runs over, the one named last changes fastest.
Arguments:
- volume: float32 [256, 32, 16, 128], P('chan', 'depth'), may hold values from -6 to 6
- kernel: float32 [3, 3, 3, 256, 256], P(None, None, None, 'chan'), may hold values from -0.078125 to 0.078125
Outputs:
- response: float32 [256, 32, 16, 128], P('chan', 'depth')
All inputs are finite; a program needn't handle non-finite values.
Results may differ from a plain program's by a relative error of at most 0.0001.
Values sent between devices are 32-bit elements; how exact they have to be, the bound alone decides.
No kernel may reach another device: no remote copies, remote signals or barrier semaphores. Data moves between devices by JAX's collectives and lax.ppermute only.
A program may use at most 128 MiB of HBM per device.

v0:
```python
import jax
import jax.numpy as jnp
from jax import lax
from jax.sharding import PartitionSpec as P


def with_halo(block, sides, width):
    for axis, dim in sides:
        count = lax.axis_size(axis)
        forward = [(i, i + 1) for i in range(count - 1)]
        backward = [(target, source) for source, target in forward]
        low = lax.ppermute(
            lax.slice_in_dim(block, block.shape[dim] - width, None, axis=dim), axis, forward
        )
        high = lax.ppermute(lax.slice_in_dim(block, 0, width, axis=dim), axis, backward)
        block = jnp.concatenate([low, block, high], axis=dim)
    return block


def spread(volume, taps):
    channels, planes, height, across = volume.shape
    filters = taps.shape[2]
    framed = jnp.pad(volume, ((0, 0), (0, 0), (1, 1), (0, 0)))
    running = jnp.zeros((filters, planes, height, across), jnp.float32)
    for row_tap in range(3):
        column_slab = framed[:, :, row_tap : row_tap + height, :].reshape(
            channels, planes * height * across
        )
        products = jnp.dot(
            taps[row_tap].reshape(3 * filters, channels),
            column_slab,
            precision=lax.Precision.HIGHEST,
            preferred_element_type=jnp.float32,
        )
        products = products.reshape(3, filters, planes, height, across)
        lower_tap = jnp.pad(products[0], ((0, 0), (0, 0), (0, 0), (1, 0)))[..., :across]
        upper_tap = jnp.pad(products[2], ((0, 0), (0, 0), (0, 0), (0, 1)))[..., 1:]
        running = running + products[1] + lower_tap + upper_tap
    return running


def convolve(padded, taps):
    planes = padded.shape[1] - 2
    response = spread(padded[:, 0:planes], taps[0])
    for depth_tap in range(1, 3):
        response = response + spread(padded[:, depth_tap : depth_tap + planes], taps[depth_tap])
    return response


def local(volume, kernel):
    gathered = lax.all_gather(volume, "chan", axis=0, tiled=True)
    padded = with_halo(gathered, (("depth", 1),), 1)
    return convolve(padded, kernel)


def solution(mesh):
    return jax.shard_map(
        local,
        mesh=mesh,
        in_specs=(P("chan", "depth", None, None), P(None, None, None, "chan", None)),
        out_specs=P("chan", "depth", None, None),
        check_vma=False,
    )
```

profile of v0, /device:TPU:1, one launch (start us, length us, event | category | flops | bytes accessed | tf_op | source)
XLA Modules:
  0.0 145.1 jit_solution(16568102281106702512)
XLA Ops:
  6.5 0.0 all-gather.2.cloned.1.call-start
  6.5 0.7 all-gather.2.cloned.1.call-update
  7.3 81.4 %all-gather.2.cloned.1.call-done = f32[256,1,16,128]{3,2,1,0:T(8,128)} async-done(((f32[32,1,16,128]{3,2,1,0:T(8,128)}), f32[256,1,16,128]{3,2,1,0:T(8,128)}) %all-gather.2.cloned.1.call-update) | async-done | bytes 2097168 | tf_op jit(solution)/shard_map/all_gather | solution.py:51
  88.7 5.0 %collective-permute-start = (f32[256,1,16,128]{3,2,1,0:T(8,128)}, f32[256,1,16,128]{3,2,1,0:T(8,128)S(1)}, u32[]{:S(2)}, u32[]{:S(2)}) collective-permute-start(f32[256,1,16,128]{3,2,1,0:T(8,128)} %all-gather.2.cloned.1.call-done), channel_id=1, source_target_pairs={{0,1},{1,2},{2,3},{3,4},{4,5},{5,6},{6,7},{7,8},{8,9},{9,10},{10,1... | collective-permute-start | bytes 6291464 | tf_op jit(solution)/shard_map/ppermute | solution.py:12
  93.6 1.3 fusion.47
  95.0 2.6 %pad_slice_fusion.2 = (f32[256,1,16,128]{3,2,1,0:T(8,128)S(1)}, f32[256,1,16,128]{3,2,1,0:T(8,128)S(1)}) fusion(f32[256,1,16,128]{3,2,1,0:T(8,128)} %all-gather.2.cloned.1.call-done), kind=kLoop, calls=%fused_computation.2 | loop fusion | bytes 6291456 | tf_op jit(solution)/shard_map/slice | solution.py:26
  97.6 0.0 copy-start
  97.6 1.9 %convolution_bitcast_fusion.3 = f32[96,2048]{1,0:T(8,128)S(1)} fusion(f32[96,256]{1,0:T(8,128)S(1)} %bitcast.308, f32[32,8,16,128]{3,2,1,0:T(8,128)S(1)} %bitcast.279), kind=kOutput, calls=%fused_computation.9 | convolution fusion | flops 603979776 | bytes 2981888 | tf_op jit(solution)/shard_map/dot_general | solution.py:29
  99.5 0.1 slice_bitcast_fusion.17
  99.7 0.0 copy-done
  99.7 1.9 %fusion.9 = f32[96,2048]{1,0:T(8,128)S(1)} fusion(f32[96,256]{1,0:T(8,128)S(1)} %bitcast.307, f32[32,8,16,128]{3,2,1,0:T(8,128)S(1)} %bitcast.273), kind=kOutput, calls=%fused_computation.21 | convolution fusion | flops 603979776 | bytes 2981888 | tf_op jit(solution)/shard_map/dot_general | solution.py:29
  101.6 0.1 slice_bitcast_fusion.14
  101.7 2.1 %collective-permute-start.1 = (f32[256,1,16,128]{3,2,1,0:T(8,128)S(1)}, f32[256,1,16,128]{3,2,1,0:T(8,128)S(1)}, u32[]{:S(2)}, u32[]{:S(2)}) collective-permute-start(f32[256,1,16,128]{3,2,1,0:T(8,128)S(1)} %copy-done), channel_id=1, source_target_pairs={{1,0},{2,1},{3,2},{4,3},{5,4},{6,5},{7,6},{8,7},{9,8},{10,9},{11,1... | collective-permute-start | bytes 6291464 | tf_op jit(solution)/shard_map/ppermute | solution.py:15
  103.8 1.9 %convolution_bitcast_fusion.2 = f32[96,2048]{1,0:T(8,128)S(1)} fusion(f32[96,256]{1,0:T(8,128)S(1)} %bitcast.306, f32[32,8,16,128]{3,2,1,0:T(8,128)S(1)} %bitcast.276), kind=kOutput, calls=%fused_computation.8 | convolution fusion | flops 603979776 | bytes 2981888 | tf_op jit(solution)/shard_map/dot_general | solution.py:29
  105.8 0.1 slice_bitcast_fusion.11
  106.1 10.8 %collective-permute-done = f32[256,1,16,128]{3,2,1,0:T(8,128)S(1)} collective-permute-done((f32[256,1,16,128]{3,2,1,0:T(8,128)}, f32[256,1,16,128]{3,2,1,0:T(8,128)S(1)}, u32[]{:S(2)}, u32[]{:S(2)}) %collective-permute-start) | collective-permute-done | bytes 2097184 | tf_op jit(solution)/shard_map/ppermute | solution.py:12
  116.9 0.4 pad_slice_fusion.4
  117.3 1.9 %convolution_bitcast_fusion.5 = f32[96,2048]{1,0:T(8,128)S(1)} fusion(f32[96,256]{1,0:T(8,128)S(1)} %bitcast.305, f32[32,8,16,128]{3,2,1,0:T(8,128)S(1)} %bitcast.280), kind=kOutput, calls=%fused_computation.11 | convolution fusion | flops 603979776 | bytes 2981888 | tf_op jit(solution)/shard_map/dot_general | solution.py:29
  119.2 0.1 slice_bitcast_fusion.26
  119.4 1.9 %fusion.16 = f32[96,2048]{1,0:T(8,128)S(1)} fusion(f32[96,256]{1,0:T(8,128)S(1)} %bitcast.304, f32[32,8,16,128]{3,2,1,0:T(8,128)S(1)} %bitcast.275), kind=kOutput, calls=%fused_computation.28 | convolution fusion | flops 603979776 | bytes 2981888 | tf_op jit(solution)/shard_map/dot_general | solution.py:29
  121.3 0.1 slice_bitcast_fusion.23
  121.4 1.9 %convolution_bitcast_fusion.4 = f32[96,2048]{1,0:T(8,128)S(1)} fusion(f32[96,256]{1,0:T(8,128)S(1)} %bitcast.303, f32[32,8,16,128]{3,2,1,0:T(8,128)S(1)} %bitcast.278), kind=kOutput, calls=%fused_computation.10 | convolution fusion | flops 603979776 | bytes 2981888 | tf_op jit(solution)/shard_map/dot_general | solution.py:29
  123.4 0.1 slice_bitcast_fusion.20
  123.5 5.5 %collective-permute-done.1 = f32[256,1,16,128]{3,2,1,0:T(8,128)S(1)} collective-permute-done((f32[256,1,16,128]{3,2,1,0:T(8,128)S(1)}, f32[256,1,16,128]{3,2,1,0:T(8,128)S(1)}, u32[]{:S(2)}, u32[]{:S(2)}) %collective-permute-start.1) | collective-permute-done | bytes 2097184 | tf_op jit(solution)/shard_map/ppermute | solution.py:15
  129.1 0.4 pad_slice_fusion
  129.5 1.9 %convolution_bitcast_fusion.1 = f32[96,2048]{1,0:T(8,128)S(1)} fusion(f32[96,256]{1,0:T(8,128)S(1)} %bitcast.302, f32[32,8,16,128]{3,2,1,0:T(8,128)S(1)} %bitcast.281), kind=kOutput, calls=%fused_computation.7 | convolution fusion | flops 603979776 | bytes 2981888 | tf_op jit(solution)/shard_map/dot_general | solution.py:29
  131.4 0.1 slice_bitcast_fusion.8
  131.6 2.1 %fusion.2 = f32[96,2048]{1,0:T(8,128)S(1)} fusion(f32[96,256]{1,0:T(8,128)S(1)} %bitcast.301, f32[32,8,16,128]{3,2,1,0:T(8,128)S(1)} %bitcast.274), kind=kOutput, calls=%fused_computation.14 | convolution fusion | flops 603979776 | bytes 2981888 | tf_op jit(solution)/shard_map/dot_general | solution.py:29
  133.6 0.1 slice_bitcast_fusion.5
  133.8 1.9 %convolution_bitcast_fusion = f32[96,2048]{1,0:T(8,128)S(1)} fusion(f32[96,256]{1,0:T(8,128)S(1)} %bitcast.300, f32[32,8,16,128]{3,2,1,0:T(8,128)S(1)} %bitcast.277), kind=kOutput, calls=%fused_computation.6 | convolution fusion | flops 603979776 | bytes 2981888 | tf_op jit(solution)/shard_map/dot_general | solution.py:29
  135.8 0.1 slice_bitcast_fusion.2
  136.3 2.0 %fusion.30 = f32[32,1,16,128]{3,2,1,0:T(8,128)} fusion(f32[32,1,16,128]{3,2,1,0:T(8,128)S(1)} %bitcast.288, f32[32,1,16,128]{3,2,1,0:T(8,128)S(1)} %bitcast.289, f32[32,1,16,128]{3,2,1,0:T(8,128)S(1)} %bitcast.290, f32[32,1,16,128]{3,2,1,0:T(8,128)S(1)} %bitcast.291, f32[32,1,16,128]{3,2,1,0:T(8,128)S(1)} %bitcast.292, f32[32,1,16,128]{3,2,1,0:T(8,128)S(1)} %bitcast.293, ...), kind=kLoop, calls=%fused_computation.60 | loop fusion | flops 1703936 | bytes 7340032 | tf_op jit(solution)/shard_map/add | solution.py:46
  (27 shorter events, 1.3 us)
Async XLA Ops:
  6.5 82.2 %all-gather.2.cloned.1.call-start = ((), (), s32[]{:S(2)}) async-start(), calls=%async_computation | async-start | bytes 2359296 | tf_op jit(solution)/shard_map/all_gather | solution.py:51
  88.7 28.2 %collective-permute-start = (f32[256,1,16,128]{3,2,1,0:T(8,128)}, f32[256,1,16,128]{3,2,1,0:T(8,128)S(1)}, u32[]{:S(2)}, u32[]{:S(2)}) collective-permute-start(f32[256,1,16,128]{3,2,1,0:T(8,128)} %all-gather.2.cloned.1.call-done), channel_id=1, source_target_pairs={{0,1},{1,2},{2,3},{3,4},{4,5},{5,6},{6,7},{7,8},{8,9},{9,10},{10,1... | collective-permute-start | bytes 6291464 | tf_op jit(solution)/shard_map/ppermute | solution.py:12
  97.6 2.1 %copy-start = (f32[256,1,16,128]{3,2,1,0:T(8,128)S(1)}, f32[256,1,16,128]{3,2,1,0:T(8,128)}, u32[]{:S(2)}) copy-start(f32[256,1,16,128]{3,2,1,0:T(8,128)} %all-gather.2.cloned.1.call-done) | copy-start | bytes 6291460
  101.7 27.4 %collective-permute-start.1 = (f32[256,1,16,128]{3,2,1,0:T(8,128)S(1)}, f32[256,1,16,128]{3,2,1,0:T(8,128)S(1)}, u32[]{:S(2)}, u32[]{:S(2)}) collective-permute-start(f32[256,1,16,128]{3,2,1,0:T(8,128)S(1)} %copy-done), channel_id=1, source_target_pairs={{1,0},{2,1},{3,2},{4,3},{5,4},{6,5},{7,6},{8,7},{9,8},{10,9},{11,1... | collective-permute-start | bytes 6291464 | tf_op jit(solution)/shard_map/ppermute | solution.py:15
Sparse Core Ops, SparseCore 0:
  10.0 78.6 all-gather.1
where the time goes:
time: 145 us
  waiting for transfers between devices  98.5 us (68%)
  matrix products  17.4 us (12%)
  between operations  13.7 us (9%)
  starting transfers between devices  7.05 us (5%)
  local copies, waits for them, and re-layouts  6.46 us (4%)
  other arithmetic  2 us (1%)
    all_gather x1, waiting for transfers between devices, local(): gathered = lax.all_gather(volume, 'chan', axis=0, tiled=True)  81.4 us
    dot_general x9, matrix products, spread(): jnp.dot(taps[row_tap].reshape(3 * filters, channels), column_slab, precis...  17.4 us
    ppermute x1, waiting for transfers between devices, with_halo(): lax.ppermute(lax.slice_in_dim(block, block.shape[dim] - width, None, axis...  10.8 us
    ppermute x1, waiting for transfers between devices, with_halo(): lax.ppermute(lax.slice_in_dim(block, 0, width, axis=dim), axis, backward)  5.54 us
    ppermute x1, starting transfers between devices, with_halo(): lax.ppermute(lax.slice_in_dim(block, block.shape[dim] - width, None, axis...  4.95 us
    slice x3, local copies, waits for them, and re-layouts, spread(): framed[:, :, row_tap:row_tap + height, :]  3.33 us
  transfers between devices with their start and end apart: 3, of which 3 were waited for; matrix products, arithmetic and copies ran while one was open for 12% of the time, Pallas kernels for 0%

commit v1 on v0

v1 whole, which is shorter than its diff:
```python
import jax
import jax.numpy as jnp
from jax import lax
from jax.experimental import pallas as pl
from jax.experimental.pallas import tpu as pltpu
from jax.sharding import PartitionSpec as P

X = 4
F32, BF16 = jnp.float32, jnp.bfloat16


def split(values):
    high = values.astype(BF16)
    return high, (values - high.astype(F32)).astype(BF16)


def taps_kernel(kernel_ref, near_ref, far_ref):
    me = lax.axis_index("chan")
    core = lax.rem(lax.axis_index("depth"), 2)
    z, x = me // X, lax.rem(me, X)
    filters = kernel_ref.shape[3]
    half = kernel_ref.shape[4] // 2
    turn = lax.rem(half - (half // X) * x, half)
    for out_ref, row in ((near_ref, z), (far_ref, 1 - z)):
        columns = pl.ds(pl.multiple_of(row * half, half), half)
        for a, plane in enumerate((2 - 2 * core, 2 * core, 1)):
            for b in range(3):
                rows = pl.ds((a * 3 + b) * filters, filters)
                for e in range(3):
                    high, low = split(
                        pltpu.roll(kernel_ref[plane, b, e, :, columns], turn, 1)
                    )
                    out_ref[rows, pl.ds(e * half, half)] = high
                    out_ref[rows, pl.ds((3 + e) * half, half)] = high
                    out_ref[rows, pl.ds((6 + e) * half, half)] = low


def accumulate(shards, taps_ref, cells, total):
    across = shards[0].shape[1]
    height = cells.shape[1] // across
    channels = shards[0].shape[0] // height
    half = channels * len(shards)
    filters = total.shape[0] // 3
    lane = lax.broadcasted_iota(jnp.int32, (channels, across), 1)
    total[...] = jnp.zeros_like(total)
    step = 2
    for start in range(0, height, step):
        for h in range(start, start + step):
            for k, ref in enumerate(shards):
                middle = ref[pl.ds(h, channels, stride=height), :]
                left = jnp.where(lane == 0, 0.0, pltpu.roll(middle, 1, 1))
                right = jnp.where(lane == across - 1, 0.0, pltpu.roll(middle, across - 1, 1))
                for e, values in enumerate((left, middle, right)):
                    high, low = split(values)
                    row = e * half + k * channels
                    cells[pl.ds(row, channels), pl.ds(h * across, across)] = high
                    cells[pl.ds(3 * half + row, channels), pl.ds(h * across, across)] = low
        wide = pl.ds(start * across, step * across)
        products = jnp.dot(
            taps_ref[:, : 6 * half], cells[:, wide], preferred_element_type=F32
        ) + jnp.dot(
            taps_ref[:, 6 * half :], cells[: 3 * half, wide], preferred_element_type=F32
        )
        for a in range(3):
            for b in range(3):
                row = (a * 3 + b) * filters
                place = pl.ds((start + 2 - b) * across, step * across)
                total[pl.ds(a * filters, filters), place] += products[row : row + filters]


def near_kernel(s0, s1, s2, s3, taps_ref, total, cells):
    accumulate((s0, s1, s2, s3), taps_ref, cells, total)


def far_kernel(s0, s1, s2, s3, taps_ref, near_ref, off_ref, on_ref, mid_ref, cells, total):
    accumulate((s0, s1, s2, s3), taps_ref, cells, total)
    across = s0.shape[1]
    height = cells.shape[1] // across
    filters = total.shape[0] // 3
    for a, out_ref in enumerate((off_ref, on_ref, mid_ref)):
        for h in range(height):
            rows, place = pl.ds(a * filters, filters), pl.ds((h + 1) * across, across)
            out_ref[pl.ds(h, filters, stride=height), :] = total[rows, place] + near_ref[rows, place]


def along_x(step):
    return [(4 * g + i, 4 * g + (i + step) % 4) for g in range(2) for i in range(4)]


def local(volume, kernel):
    filters, channels = kernel.shape[3], kernel.shape[4]
    shard, _, height, across = volume.shape
    half = channels // 2
    cells = shard * height
    limit = pltpu.CompilerParams(vmem_limit_bytes=24 * 1024 * 1024)
    own = volume.reshape(cells, across)
    other = lax.ppermute(own, "chan", [(i, (i + X) % (2 * X)) for i in range(2 * X)])
    near = [own] + [lax.ppermute(own, "chan", along_x(step)) for step in (3, 2, 1)]
    far = [other] + [lax.ppermute(other, "chan", along_x(step)) for step in (3, 2, 1)]
    weights = jax.ShapeDtypeStruct((9 * filters, 9 * half), BF16)
    near_taps, far_taps = pl.pallas_call(
        taps_kernel,
        out_shape=(weights, weights),
        compiler_params=limit,
        cost_estimate=pl.CostEstimate(flops=0, bytes_accessed=4_000_000, transcendentals=0),
        name="taps",
    )(kernel)
    work = pl.CostEstimate(
        flops=2 * 9 * filters * 9 * half * height * across,
        bytes_accessed=4_000_000,
        transcendentals=0,
    )
    total = (3 * filters, (height + 2) * across)
    scratch = pltpu.VMEM((6 * half, height * across), BF16)
    near_total = pl.pallas_call(
        near_kernel,
        out_shape=jax.ShapeDtypeStruct(total, F32),
        scratch_shapes=[scratch],
        compiler_params=limit,
        cost_estimate=work,
        name="near",
    )(*near, near_taps)
    part = jax.ShapeDtypeStruct((filters * height, across), F32)
    off, on, mid = pl.pallas_call(
        far_kernel,
        out_shape=(part, part, part),
        scratch_shapes=[scratch, pltpu.VMEM(total, F32)],
        compiler_params=limit,
        cost_estimate=work,
        name="far",
    )(*far, far_taps, near_total)
    planes = lax.axis_size("depth")
    between = [(i, i + 1) for i in range(1, planes - 1, 2)]
    within = [(i, i + 1) for i in range(0, planes, 2)]
    off = lax.ppermute(off, "depth", between + [(j, i) for i, j in between])
    on = lax.ppermute(on, "depth", within + [(j, i) for i, j in within])
    return (mid + off + on).reshape(filters, 1, height, across)


def solution(mesh):
    return jax.shard_map(
        local,
        mesh=mesh,
        in_specs=(P("chan", "depth", None, None), P(None, None, None, "chan", None)),
        out_specs=P("chan", "depth", None, None),
        check_vma=False,
    )
```

time: 145 us -> 48.9 us (0.34)
  the two profiles are of different devices: /device:TPU:1 before, /device:TPU:25 now
where the time goes in v1:
time: 48.9 us; the launch traced here: 48.7 us
  waiting for transfers between devices  25 us (51%)
  starting transfers between devices  17.4 us (36%)
  Pallas kernels  4.38 us (9%)
  local copies, waits for them, and re-layouts  1.17 us (2%)
  other arithmetic  0.74 us (2%)
    ppermute x3, waiting for transfers between devices, local(): lax.ppermute(other, 'chan', along_x(step))  7.5 us
    ppermute x3, waiting for transfers between devices, local(): lax.ppermute(own, 'chan', along_x(step))  7.34 us
    ppermute x1, starting transfers between devices, local(): lax.ppermute(own, 'chan', [(i, (i + X) % (2 * X)) for i in range(2 * X)])  6.91 us
    ppermute x1, waiting for transfers between devices, local(): off = lax.ppermute(off, 'depth', between + [(j, i) for i, j in between])  6.49 us
    ppermute x1, waiting for transfers between devices, local(): lax.ppermute(own, 'chan', [(i, (i + X) % (2 * X)) for i in range(2 * X)])  3.62 us
    ppermute x3, starting transfers between devices, local(): lax.ppermute(other, 'chan', along_x(step))  3.6 us
    ppermute x3, starting transfers between devices, local(): lax.ppermute(own, 'chan', along_x(step))  3.6 us
    ppermute x1, starting transfers between devices, local(): off = lax.ppermute(off, 'depth', between + [(j, i) for i, j in between])  3.2 us
  transfers between devices with their start and end apart: 9, of which 5 were waited for; matrix products, arithmetic and copies ran while one was open for 0% of the time, Pallas kernels for 5%

profile of v1, /device:TPU:25, one launch (start us, length us, event | category | flops | bytes accessed | tf_op | source)
XLA Modules:
  0.0 48.7 jit_solution(10979774484062676728)
XLA Ops:
  0.0 6.9 %collective-permute-start = (f32[512,128]{1,0:T(8,128)}, f32[512,128]{1,0:T(8,128)S(1)}, u32[]{:S(2)}, u32[]{:S(2)}) collective-permute-start(f32[512,128]{1,0:T(8,128)} %bitcast.4), channel_id=1, source_target_pairs={{0,128},{32,160},{64,192},{96,224},{128,0},{160,32},{192,64},{224,... | collective-permute-start | bytes 786440 | tf_op jit(solution)/shard_map/ppermute | solution.py:97
  6.9 2.5 %collective-permute-start.4 = (f32[512,128]{1,0:T(8,128)}, f32[512,128]{1,0:T(8,128)S(1)}, u32[]{:S(2)}, u32[]{:S(2)}) collective-permute-start(f32[512,128]{1,0:T(8,128)} %bitcast.5), channel_id=1, source_target_pairs={{0,96},{32,0},{64,32},{96,64},{128,224},{160,128},{192,160},{224,1... | collective-permute-start | bytes 786440 | tf_op jit(solution)/shard_map/ppermute | solution.py:98
  9.4 0.5 %collective-permute-start.5 = (f32[512,128]{1,0:T(8,128)}, f32[512,128]{1,0:T(8,128)S(1)}, u32[]{:S(2)}, u32[]{:S(2)}) collective-permute-start(f32[512,128]{1,0:T(8,128)} %bitcast.6), channel_id=1, source_target_pairs={{0,64},{32,96},{64,0},{96,32},{128,192},{160,224},{192,128},{224,1... | collective-permute-start | bytes 786440 | tf_op jit(solution)/shard_map/ppermute | solution.py:98
  9.9 0.6 %collective-permute-start.6 = (f32[512,128]{1,0:T(8,128)}, f32[512,128]{1,0:T(8,128)S(1)}, u32[]{:S(2)}, u32[]{:S(2)}) collective-permute-start(f32[512,128]{1,0:T(8,128)} %bitcast.7), channel_id=1, source_target_pairs={{0,32},{32,64},{64,96},{96,0},{128,160},{160,192},{192,224},{224,1... | collective-permute-start | bytes 786440 | tf_op jit(solution)/shard_map/ppermute | solution.py:98
  10.5 3.6 %collective-permute-done.s0 = f32[512,128]{1,0:T(8,128)S(1)} collective-permute-done((f32[512,128]{1,0:T(8,128)}, f32[512,128]{1,0:T(8,128)S(1)}, u32[]{:S(2)}, u32[]{:S(2)}) %collective-permute-start) | collective-permute-done | bytes 262176 | tf_op jit(solution)/shard_map/ppermute | solution.py:97
  14.1 2.5 %collective-permute-start.1 = (f32[512,128]{1,0:T(8,128)S(1)}, f32[512,128]{1,0:T(8,128)S(1)}, u32[]{:S(2)}, u32[]{:S(2)}) collective-permute-start(f32[512,128]{1,0:T(8,128)S(1)} %collective-permute-done.s0), channel_id=1, source_target_pairs={{0,96},{32,0},{64,32},{96,64},{128,224},{160,128},{192,160},{224,1... | collective-permute-start | bytes 786440 | tf_op jit(solution)/shard_map/ppermute | solution.py:99
  16.6 0.5 %collective-permute-start.2 = (f32[512,128]{1,0:T(8,128)S(1)}, f32[512,128]{1,0:T(8,128)S(1)}, u32[]{:S(2)}, u32[]{:S(2)}) collective-permute-start(f32[512,128]{1,0:T(8,128)S(1)} %collective-permute-done.s0), channel_id=1, source_target_pairs={{0,64},{32,96},{64,0},{96,32},{128,192},{160,224},{192,128},{224,1... | collective-permute-start | bytes 786440 | tf_op jit(solution)/shard_map/ppermute | solution.py:99
  17.1 0.0 collective-permute-done.4.s1
  17.1 0.6 %collective-permute-start.3 = (f32[512,128]{1,0:T(8,128)S(1)}, f32[512,128]{1,0:T(8,128)S(1)}, u32[]{:S(2)}, u32[]{:S(2)}) collective-permute-start(f32[512,128]{1,0:T(8,128)S(1)} %collective-permute-done.s0), channel_id=1, source_target_pairs={{0,32},{32,64},{64,96},{96,0},{128,160},{160,192},{192,224},{224,1... | collective-permute-start | bytes 786440 | tf_op jit(solution)/shard_map/ppermute | solution.py:99
  17.7 0.0 copy-start
  17.7 1.2 %copy-done = f32[3,3,3,32,256]{4,3,2,1,0:T(8,128)S(1)} copy-done((f32[3,3,3,32,256]{4,3,2,1,0:T(8,128)S(1)}, f32[3,3,3,32,256]{4,3,2,1,0:T(8,128)}, u32[]{:S(2)}) %copy-start) | copy-done | bytes 884760
  18.9 0.0 copy-start.1
  18.9 0.3 taps.1
  19.2 0.0 collective-permute-done.5.s2
  19.2 7.3 %collective-permute-done.6.s3 = f32[512,128]{1,0:T(8,128)S(1)} collective-permute-done((f32[512,128]{1,0:T(8,128)}, f32[512,128]{1,0:T(8,128)S(1)}, u32[]{:S(2)}, u32[]{:S(2)}) %collective-permute-start.6) | collective-permute-done | bytes 262176 | tf_op jit(solution)/shard_map/ppermute | solution.py:98
  26.6 0.0 copy-done.1
  26.6 2.0 %near.1.near_ref = f32[96,2304]{1,0:T(8,128)S(1)} custom-call(f32[512,128]{1,0:T(8,128)S(1)} %bitcast.8, f32[512,128]{1,0:T(8,128)S(1)} %collective-permute-done.4.s1, f32[512,128]{1,0:T(8,128)S(1)} %collective-permute-done.5.s2, f32[512,128]{1,0:T(8,128)S(1)} %collective-permute-done.6.s3, bf16[288,1152]{1,0:T(8,128)(2,1)S(1)} %get-tuple-element.11.taps_ref), custom_call_target="tpu_custom_call" | custom-call | flops 1358954496 | bytes 4000000 | tf_op jit(solution)/shard_map/near/pallas_call | solution.py:115
  28.6 0.0 collective-permute-done.1.s1
  28.6 0.4 collective-permute-done.2.s2
  29.0 7.1 %collective-permute-done.3.s3 = f32[512,128]{1,0:T(8,128)S(1)} collective-permute-done((f32[512,128]{1,0:T(8,128)S(1)}, f32[512,128]{1,0:T(8,128)S(1)}, u32[]{:S(2)}, u32[]{:S(2)}) %collective-permute-start.3) | collective-permute-done | bytes 262176 | tf_op jit(solution)/shard_map/ppermute | solution.py:99
  36.1 2.1 %far.1 = (f32[512,128]{1,0:T(8,128)S(1)}, f32[512,128]{1,0:T(8,128)S(1)}, f32[512,128]{1,0:T(8,128)S(1)}) custom-call(f32[512,128]{1,0:T(8,128)S(1)} %collective-permute-done.s0, f32[512,128]{1,0:T(8,128)S(1)} %collective-permute-done.1.s1, f32[512,128]{1,0:T(8,128)S(1)} %collective-permute-done.2.s2, f32[512,128]{1,0:T(8,128)S(1)} %collective-permute-done.3.s3, ...), custom_call_target="tpu_custom_call" | custom-call | flops 1358954496 | bytes 4000000 | tf_op jit(solution)/shard_map/far/pallas_call | solution.py:124
  38.2 3.2 %collective-permute-start.7 = (f32[512,128]{1,0:T(8,128)S(1)}, f32[512,128]{1,0:T(8,128)S(1)}, u32[]{:S(2)}, u32[]{:S(2)}) collective-permute-start(f32[512,128]{1,0:T(8,128)S(1)} %get-tuple-element.13), channel_id=1, source_target_pairs={{1,2},{3,4},{5,6},{7,8},{9,10},{11,12},{13,14},{15,16},{17,18},{19... | collective-permute-start | bytes 786440 | tf_op jit(solution)/shard_map/ppermute | solution.py:135
  41.4 0.1 collective-permute-start.8
  41.5 6.5 %collective-permute-done.7 = f32[512,128]{1,0:T(8,128)S(1)} collective-permute-done((f32[512,128]{1,0:T(8,128)S(1)}, f32[512,128]{1,0:T(8,128)S(1)}, u32[]{:S(2)}, u32[]{:S(2)}) %collective-permute-start.7) | collective-permute-done | bytes 262176 | tf_op jit(solution)/shard_map/ppermute | solution.py:135
  48.0 0.0 collective-permute-done.8
  48.0 0.7 %add_add_fusion = f32[512,128]{1,0:T(8,128)} fusion(f32[512,128]{1,0:T(8,128)S(1)} %collective-permute-done.8, f32[512,128]{1,0:T(8,128)S(1)} %get-tuple-element.12, f32[512,128]{1,0:T(8,128)S(1)} %collective-permute-done.7), kind=kLoop, calls=%fused_computation | loop fusion | flops 131072 | bytes 1048576 | tf_op jit(solution)/shard_map/add | solution.py:137
Async XLA Ops:
  0.0 14.1 %collective-permute-start = (f32[512,128]{1,0:T(8,128)}, f32[512,128]{1,0:T(8,128)S(1)}, u32[]{:S(2)}, u32[]{:S(2)}) collective-permute-start(f32[512,128]{1,0:T(8,128)} %bitcast.4), channel_id=1, source_target_pairs={{0,128},{32,160},{64,192},{96,224},{128,0},{160,32},{192,64},{224,... | collective-permute-start | bytes 786440 | tf_op jit(solution)/shard_map/ppermute | solution.py:97
  6.9 10.2 %collective-permute-start.4 = (f32[512,128]{1,0:T(8,128)}, f32[512,128]{1,0:T(8,128)S(1)}, u32[]{:S(2)}, u32[]{:S(2)}) collective-permute-start(f32[512,128]{1,0:T(8,128)} %bitcast.5), channel_id=1, source_target_pairs={{0,96},{32,0},{64,32},{96,64},{128,224},{160,128},{192,160},{224,1... | collective-permute-start | bytes 786440 | tf_op jit(solution)/shard_map/ppermute | solution.py:98
  9.4 9.8 %collective-permute-start.5 = (f32[512,128]{1,0:T(8,128)}, f32[512,128]{1,0:T(8,128)S(1)}, u32[]{:S(2)}, u32[]{:S(2)}) collective-permute-start(f32[512,128]{1,0:T(8,128)} %bitcast.6), channel_id=1, source_target_pairs={{0,64},{32,96},{64,0},{96,32},{128,192},{160,224},{192,128},{224,1... | collective-permute-start | bytes 786440 | tf_op jit(solution)/shard_map/ppermute | solution.py:98
  9.9 16.7 %collective-permute-start.6 = (f32[512,128]{1,0:T(8,128)}, f32[512,128]{1,0:T(8,128)S(1)}, u32[]{:S(2)}, u32[]{:S(2)}) collective-permute-start(f32[512,128]{1,0:T(8,128)} %bitcast.7), channel_id=1, source_target_pairs={{0,32},{32,64},{64,96},{96,0},{128,160},{160,192},{192,224},{224,1... | collective-permute-start | bytes 786440 | tf_op jit(solution)/shard_map/ppermute | solution.py:98
  14.1 14.4 %collective-permute-start.1 = (f32[512,128]{1,0:T(8,128)S(1)}, f32[512,128]{1,0:T(8,128)S(1)}, u32[]{:S(2)}, u32[]{:S(2)}) collective-permute-start(f32[512,128]{1,0:T(8,128)S(1)} %collective-permute-done.s0), channel_id=1, source_target_pairs={{0,96},{32,0},{64,32},{96,64},{128,224},{160,128},{192,160},{224,1... | collective-permute-start | bytes 786440 | tf_op jit(solution)/shard_map/ppermute | solution.py:99
  16.6 12.4 %collective-permute-start.2 = (f32[512,128]{1,0:T(8,128)S(1)}, f32[512,128]{1,0:T(8,128)S(1)}, u32[]{:S(2)}, u32[]{:S(2)}) collective-permute-start(f32[512,128]{1,0:T(8,128)S(1)} %collective-permute-done.s0), channel_id=1, source_target_pairs={{0,64},{32,96},{64,0},{96,32},{128,192},{160,224},{192,128},{224,1... | collective-permute-start | bytes 786440 | tf_op jit(solution)/shard_map/ppermute | solution.py:99
  17.1 18.9 %collective-permute-start.3 = (f32[512,128]{1,0:T(8,128)S(1)}, f32[512,128]{1,0:T(8,128)S(1)}, u32[]{:S(2)}, u32[]{:S(2)}) collective-permute-start(f32[512,128]{1,0:T(8,128)S(1)} %collective-permute-done.s0), channel_id=1, source_target_pairs={{0,32},{32,64},{64,96},{96,0},{128,160},{160,192},{192,224},{224,1... | collective-permute-start | bytes 786440 | tf_op jit(solution)/shard_map/ppermute | solution.py:99
  17.7 1.2 %copy-start = (f32[3,3,3,32,256]{4,3,2,1,0:T(8,128)S(1)}, f32[3,3,3,32,256]{4,3,2,1,0:T(8,128)}, u32[]{:S(2)}) copy-start(f32[3,3,3,32,256]{4,3,2,1,0:T(8,128)} %kernel_ref.1) | copy-start | bytes 2654212
  18.9 7.7 %copy-start.1 = (f32[32,1,16,128]{3,2,1,0:T(8,128)S(1)}, f32[32,1,16,128]{3,2,1,0:T(8,128)}, u32[]{:S(2)}) copy-start(f32[32,1,16,128]{3,2,1,0:T(8,128)} %param.2) | copy-start | bytes 786436
  38.2 9.8 %collective-permute-start.7 = (f32[512,128]{1,0:T(8,128)S(1)}, f32[512,128]{1,0:T(8,128)S(1)}, u32[]{:S(2)}, u32[]{:S(2)}) collective-permute-start(f32[512,128]{1,0:T(8,128)S(1)} %get-tuple-element.13), channel_id=1, source_target_pairs={{1,2},{3,4},{5,6},{7,8},{9,10},{11,12},{13,14},{15,16},{17,18},{19... | collective-permute-start | bytes 786440 | tf_op jit(solution)/shard_map/ppermute | solution.py:135
  41.4 6.6 %collective-permute-start.8 = (f32[512,128]{1,0:T(8,128)S(1)}, f32[512,128]{1,0:T(8,128)S(1)}, u32[]{:S(2)}, u32[]{:S(2)}) collective-permute-start(f32[512,128]{1,0:T(8,128)S(1)} %get-tuple-element.14), channel_id=1, source_target_pairs={{0,1},{2,3},{4,5},{6,7},{8,9},{10,11},{12,13},{14,15},{16,17},{18,... | collective-permute-start | bytes 786440 | tf_op jit(solution)/shard_map/ppermute | solution.py:136

commit v2 on v1

v2 whole, which is shorter than its diff:
```python
import functools

import jax
import jax.numpy as jnp
from jax import lax
from jax.experimental import pallas as pl
from jax.experimental.pallas import tpu as pltpu
from jax.sharding import PartitionSpec as P

X = 4
ROWS = 2
F32, BF16 = jnp.float32, jnp.bfloat16


def split(values):
    high = values.astype(BF16)
    return high, (values - high.astype(F32)).astype(BF16)


def taps_kernel(kernel_ref, near_ref, far_ref, last_ref):
    me = lax.axis_index("chan")
    core = lax.rem(lax.axis_index("depth"), 2)
    z, x = me // X, lax.rem(me, X)
    filters = kernel_ref.shape[3]
    half = kernel_ref.shape[4] // 2
    shard = half // X
    turn = lax.rem((X - x) * shard, half)
    slot = lax.broadcasted_iota(jnp.int32, (filters, half), 1) // shard
    for out_ref, row in ((near_ref, z), (far_ref, 1 - z)):
        columns = pl.ds(pl.multiple_of(row * half, half), half)
        for a, plane in enumerate((2 - 2 * core, 2 * core, 1)):
            for b in range(3):
                rows = pl.ds((a * 3 + b) * filters, filters)
                blocks = []
                for e in range(3):
                    values = pltpu.roll(kernel_ref[plane, b, e, :, columns], turn, 1)
                    high, low = split(values)
                    out_ref[rows, pl.ds(e * half, half)] = high
                    out_ref[rows, pl.ds((3 + e) * half, half)] = high
                    out_ref[rows, pl.ds((6 + e) * half, half)] = low
                    blocks.append((high.astype(F32), low.astype(F32)))
                if out_ref is far_ref:
                    blocks = [h for h, _ in blocks] * 2 + [l for _, l in blocks]
                    for tile in range(last_ref.shape[1] // half):
                        result = jnp.zeros((filters, half), F32)
                        for k, values in enumerate(blocks[tile * X : tile * X + X]):
                            placed = pltpu.roll(values, (k + X - 2) % X * shard, 1)
                            result = jnp.where(slot == k, placed, result)
                        last_ref[rows, pl.ds(tile * half, half)] = result.astype(BF16)


def pack(ref, cells, h, height, row_sets):
    channels, across = ref.shape[0] // height, ref.shape[1]
    lane = lax.broadcasted_iota(jnp.int32, (channels, across), 1)
    middle = ref[pl.ds(h, channels, stride=height), :]
    left = jnp.where(lane == 0, 0.0, pltpu.roll(middle, 1, 1))
    right = jnp.where(lane == across - 1, 0.0, pltpu.roll(middle, across - 1, 1))
    for values, rows in zip((left, middle, right), row_sets):
        high, low = split(values)
        for row, part in zip(rows, (high, low, high)):
            cells[pl.ds(row, channels), pl.ds(h * across, across)] = part


def accumulate(shards, taps_ref, cells, total):
    across = shards[0].shape[1]
    height = cells.shape[1] // across
    channels = shards[0].shape[0] // height
    half = cells.shape[0] // 6
    for k, ref in enumerate(shards):
        if ref is None:
            for e in range(6):
                rows = pl.ds(e * half + k * channels, channels)
                cells[rows, :] = jnp.zeros((channels, cells.shape[1]), BF16)
    for start in range(0, height, ROWS):
        for h in range(start, start + ROWS):
            for k, ref in enumerate(shards):
                if ref is not None:
                    row = k * channels
                    pack(ref, cells, h, height, [(e * half + row, (3 + e) * half + row) for e in range(3)])
        wide = pl.ds(start * across, ROWS * across)
        products = jnp.dot(
            taps_ref[:, : 6 * half], cells[:, wide], preferred_element_type=F32
        ) + jnp.dot(
            taps_ref[:, 6 * half :], cells[: 3 * half, wide], preferred_element_type=F32
        )
        scatter(products, total, total.shape[0] // 3, start, across)


def scatter(products, total, filters, start, across):
    for a in range(total.shape[0] // filters):
        for b in range(3):
            row = (a * 3 + b) * filters
            place = pl.ds((start + 2 - b) * across, ROWS * across)
            total[pl.ds(a * filters, filters), place] += products[row : row + filters]


def near_kernel(s0, s1, s2, s3, taps_ref, total, cells):
    total[...] = jnp.zeros_like(total)
    accumulate((s0, s1, s2, s3), taps_ref, cells, total)


def far_kernel(s0, s1, s3, taps_ref, near_ref, total, cells):
    total[...] = near_ref[...]
    accumulate((s0, s1, None, s3), taps_ref, cells, total)


def last_kernel(planes, ref, taps_ref, before_ref, *rest):
    *out_refs, cells, total = rest
    across = ref.shape[1]
    height = cells.shape[1] // across
    channels = ref.shape[0] // height
    filters = before_ref.shape[0] // 3
    first = planes[0] * filters
    total[...] = before_ref[pl.ds(first, total.shape[0]), :]
    unused = cells.shape[0] - 9 * channels
    cells[pl.ds(9 * channels, unused), :] = jnp.zeros((unused, cells.shape[1]), BF16)
    for start in range(0, height, ROWS):
        for h in range(start, start + ROWS):
            pack(ref, cells, h, height, [[(3 * t + e) * channels for t in range(3)] for e in range(3)])
        products = jnp.dot(
            taps_ref[pl.ds(3 * first, 3 * total.shape[0]), :],
            cells[:, pl.ds(start * across, ROWS * across)],
            preferred_element_type=F32,
        )
        scatter(products, total, filters, start, across)
    for a, out_ref in enumerate(out_refs):
        for h in range(height):
            out_ref[pl.ds(h, filters, stride=height), :] = total[
                pl.ds(a * filters, filters), pl.ds((h + 1) * across, across)
            ]


def spread(block):
    return [
        lax.ppermute(
            block, "chan", [(g * X + i, g * X + (i - step) % X) for g in range(2) for i in range(X)]
        )
        for step in (1, 3, 2)
    ]


def local(volume, kernel):
    filters, channels = kernel.shape[3], kernel.shape[4]
    shard, _, height, across = volume.shape
    half = channels // 2
    cells = shard * height
    limit = pltpu.CompilerParams(vmem_limit_bytes=24 * 1024 * 1024)
    own = volume.reshape(cells, across)
    other = lax.ppermute(own, "chan", [(i, (i + X) % (2 * X)) for i in range(2 * X)])
    s1, s3, s2 = spread(own)
    t1, t3, t2 = spread(other)
    weights = jax.ShapeDtypeStruct((9 * filters, 9 * half), BF16)
    last_weights = jax.ShapeDtypeStruct((9 * filters, 3 * half), BF16)
    near_taps, far_taps, last_taps = pl.pallas_call(
        taps_kernel,
        out_shape=(weights, weights, last_weights),
        compiler_params=limit,
        cost_estimate=pl.CostEstimate(flops=0, bytes_accessed=4_000_000, transcendentals=0),
        name="taps",
    )(kernel)

    def work(planes, part):
        return pl.CostEstimate(
            flops=int(2 * 3 * planes * filters * 9 * half * part * height * across),
            bytes_accessed=3_000_000,
            transcendentals=0,
        )

    total = jax.ShapeDtypeStruct((3 * filters, (height + 2) * across), F32)
    packed = pltpu.VMEM((6 * half, height * across), BF16)
    before = pl.pallas_call(
        near_kernel,
        out_shape=total,
        scratch_shapes=[packed],
        compiler_params=limit,
        cost_estimate=work(3, 1),
        name="near",
    )(own, s1, s2, s3, near_taps)
    before = pl.pallas_call(
        far_kernel,
        out_shape=total,
        scratch_shapes=[packed],
        compiler_params=limit,
        cost_estimate=work(3, 1),
        name="far",
    )(other, t1, t3, far_taps, before)

    def last(name, *taps):
        part = jax.ShapeDtypeStruct((filters * height, across), F32)
        return pl.pallas_call(
            functools.partial(last_kernel, taps),
            out_shape=[part] * len(taps),
            scratch_shapes=[
                pltpu.VMEM((3 * half, height * across), BF16),
                pltpu.VMEM((len(taps) * filters, total.shape[1]), F32),
            ],
            compiler_params=limit,
            cost_estimate=work(len(taps), 0.25),
            name=name,
        )(t2, last_taps, before)

    (off,) = last("off", 0)
    on, mid = last("rest", 1, 2)
    planes = lax.axis_size("depth")
    between = [(i, i + 1) for i in range(1, planes - 1, 2)]
    within = [(i, i + 1) for i in range(0, planes, 2)]
    off = lax.ppermute(off, "depth", between + [(j, i) for i, j in between])
    on = lax.ppermute(on, "depth", within + [(j, i) for i, j in within])
    return (mid + off + on).reshape(filters, 1, height, across)


def solution(mesh):
    return jax.shard_map(
        local,
        mesh=mesh,
        in_specs=(P("chan", "depth", None, None), P(None, None, None, "chan", None)),
        out_specs=P("chan", "depth", None, None),
        check_vma=False,
    )
```

time: 48.9 us -> 47.9 us (0.980)
  the two profiles are of different devices: /device:TPU:25 before, /device:TPU:64 now
where the time goes in v2:
time: 47.9 us; the launch traced here: 47.8 us
  waiting for transfers between devices  21 us (44%)
  starting transfers between devices  18.6 us (39%)
  Pallas kernels  6.17 us (13%)
  local copies, waits for them, and re-layouts  1.17 us (2%)
  other arithmetic  0.75 us (2%)
    ppermute x6, starting transfers between devices, spread(): lax.ppermute(block, 'chan', [(g * X + i, g * X + (i - step) % X) for g in...  9.49 us
    ppermute x1, waiting for transfers between devices, local(): lax.ppermute(own, 'chan', [(i, (i + X) % (2 * X)) for i in range(2 * X)])  8.13 us
    ppermute x6, waiting for transfers between devices, spread(): lax.ppermute(block, 'chan', [(g * X + i, g * X + (i - step) % X) for g in...  7.53 us
    ppermute x1, starting transfers between devices, local(): lax.ppermute(own, 'chan', [(i, (i + X) % (2 * X)) for i in range(2 * X)])  5.39 us
    ppermute x1, waiting for transfers between devices, local(): off = lax.ppermute(off, 'depth', between + [(j, i) for i, j in between])  5.34 us
    pallas_call x1, Pallas kernels, local(): pl.pallas_call(near_kernel, out_shape=total, scratch_shapes=[packed], com...  1.99 us
    ppermute x1, starting transfers between devices, local(): off = lax.ppermute(off, 'depth', between + [(j, i) for i, j in between])  1.92 us
    pallas_call x1, Pallas kernels, local(): pl.pallas_call(far_kernel, out_shape=total, scratch_shapes=[packed], comp...  1.91 us
  transfers between devices with their start and end apart: 9, of which 4 were waited for; matrix products, arithmetic and copies ran while one was open for 0% of the time, Pallas kernels for 12%

profile of v2, /device:TPU:64, one launch (start us, length us, event | category | flops | bytes accessed | tf_op | source)
XLA Modules:
  0.0 47.8 jit_solution(18082175868282080478)
XLA Ops:
  0.0 5.4 %collective-permute-start = (f32[512,128]{1,0:T(8,128)}, f32[512,128]{1,0:T(8,128)S(1)}, u32[]{:S(2)}, u32[]{:S(2)}) collective-permute-start(f32[512,128]{1,0:T(8,128)} %bitcast.4), channel_id=1, source_target_pairs={{0,128},{32,160},{64,192},{96,224},{128,0},{160,32},{192,64},{224,... | collective-permute-start | bytes 786440 | tf_op jit(solution)/shard_map/ppermute | solution.py:149
  5.4 2.8 %collective-permute-start.4 = (f32[512,128]{1,0:T(8,128)}, f32[512,128]{1,0:T(8,128)S(1)}, u32[]{:S(2)}, u32[]{:S(2)}) collective-permute-start(f32[512,128]{1,0:T(8,128)} %bitcast.5), channel_id=1, source_target_pairs={{0,96},{32,0},{64,32},{96,64},{128,224},{160,128},{192,160},{224,1... | collective-permute-start | bytes 786440 | tf_op jit(solution)/shard_map/ppermute | solution.py:135
  8.2 0.8 %collective-permute-start.5 = (f32[512,128]{1,0:T(8,128)}, f32[512,128]{1,0:T(8,128)S(1)}, u32[]{:S(2)}, u32[]{:S(2)}) collective-permute-start(f32[512,128]{1,0:T(8,128)} %bitcast.6), channel_id=1, source_target_pairs={{0,64},{32,96},{64,0},{96,32},{128,192},{160,224},{192,128},{224,1... | collective-permute-start | bytes 786440 | tf_op jit(solution)/shard_map/ppermute | solution.py:135
  9.0 0.9 %collective-permute-start.6 = (f32[512,128]{1,0:T(8,128)}, f32[512,128]{1,0:T(8,128)S(1)}, u32[]{:S(2)}, u32[]{:S(2)}) collective-permute-start(f32[512,128]{1,0:T(8,128)} %bitcast.7), channel_id=1, source_target_pairs={{0,32},{32,64},{64,96},{96,0},{128,160},{160,192},{192,224},{224,1... | collective-permute-start | bytes 786440 | tf_op jit(solution)/shard_map/ppermute | solution.py:135
  9.8 8.1 %collective-permute-done.s0 = f32[512,128]{1,0:T(8,128)S(1)} collective-permute-done((f32[512,128]{1,0:T(8,128)}, f32[512,128]{1,0:T(8,128)S(1)}, u32[]{:S(2)}, u32[]{:S(2)}) %collective-permute-start) | collective-permute-done | bytes 262176 | tf_op jit(solution)/shard_map/ppermute | solution.py:149
  18.0 2.8 %collective-permute-start.2 = (f32[512,128]{1,0:T(8,128)S(1)}, f32[512,128]{1,0:T(8,128)S(1)}, u32[]{:S(2)}, u32[]{:S(2)}) collective-permute-start(f32[512,128]{1,0:T(8,128)S(1)} %collective-permute-done.s0), channel_id=1, source_target_pairs={{0,96},{32,0},{64,32},{96,64},{128,224},{160,128},{192,160},{224,1... | collective-permute-start | bytes 786440 | tf_op jit(solution)/shard_map/ppermute | solution.py:135
  20.7 0.0 collective-permute-start.3
  20.7 0.0 collective-permute-done.4.s1
  20.7 2.3 %collective-permute-start.1 = (f32[512,128]{1,0:T(8,128)S(1)}, f32[512,128]{1,0:T(8,128)S(1)}, u32[]{:S(2)}, u32[]{:S(2)}) collective-permute-start(f32[512,128]{1,0:T(8,128)S(1)} %collective-permute-done.s0), channel_id=1, source_target_pairs={{0,64},{32,96},{64,0},{96,32},{128,192},{160,224},{192,128},{224,1... | collective-permute-start | bytes 786440 | tf_op jit(solution)/shard_map/ppermute | solution.py:135
  23.0 0.0 copy-start
  23.0 1.2 %copy-done = f32[3,3,3,32,256]{4,3,2,1,0:T(8,128)S(1)} copy-done((f32[3,3,3,32,256]{4,3,2,1,0:T(8,128)S(1)}, f32[3,3,3,32,256]{4,3,2,1,0:T(8,128)}, u32[]{:S(2)}) %copy-start) | copy-done | bytes 884760
  24.2 0.0 copy-start.1
  24.2 0.9 %taps.1 = (bf16[288,1152]{1,0:T(8,128)(2,1)S(1)}, bf16[288,1152]{1,0:T(8,128)(2,1)S(1)}, bf16[288,384]{1,0:T(8,128)(2,1)S(1)}) custom-call(f32[3,3,3,32,256]{4,3,2,1,0:T(8,128)S(1)} %copy-done), custom_call_target="tpu_custom_call" | custom-call | bytes 4000000 | tf_op jit(solution)/shard_map/taps/pallas_call | solution.py:154
  25.1 0.0 collective-permute-done.5.s2
  25.1 0.0 collective-permute-done.6.s3
  25.1 0.0 copy-done.1
  25.2 2.0 %near.1.near_ref = f32[96,2304]{1,0:T(8,128)S(1)} custom-call(f32[512,128]{1,0:T(8,128)S(1)} %bitcast.8, f32[512,128]{1,0:T(8,128)S(1)} %collective-permute-done.4.s1, f32[512,128]{1,0:T(8,128)S(1)} %collective-permute-done.5.s2, f32[512,128]{1,0:T(8,128)S(1)} %collective-permute-done.6.s3, bf16[288,1152]{1,0:T(8,128)(2,1)S(1)} %get-tuple-element.12.taps_ref), custom_call_target="tpu_custom_call" | custom-call | flops 1358954496 | bytes 3000000 | tf_op jit(solution)/shard_map/near/pallas_call | solution.py:171
  27.2 4.1 %collective-permute-done.2.s1 = f32[512,128]{1,0:T(8,128)S(1)} collective-permute-done((f32[512,128]{1,0:T(8,128)S(1)}, f32[512,128]{1,0:T(8,128)S(1)}, u32[]{:S(2)}, u32[]{:S(2)}) %collective-permute-start.2) | collective-permute-done | bytes 262176 | tf_op jit(solution)/shard_map/ppermute | solution.py:135
  31.3 3.4 %collective-permute-done.3.s3 = f32[512,128]{1,0:T(8,128)S(1)} collective-permute-done((f32[512,128]{1,0:T(8,128)S(1)}, f32[512,128]{1,0:T(8,128)S(1)}, u32[]{:S(2)}, u32[]{:S(2)}) %collective-permute-start.3) | collective-permute-done | bytes 262176 | tf_op jit(solution)/shard_map/ppermute | solution.py:135
  34.7 1.9 %far.1.before_ref = f32[96,2304]{1,0:T(8,128)S(1)} custom-call(f32[512,128]{1,0:T(8,128)S(1)} %collective-permute-done.s0, f32[512,128]{1,0:T(8,128)S(1)} %collective-permute-done.2.s1, f32[512,128]{1,0:T(8,128)S(1)} %collective-permute-done.3.s3, bf16[288,1152]{1,0:T(8,128)(2,1)S(1)} %get-tuple-element.11.taps_ref, f32[96,2304]{1,0:T(8,128)S(1)} %near.1.near_ref), custom_call_target="tpu_custom_call" | custom-call | flops 1358954496 | bytes 3000000 | tf_op jit(solution)/shard_map/far/pallas_call | solution.py:179
  36.6 0.0 collective-permute-done.1.ref
  36.6 0.6 %off.1 = f32[512,128]{1,0:T(8,128)S(1)} custom-call(f32[512,128]{1,0:T(8,128)S(1)} %collective-permute-done.1.ref, bf16[288,384]{1,0:T(8,128)(2,1)S(1)} %get-tuple-element.10.taps_ref, f32[96,2304]{1,0:T(8,128)S(1)} %far.1.before_ref), custom_call_target="tpu_custom_call" | custom-call | flops 113246208 | bytes 3000000 | tf_op jit(solution)/shard_map/off/pallas_call | solution.py:190
  37.2 1.9 %collective-permute-start.7 = (f32[512,128]{1,0:T(8,128)S(1)}, f32[512,128]{1,0:T(8,128)S(1)}, u32[]{:S(2)}, u32[]{:S(2)}) collective-permute-start(f32[512,128]{1,0:T(8,128)S(1)} %off.1), channel_id=1, source_target_pairs={{1,2},{3,4},{5,6},{7,8},{9,10},{11,12},{13,14},{15,16},{17,18},{19... | collective-permute-start | bytes 786440 | tf_op jit(solution)/shard_map/ppermute | solution.py:207
  39.1 0.8 %rest.1 = (f32[512,128]{1,0:T(8,128)S(1)}, f32[512,128]{1,0:T(8,128)S(1)}) custom-call(f32[512,128]{1,0:T(8,128)S(1)} %collective-permute-done.1.ref, bf16[288,384]{1,0:T(8,128)(2,1)S(1)} %get-tuple-element.10.taps_ref, f32[96,2304]{1,0:T(8,128)S(1)} %far.1.before_ref), custom_call_target="tpu_custom_call" | custom-call | flops 226492416 | bytes 3000000 | tf_op jit(solution)/shard_map/rest/pallas_call | solution.py:190
  39.9 1.8 %collective-permute-start.8 = (f32[512,128]{1,0:T(8,128)S(1)}, f32[512,128]{1,0:T(8,128)S(1)}, u32[]{:S(2)}, u32[]{:S(2)}) collective-permute-start(f32[512,128]{1,0:T(8,128)S(1)} %get-tuple-element.14), channel_id=1, source_target_pairs={{0,1},{2,3},{4,5},{6,7},{8,9},{10,11},{12,13},{14,15},{16,17},{18,... | collective-permute-start | bytes 786440 | tf_op jit(solution)/shard_map/ppermute | solution.py:208
  41.7 5.3 %collective-permute-done.7 = f32[512,128]{1,0:T(8,128)S(1)} collective-permute-done((f32[512,128]{1,0:T(8,128)S(1)}, f32[512,128]{1,0:T(8,128)S(1)}, u32[]{:S(2)}, u32[]{:S(2)}) %collective-permute-start.7) | collective-permute-done | bytes 262176 | tf_op jit(solution)/shard_map/ppermute | solution.py:207
  47.0 0.0 collective-permute-done.8
  47.0 0.8 %add_add_fusion = f32[512,128]{1,0:T(8,128)} fusion(f32[512,128]{1,0:T(8,128)S(1)} %collective-permute-done.8, f32[512,128]{1,0:T(8,128)S(1)} %get-tuple-element.13, f32[512,128]{1,0:T(8,128)S(1)} %collective-permute-done.7), kind=kLoop, calls=%fused_computation | loop fusion | flops 131072 | bytes 1048576 | tf_op jit(solution)/shard_map/add | solution.py:209
Async XLA Ops:
  0.0 18.0 %collective-permute-start = (f32[512,128]{1,0:T(8,128)}, f32[512,128]{1,0:T(8,128)S(1)}, u32[]{:S(2)}, u32[]{:S(2)}) collective-permute-start(f32[512,128]{1,0:T(8,128)} %bitcast.4), channel_id=1, source_target_pairs={{0,128},{32,160},{64,192},{96,224},{128,0},{160,32},{192,64},{224,... | collective-permute-start | bytes 786440 | tf_op jit(solution)/shard_map/ppermute | solution.py:149
  5.4 15.3 %collective-permute-start.4 = (f32[512,128]{1,0:T(8,128)}, f32[512,128]{1,0:T(8,128)S(1)}, u32[]{:S(2)}, u32[]{:S(2)}) collective-permute-start(f32[512,128]{1,0:T(8,128)} %bitcast.5), channel_id=1, source_target_pairs={{0,96},{32,0},{64,32},{96,64},{128,224},{160,128},{192,160},{224,1... | collective-permute-start | bytes 786440 | tf_op jit(solution)/shard_map/ppermute | solution.py:135
  8.2 17.0 %collective-permute-start.5 = (f32[512,128]{1,0:T(8,128)}, f32[512,128]{1,0:T(8,128)S(1)}, u32[]{:S(2)}, u32[]{:S(2)}) collective-permute-start(f32[512,128]{1,0:T(8,128)} %bitcast.6), channel_id=1, source_target_pairs={{0,64},{32,96},{64,0},{96,32},{128,192},{160,224},{192,128},{224,1... | collective-permute-start | bytes 786440 | tf_op jit(solution)/shard_map/ppermute | solution.py:135
  9.0 16.2 %collective-permute-start.6 = (f32[512,128]{1,0:T(8,128)}, f32[512,128]{1,0:T(8,128)S(1)}, u32[]{:S(2)}, u32[]{:S(2)}) collective-permute-start(f32[512,128]{1,0:T(8,128)} %bitcast.7), channel_id=1, source_target_pairs={{0,32},{32,64},{64,96},{96,0},{128,160},{160,192},{192,224},{224,1... | collective-permute-start | bytes 786440 | tf_op jit(solution)/shard_map/ppermute | solution.py:135
  18.0 13.3 %collective-permute-start.2 = (f32[512,128]{1,0:T(8,128)S(1)}, f32[512,128]{1,0:T(8,128)S(1)}, u32[]{:S(2)}, u32[]{:S(2)}) collective-permute-start(f32[512,128]{1,0:T(8,128)S(1)} %collective-permute-done.s0), channel_id=1, source_target_pairs={{0,96},{32,0},{64,32},{96,64},{128,224},{160,128},{192,160},{224,1... | collective-permute-start | bytes 786440 | tf_op jit(solution)/shard_map/ppermute | solution.py:135
  20.7 13.9 %collective-permute-start.3 = (f32[512,128]{1,0:T(8,128)S(1)}, f32[512,128]{1,0:T(8,128)S(1)}, u32[]{:S(2)}, u32[]{:S(2)}) collective-permute-start(f32[512,128]{1,0:T(8,128)S(1)} %collective-permute-done.s0), channel_id=1, source_target_pairs={{0,32},{32,64},{64,96},{96,0},{128,160},{160,192},{192,224},{224,1... | collective-permute-start | bytes 786440 | tf_op jit(solution)/shard_map/ppermute | solution.py:135
  20.7 15.8 %collective-permute-start.1 = (f32[512,128]{1,0:T(8,128)S(1)}, f32[512,128]{1,0:T(8,128)S(1)}, u32[]{:S(2)}, u32[]{:S(2)}) collective-permute-start(f32[512,128]{1,0:T(8,128)S(1)} %collective-permute-done.s0), channel_id=1, source_target_pairs={{0,64},{32,96},{64,0},{96,32},{128,192},{160,224},{192,128},{224,1... | collective-permute-start | bytes 786440 | tf_op jit(solution)/shard_map/ppermute | solution.py:135
  23.0 1.2 %copy-start = (f32[3,3,3,32,256]{4,3,2,1,0:T(8,128)S(1)}, f32[3,3,3,32,256]{4,3,2,1,0:T(8,128)}, u32[]{:S(2)}) copy-start(f32[3,3,3,32,256]{4,3,2,1,0:T(8,128)} %kernel_ref.1) | copy-start | bytes 2654212
  24.2 1.0 %copy-start.1 = (f32[32,1,16,128]{3,2,1,0:T(8,128)S(1)}, f32[32,1,16,128]{3,2,1,0:T(8,128)}, u32[]{:S(2)}) copy-start(f32[32,1,16,128]{3,2,1,0:T(8,128)} %param.2) | copy-start | bytes 786436
  37.2 9.8 %collective-permute-start.7 = (f32[512,128]{1,0:T(8,128)S(1)}, f32[512,128]{1,0:T(8,128)S(1)}, u32[]{:S(2)}, u32[]{:S(2)}) collective-permute-start(f32[512,128]{1,0:T(8,128)S(1)} %off.1), channel_id=1, source_target_pairs={{1,2},{3,4},{5,6},{7,8},{9,10},{11,12},{13,14},{15,16},{17,18},{19... | collective-permute-start | bytes 786440 | tf_op jit(solution)/shard_map/ppermute | solution.py:207
  39.9 7.1 %collective-permute-start.8 = (f32[512,128]{1,0:T(8,128)S(1)}, f32[512,128]{1,0:T(8,128)S(1)}, u32[]{:S(2)}, u32[]{:S(2)}) collective-permute-start(f32[512,128]{1,0:T(8,128)S(1)} %get-tuple-element.14), channel_id=1, source_target_pairs={{0,1},{2,3},{4,5},{6,7},{8,9},{10,11},{12,13},{14,15},{16,17},{18,... | collective-permute-start | bytes 786440 | tf_op jit(solution)/shard_map/ppermute | solution.py:208

commit v3 on v2

--- a/solution.py
+++ b/solution.py
@@ -62,20 +62,20 @@
 
 
 def accumulate(shards, taps_ref, cells, total):
-    across = shards[0].shape[1]
+    across = shards[0][0].shape[1]
     height = cells.shape[1] // across
-    channels = shards[0].shape[0] // height
     half = cells.shape[0] // 6
-    for k, ref in enumerate(shards):
-        if ref is None:
+    channels = half // X
+    for k, refs in enumerate(shards):
+        if not refs:
             for e in range(6):
                 rows = pl.ds(e * half + k * channels, channels)
                 cells[rows, :] = jnp.zeros((channels, cells.shape[1]), BF16)
     for start in range(0, height, ROWS):
         for h in range(start, start + ROWS):
-            for k, ref in enumerate(shards):
-                if ref is not None:
-                    row = k * channels
+            for k, refs in enumerate(shards):
+                for j, ref in enumerate(refs):
+                    row = k * channels + j * channels // len(refs)
                     pack(ref, cells, h, height, [(e * half + row, (3 + e) * half + row) for e in range(3)])
         wide = pl.ds(start * across, ROWS * across)
         products = jnp.dot(
@@ -96,19 +96,20 @@
 
 def near_kernel(s0, s1, s2, s3, taps_ref, total, cells):
     total[...] = jnp.zeros_like(total)
-    accumulate((s0, s1, s2, s3), taps_ref, cells, total)
-
-
-def far_kernel(s0, s1, s3, taps_ref, near_ref, total, cells):
+    accumulate(((s0,), (s1,), (s2,), (s3,)), taps_ref, cells, total)
+
+
+def far_kernel(s0, s1a, s1b, s3a, s3b, taps_ref, near_ref, total, cells):
     total[...] = near_ref[...]
-    accumulate((s0, s1, None, s3), taps_ref, cells, total)
-
-
-def last_kernel(planes, ref, taps_ref, before_ref, *rest):
+    accumulate(((s0,), (s1a, s1b), (), (s3a, s3b)), taps_ref, cells, total)
+
+
+def last_kernel(planes, s2a, s2b, taps_ref, before_ref, *rest):
     *out_refs, cells, total = rest
-    across = ref.shape[1]
+    across = s2a.shape[1]
     height = cells.shape[1] // across
-    channels = ref.shape[0] // height
+    part = s2a.shape[0] // height
+    channels = 2 * part
     filters = before_ref.shape[0] // 3
     first = planes[0] * filters
     total[...] = before_ref[pl.ds(first, total.shape[0]), :]
@@ -116,7 +117,9 @@
     cells[pl.ds(9 * channels, unused), :] = jnp.zeros((unused, cells.shape[1]), BF16)
     for start in range(0, height, ROWS):
         for h in range(start, start + ROWS):
-            pack(ref, cells, h, height, [[(3 * t + e) * channels for t in range(3)] for e in range(3)])
+            for j, ref in enumerate((s2a, s2b)):
+                rows = [[(3 * t + e) * channels + j * part for t in range(3)] for e in range(3)]
+                pack(ref, cells, h, height, rows)
         products = jnp.dot(
             taps_ref[pl.ds(3 * first, 3 * total.shape[0]), :],
             cells[:, pl.ds(start * across, ROWS * across)],
@@ -130,13 +133,14 @@
             ]
 
 
-def spread(block):
-    return [
-        lax.ppermute(
-            block, "chan", [(g * X + i, g * X + (i - step) % X) for g in range(2) for i in range(X)]
-        )
-        for step in (1, 3, 2)
-    ]
+def from_x(block, step):
+    pairs = [(g * X + i, g * X + (i - step) % X) for g in range(2) for i in range(X)]
+    return lax.ppermute(block, "chan", pairs)
+
+
+def divide_kernel(whole_ref, order_ref, low_ref, high_ref):
+    low_ref[...] = whole_ref[: low_ref.shape[0]]
+    high_ref[...] = whole_ref[low_ref.shape[0] :]
 
 
 def local(volume, kernel):
@@ -147,8 +151,7 @@
     limit = pltpu.CompilerParams(vmem_limit_bytes=24 * 1024 * 1024)
     own = volume.reshape(cells, across)
     other = lax.ppermute(own, "chan", [(i, (i + X) % (2 * X)) for i in range(2 * X)])
-    s1, s3, s2 = spread(own)
-    t1, t3, t2 = spread(other)
+    s1, s3, s2 = [from_x(own, step) for step in (1, 3, 2)]
     weights = jax.ShapeDtypeStruct((9 * filters, 9 * half), BF16)
     last_weights = jax.ShapeDtypeStruct((9 * filters, 3 * half), BF16)
     near_taps, far_taps, last_taps = pl.pallas_call(
@@ -158,6 +161,18 @@
         cost_estimate=pl.CostEstimate(flops=0, bytes_accessed=4_000_000, transcendentals=0),
         name="taps",
     )(kernel)
+
+    part = jax.ShapeDtypeStruct((cells // 2, across), F32)
+    low, high = pl.pallas_call(
+        divide_kernel,
+        out_shape=(part, part),
+        in_specs=[pl.BlockSpec(memory_space=pltpu.VMEM), pl.BlockSpec(memory_space=pl.ANY)],
+        compiler_params=limit,
+        name="divide",
+    )(other, last_taps)
+    t3a, t1b = from_x(low, 3), from_x(high, 1)
+    t3b, t1a = from_x(high, 3), from_x(low, 1)
+    t2a, t2b = from_x(t3a, 3), from_x(t1b, 1)
 
     def work(planes, part):
         return pl.CostEstimate(
@@ -183,7 +198,7 @@
         compiler_params=limit,
         cost_estimate=work(3, 1),
         name="far",
-    )(other, t1, t3, far_taps, before)
+    )(other, t1a, t1b, t3a, t3b, far_taps, before)
 
     def last(name, *taps):
         part = jax.ShapeDtypeStruct((filters * height, across), F32)
@@ -197,7 +212,7 @@
             compiler_params=limit,
             cost_estimate=work(len(taps), 0.25),
             name=name,
-        )(t2, last_taps, before)
+        )(t2a, t2b, last_taps, before)
 
     (off,) = last("off", 0)
     on, mid = last("rest", 1, 2)

time: 47.9 us -> 45.7 us (0.954)
  the two profiles are of different devices: /device:TPU:64 before, /device:TPU:1 now
where the time goes in v3:
time: 45.7 us; the launch traced here: 44.9 us
  starting transfers between devices  27.4 us (60%)
  waiting for transfers between devices  9.25 us (20%)
  Pallas kernels  6.18 us (14%)
  local copies, waits for them, and re-layouts  1.17 us (3%)
  other arithmetic  0.75 us (2%)
    ppermute x9, starting transfers between devices, from_x(): return lax.ppermute(block, 'chan', pairs)  15.4 us
    ppermute x1, starting transfers between devices, local(): lax.ppermute(own, 'chan', [(i, (i + X) % (2 * X)) for i in range(2 * X)])  7.74 us
    ppermute x9, waiting for transfers between devices, from_x(): return lax.ppermute(block, 'chan', pairs)  6.07 us
    ppermute x1, starting transfers between devices, local(): off = lax.ppermute(off, 'depth', between + [(j, i) for i, j in between])  4.2 us
    ppermute x1, waiting for transfers between devices, local(): off = lax.ppermute(off, 'depth', between + [(j, i) for i, j in between])  3.18 us
    pallas_call x1, Pallas kernels, local(): pl.pallas_call(near_kernel, out_shape=total, scratch_shapes=[packed], com...  1.99 us
    pallas_call x1, Pallas kernels, local(): pl.pallas_call(far_kernel, out_shape=total, scratch_shapes=[packed], comp...  1.91 us
    pallas_call x2, Pallas kernels, last(): pl.pallas_call(functools.partial(last_kernel, taps), out_shape=[part] * l...  1.34 us
  transfers between devices with their start and end apart: 12, of which 3 were waited for; matrix products, arithmetic and copies ran while one was open for 0% of the time, Pallas kernels for 12%

profile of v3, /device:TPU:1, one launch (start us, length us, event | category | flops | bytes accessed | tf_op | source)
XLA Modules:
  0.0 44.9 jit_solution(12090756876034744139)
XLA Ops:
  0.0 7.7 %collective-permute-start = (f32[512,128]{1,0:T(8,128)}, f32[512,128]{1,0:T(8,128)S(1)}, u32[]{:S(2)}, u32[]{:S(2)}) collective-permute-start(f32[512,128]{1,0:T(8,128)} %bitcast.4), channel_id=1, source_target_pairs={{0,128},{32,160},{64,192},{96,224},{128,0},{160,32},{192,64},{224,... | collective-permute-start | bytes 786440 | tf_op jit(solution)/shard_map/ppermute | solution.py:153
  7.7 2.5 %collective-permute-start.7 = (f32[512,128]{1,0:T(8,128)}, f32[512,128]{1,0:T(8,128)S(1)}, u32[]{:S(2)}, u32[]{:S(2)}) collective-permute-start(f32[512,128]{1,0:T(8,128)} %bitcast.5), channel_id=1, source_target_pairs={{0,96},{32,0},{64,32},{96,64},{128,224},{160,128},{192,160},{224,1... | collective-permute-start | bytes 786440 | tf_op jit(solution)/shard_map/ppermute | solution.py:138
  10.2 0.5 %collective-permute-start.8 = (f32[512,128]{1,0:T(8,128)}, f32[512,128]{1,0:T(8,128)S(1)}, u32[]{:S(2)}, u32[]{:S(2)}) collective-permute-start(f32[512,128]{1,0:T(8,128)} %bitcast.6), channel_id=1, source_target_pairs={{0,64},{32,96},{64,0},{96,32},{128,192},{160,224},{192,128},{224,1... | collective-permute-start | bytes 786440 | tf_op jit(solution)/shard_map/ppermute | solution.py:138
  10.7 0.6 %collective-permute-start.9 = (f32[512,128]{1,0:T(8,128)}, f32[512,128]{1,0:T(8,128)S(1)}, u32[]{:S(2)}, u32[]{:S(2)}) collective-permute-start(f32[512,128]{1,0:T(8,128)} %bitcast.7), channel_id=1, source_target_pairs={{0,32},{32,64},{64,96},{96,0},{128,160},{160,192},{192,224},{224,1... | collective-permute-start | bytes 786440 | tf_op jit(solution)/shard_map/ppermute | solution.py:138
  11.3 0.0 copy-start
  11.3 1.2 %copy-done = f32[3,3,3,32,256]{4,3,2,1,0:T(8,128)S(1)} copy-done((f32[3,3,3,32,256]{4,3,2,1,0:T(8,128)S(1)}, f32[3,3,3,32,256]{4,3,2,1,0:T(8,128)}, u32[]{:S(2)}) %copy-start) | copy-done | bytes 884760
  12.5 0.9 %taps.1 = (bf16[288,1152]{1,0:T(8,128)(2,1)S(1)}, bf16[288,1152]{1,0:T(8,128)(2,1)S(1)}, bf16[288,384]{1,0:T(8,128)(2,1)S(1)}) custom-call(f32[3,3,3,32,256]{4,3,2,1,0:T(8,128)S(1)} %copy-done), custom_call_target="tpu_custom_call" | custom-call | bytes 4000000 | tf_op jit(solution)/shard_map/taps/pallas_call | solution.py:157
  13.4 0.0 copy-start.1
  13.5 0.0 collective-permute-done.whole_ref.s0
  13.5 2.8 %collective-permute-start.1 = (f32[256,128]{1,0:T(8,128)S(1)}, f32[256,128]{1,0:T(8,128)S(1)}, u32[]{:S(2)}, u32[]{:S(2)}) collective-permute-start(f32[256,128]{1,0:T(8,128)S(1)} %get-tuple-element.13), channel_id=1, source_target_pairs={{0,32},{32,64},{64,96},{96,0},{128,160},{160,192},{192,224},{224,1... | collective-permute-start | bytes 393224 | tf_op jit(solution)/shard_map/ppermute | solution.py:138
  16.3 1.4 %collective-permute-start.3 = (f32[256,128]{1,0:T(8,128)S(1)}, f32[256,128]{1,0:T(8,128)S(1)}, u32[]{:S(2)}, u32[]{:S(2)}) collective-permute-start(f32[256,128]{1,0:T(8,128)S(1)} %get-tuple-element.14), channel_id=1, source_target_pairs={{0,96},{32,0},{64,32},{96,64},{128,224},{160,128},{192,160},{224,1... | collective-permute-start | bytes 393224 | tf_op jit(solution)/shard_map/ppermute | solution.py:138
  17.6 0.0 collective-permute-done.7.s1
  17.6 2.1 %collective-permute-start.5 = (f32[256,128]{1,0:T(8,128)S(1)}, f32[256,128]{1,0:T(8,128)S(1)}, u32[]{:S(2)}, u32[]{:S(2)}) collective-permute-start(f32[256,128]{1,0:T(8,128)S(1)} %get-tuple-element.13), channel_id=1, source_target_pairs={{0,96},{32,0},{64,32},{96,64},{128,224},{160,128},{192,160},{224,1... | collective-permute-start | bytes 393224 | tf_op jit(solution)/shard_map/ppermute | solution.py:138
  19.8 0.0 collective-permute-done.8.s2
  19.8 2.8 %collective-permute-start.6 = (f32[256,128]{1,0:T(8,128)S(1)}, f32[256,128]{1,0:T(8,128)S(1)}, u32[]{:S(2)}, u32[]{:S(2)}) collective-permute-start(f32[256,128]{1,0:T(8,128)S(1)} %get-tuple-element.14), channel_id=1, source_target_pairs={{0,32},{32,64},{64,96},{96,0},{128,160},{160,192},{192,224},{224,1... | collective-permute-start | bytes 393224 | tf_op jit(solution)/shard_map/ppermute | solution.py:138
  22.6 6.0 %collective-permute-done.1.s3a = f32[256,128]{1,0:T(8,128)S(1)} collective-permute-done((f32[256,128]{1,0:T(8,128)S(1)}, f32[256,128]{1,0:T(8,128)S(1)}, u32[]{:S(2)}, u32[]{:S(2)}) %collective-permute-start.1) | collective-permute-done | bytes 131104 | tf_op jit(solution)/shard_map/ppermute | solution.py:138
  28.6 0.0 collective-permute-start.2
  28.6 0.0 collective-permute-done.3.s1b
  28.6 2.7 %collective-permute-start.4 = (f32[256,128]{1,0:T(8,128)S(1)}, f32[256,128]{1,0:T(8,128)S(1)}, u32[]{:S(2)}, u32[]{:S(2)}) collective-permute-start(f32[256,128]{1,0:T(8,128)S(1)} %collective-permute-done.3.s1b), channel_id=1, source_target_pairs={{0,96},{32,0},{64,32},{96,64},{128,224},{160,128},{192,160},{224,1... | collective-permute-start | bytes 393224 | tf_op jit(solution)/shard_map/ppermute | solution.py:138
  31.3 0.0 collective-permute-done.9.s3
  31.3 0.0 copy-done.1
  31.3 2.0 %near.1.near_ref = f32[96,2304]{1,0:T(8,128)S(1)} custom-call(f32[512,128]{1,0:T(8,128)S(1)} %bitcast.8, f32[512,128]{1,0:T(8,128)S(1)} %collective-permute-done.7.s1, f32[512,128]{1,0:T(8,128)S(1)} %collective-permute-done.8.s2, f32[512,128]{1,0:T(8,128)S(1)} %collective-permute-done.9.s3, bf16[288,1152]{1,0:T(8,128)(2,1)S(1)} %get-tuple-element.16.taps_ref), custom_call_target="tpu_custom_call" | custom-call | flops 1358954496 | bytes 3000000 | tf_op jit(solution)/shard_map/near/pallas_call | solution.py:186
  33.3 0.0 collective-permute-done.5.s1a
  33.3 0.0 collective-permute-done.6.s3b
  33.3 1.9 %far.1.before_ref = f32[96,2304]{1,0:T(8,128)S(1)} custom-call(f32[512,128]{1,0:T(8,128)S(1)} %collective-permute-done.whole_ref.s0, f32[256,128]{1,0:T(8,128)S(1)} %collective-permute-done.5.s1a, f32[256,128]{1,0:T(8,128)S(1)} %collective-permute-done.3.s1b, f32[256,128]{1,0:T(8,128)S(1)} %collective-permute-done.1.s3a, ...), custom_call_target="tpu_custom_call" | custom-call | flops 1358954496 | bytes 3000000 | tf_op jit(solution)/shard_map/far/pallas_call | solution.py:194
  35.2 0.1 collective-permute-done.2.s2a
  35.3 0.0 collective-permute-done.4.s2b
  35.3 0.6 %off.1 = f32[512,128]{1,0:T(8,128)S(1)} custom-call(f32[256,128]{1,0:T(8,128)S(1)} %collective-permute-done.2.s2a, f32[256,128]{1,0:T(8,128)S(1)} %collective-permute-done.4.s2b, bf16[288,384]{1,0:T(8,128)(2,1)S(1)} %get-tuple-element.12.order_ref.taps_ref, f32[96,2304]{1,0:T(8,128)S(1)} %far.1.before_ref), custom_call_target="tpu_custom_call" | custom-call | flops 113246208 | bytes 3000000 | tf_op jit(solution)/shard_map/off/pallas_call | solution.py:205
  35.9 4.2 %collective-permute-start.10 = (f32[512,128]{1,0:T(8,128)S(1)}, f32[512,128]{1,0:T(8,128)S(1)}, u32[]{:S(2)}, u32[]{:S(2)}) collective-permute-start(f32[512,128]{1,0:T(8,128)S(1)} %off.1), channel_id=1, source_target_pairs={{1,2},{3,4},{5,6},{7,8},{9,10},{11,12},{13,14},{15,16},{17,18},{19... | collective-permute-start | bytes 786440 | tf_op jit(solution)/shard_map/ppermute | solution.py:222
  40.1 0.8 %rest.1 = (f32[512,128]{1,0:T(8,128)S(1)}, f32[512,128]{1,0:T(8,128)S(1)}) custom-call(f32[256,128]{1,0:T(8,128)S(1)} %collective-permute-done.2.s2a, f32[256,128]{1,0:T(8,128)S(1)} %collective-permute-done.4.s2b, bf16[288,384]{1,0:T(8,128)(2,1)S(1)} %get-tuple-element.12.order_ref.taps_ref, f32[96,2304]{1,0:T(8,128)S(1)} %far.1.before_ref), custom_call_target="tpu_custom_call" | custom-call | flops 226492416 | bytes 3000000 | tf_op jit(solution)/shard_map/rest/pallas_call | solution.py:205
  40.8 0.1 collective-permute-start.11
  40.9 3.2 %collective-permute-done.10 = f32[512,128]{1,0:T(8,128)S(1)} collective-permute-done((f32[512,128]{1,0:T(8,128)S(1)}, f32[512,128]{1,0:T(8,128)S(1)}, u32[]{:S(2)}, u32[]{:S(2)}) %collective-permute-start.10) | collective-permute-done | bytes 262176 | tf_op jit(solution)/shard_map/ppermute | solution.py:222
  44.1 0.0 collective-permute-done.11
  44.1 0.8 %add_add_fusion = f32[512,128]{1,0:T(8,128)} fusion(f32[512,128]{1,0:T(8,128)S(1)} %collective-permute-done.11, f32[512,128]{1,0:T(8,128)S(1)} %get-tuple-element.17, f32[512,128]{1,0:T(8,128)S(1)} %collective-permute-done.10), kind=kLoop, calls=%fused_computation | loop fusion | flops 131072 | bytes 1048576 | tf_op jit(solution)/shard_map/add | solution.py:224
  (1 shorter events, 0.0 us)
Async XLA Ops:
  0.0 13.5 %collective-permute-start = (f32[512,128]{1,0:T(8,128)}, f32[512,128]{1,0:T(8,128)S(1)}, u32[]{:S(2)}, u32[]{:S(2)}) collective-permute-start(f32[512,128]{1,0:T(8,128)} %bitcast.4), channel_id=1, source_target_pairs={{0,128},{32,160},{64,192},{96,224},{128,0},{160,32},{192,64},{224,... | collective-permute-start | bytes 786440 | tf_op jit(solution)/shard_map/ppermute | solution.py:153
  7.7 9.9 %collective-permute-start.7 = (f32[512,128]{1,0:T(8,128)}, f32[512,128]{1,0:T(8,128)S(1)}, u32[]{:S(2)}, u32[]{:S(2)}) collective-permute-start(f32[512,128]{1,0:T(8,128)} %bitcast.5), channel_id=1, source_target_pairs={{0,96},{32,0},{64,32},{96,64},{128,224},{160,128},{192,160},{224,1... | collective-permute-start | bytes 786440 | tf_op jit(solution)/shard_map/ppermute | solution.py:138
  10.2 9.6 %collective-permute-start.8 = (f32[512,128]{1,0:T(8,128)}, f32[512,128]{1,0:T(8,128)S(1)}, u32[]{:S(2)}, u32[]{:S(2)}) collective-permute-start(f32[512,128]{1,0:T(8,128)} %bitcast.6), channel_id=1, source_target_pairs={{0,64},{32,96},{64,0},{96,32},{128,192},{160,224},{192,128},{224,1... | collective-permute-start | bytes 786440 | tf_op jit(solution)/shard_map/ppermute | solution.py:138
  10.7 20.5 %collective-permute-start.9 = (f32[512,128]{1,0:T(8,128)}, f32[512,128]{1,0:T(8,128)S(1)}, u32[]{:S(2)}, u32[]{:S(2)}) collective-permute-start(f32[512,128]{1,0:T(8,128)} %bitcast.7), channel_id=1, source_target_pairs={{0,32},{32,64},{64,96},{96,0},{128,160},{160,192},{192,224},{224,1... | collective-permute-start | bytes 786440 | tf_op jit(solution)/shard_map/ppermute | solution.py:138
  11.3 1.2 %copy-start = (f32[3,3,3,32,256]{4,3,2,1,0:T(8,128)S(1)}, f32[3,3,3,32,256]{4,3,2,1,0:T(8,128)}, u32[]{:S(2)}) copy-start(f32[3,3,3,32,256]{4,3,2,1,0:T(8,128)} %kernel_ref.1) | copy-start | bytes 2654212
  13.4 17.8 %copy-start.1 = (f32[32,1,16,128]{3,2,1,0:T(8,128)S(1)}, f32[32,1,16,128]{3,2,1,0:T(8,128)}, u32[]{:S(2)}) copy-start(f32[32,1,16,128]{3,2,1,0:T(8,128)} %param.2) | copy-start | bytes 786436
  13.5 15.1 %collective-permute-start.1 = (f32[256,128]{1,0:T(8,128)S(1)}, f32[256,128]{1,0:T(8,128)S(1)}, u32[]{:S(2)}, u32[]{:S(2)}) collective-permute-start(f32[256,128]{1,0:T(8,128)S(1)} %get-tuple-element.13), channel_id=1, source_target_pairs={{0,32},{32,64},{64,96},{96,0},{128,160},{160,192},{192,224},{224,1... | collective-permute-start | bytes 393224 | tf_op jit(solution)/shard_map/ppermute | solution.py:138
  16.3 12.3 %collective-permute-start.3 = (f32[256,128]{1,0:T(8,128)S(1)}, f32[256,128]{1,0:T(8,128)S(1)}, u32[]{:S(2)}, u32[]{:S(2)}) collective-permute-start(f32[256,128]{1,0:T(8,128)S(1)} %get-tuple-element.14), channel_id=1, source_target_pairs={{0,96},{32,0},{64,32},{96,64},{128,224},{160,128},{192,160},{224,1... | collective-permute-start | bytes 393224 | tf_op jit(solution)/shard_map/ppermute | solution.py:138
  17.6 15.6 %collective-permute-start.5 = (f32[256,128]{1,0:T(8,128)S(1)}, f32[256,128]{1,0:T(8,128)S(1)}, u32[]{:S(2)}, u32[]{:S(2)}) collective-permute-start(f32[256,128]{1,0:T(8,128)S(1)} %get-tuple-element.13), channel_id=1, source_target_pairs={{0,96},{32,0},{64,32},{96,64},{128,224},{160,128},{192,160},{224,1... | collective-permute-start | bytes 393224 | tf_op jit(solution)/shard_map/ppermute | solution.py:138
  19.8 13.5 %collective-permute-start.6 = (f32[256,128]{1,0:T(8,128)S(1)}, f32[256,128]{1,0:T(8,128)S(1)}, u32[]{:S(2)}, u32[]{:S(2)}) collective-permute-start(f32[256,128]{1,0:T(8,128)S(1)} %get-tuple-element.14), channel_id=1, source_target_pairs={{0,32},{32,64},{64,96},{96,0},{128,160},{160,192},{192,224},{224,1... | collective-permute-start | bytes 393224 | tf_op jit(solution)/shard_map/ppermute | solution.py:138
  28.6 6.7 %collective-permute-start.2 = (f32[256,128]{1,0:T(8,128)S(1)}, f32[256,128]{1,0:T(8,128)S(1)}, u32[]{:S(2)}, u32[]{:S(2)}) collective-permute-start(f32[256,128]{1,0:T(8,128)S(1)} %collective-permute-done.1.s3a), channel_id=1, source_target_pairs={{0,32},{32,64},{64,96},{96,0},{128,160},{160,192},{192,224},{224,1... | collective-permute-start | bytes 393224 | tf_op jit(solution)/shard_map/ppermute | solution.py:138
  28.6 6.7 %collective-permute-start.4 = (f32[256,128]{1,0:T(8,128)S(1)}, f32[256,128]{1,0:T(8,128)S(1)}, u32[]{:S(2)}, u32[]{:S(2)}) collective-permute-start(f32[256,128]{1,0:T(8,128)S(1)} %collective-permute-done.3.s1b), channel_id=1, source_target_pairs={{0,96},{32,0},{64,32},{96,64},{128,224},{160,128},{192,160},{224,1... | collective-permute-start | bytes 393224 | tf_op jit(solution)/shard_map/ppermute | solution.py:138
  35.9 8.3 %collective-permute-start.10 = (f32[512,128]{1,0:T(8,128)S(1)}, f32[512,128]{1,0:T(8,128)S(1)}, u32[]{:S(2)}, u32[]{:S(2)}) collective-permute-start(f32[512,128]{1,0:T(8,128)S(1)} %off.1), channel_id=1, source_target_pairs={{1,2},{3,4},{5,6},{7,8},{9,10},{11,12},{13,14},{15,16},{17,18},{19... | collective-permute-start | bytes 786440 | tf_op jit(solution)/shard_map/ppermute | solution.py:222
  40.8 3.3 %collective-permute-start.11 = (f32[512,128]{1,0:T(8,128)S(1)}, f32[512,128]{1,0:T(8,128)S(1)}, u32[]{:S(2)}, u32[]{:S(2)}) collective-permute-start(f32[512,128]{1,0:T(8,128)S(1)} %get-tuple-element.18), channel_id=1, source_target_pairs={{0,1},{2,3},{4,5},{6,7},{8,9},{10,11},{12,13},{14,15},{16,17},{18,... | collective-permute-start | bytes 786440 | tf_op jit(solution)/shard_map/ppermute | solution.py:223

commit v4 on v3

--- a/solution.py
+++ b/solution.py
@@ -9,6 +9,7 @@
 
 X = 4
 ROWS = 2
+LIMIT = pltpu.CompilerParams(vmem_limit_bytes=24 * 1024 * 1024)
 F32, BF16 = jnp.float32, jnp.bfloat16
 
 
@@ -34,7 +35,8 @@
                 blocks = []
                 for e in range(3):
                     values = pltpu.roll(kernel_ref[plane, b, e, :, columns], turn, 1)
-                    high, low = split(values)
+                    mirrored = pltpu.roll(values, half // 2, 1)
+                    high, low = split(jnp.where(slot % 2 * core == 1, mirrored, values))
                     out_ref[rows, pl.ds(e * half, half)] = high
                     out_ref[rows, pl.ds((3 + e) * half, half)] = high
                     out_ref[rows, pl.ds((6 + e) * half, half)] = low
@@ -94,12 +96,12 @@
             total[pl.ds(a * filters, filters), place] += products[row : row + filters]
 
 
-def near_kernel(s0, s1, s2, s3, taps_ref, total, cells):
+def near_kernel(s0, s1, s3, s2a, s2b, taps_ref, total, cells):
     total[...] = jnp.zeros_like(total)
-    accumulate(((s0,), (s1,), (s2,), (s3,)), taps_ref, cells, total)
-
-
-def far_kernel(s0, s1a, s1b, s3a, s3b, taps_ref, near_ref, total, cells):
+    accumulate(((s0,), (s1,), (s2a, s2b), (s3,)), taps_ref, cells, total)
+
+
+def far_kernel(s0, s1a, s1b, s3b, s3a, taps_ref, near_ref, total, cells):
     total[...] = near_ref[...]
     accumulate(((s0,), (s1a, s1b), (), (s3a, s3b)), taps_ref, cells, total)
 
@@ -126,21 +128,61 @@
             preferred_element_type=F32,
         )
         scatter(products, total, filters, start, across)
+    depth = lax.axis_index("depth")
+    edge = (depth == 0) | (depth == lax.axis_size("depth") - 1)
     for a, out_ref in enumerate(out_refs):
         for h in range(height):
-            out_ref[pl.ds(h, filters, stride=height), :] = total[
-                pl.ds(a * filters, filters), pl.ds((h + 1) * across, across)
-            ]
-
-
-def from_x(block, step):
-    pairs = [(g * X + i, g * X + (i - step) % X) for g in range(2) for i in range(X)]
-    return lax.ppermute(block, "chan", pairs)
+            values = total[pl.ds(a * filters, filters), pl.ds((h + 1) * across, across)]
+            if planes[a] == 0:
+                values = jnp.where(edge, 0.0, values)
+            out_ref[pl.ds(h, filters, stride=height), :] = values
 
 
 def divide_kernel(whole_ref, order_ref, low_ref, high_ref):
     low_ref[...] = whole_ref[: low_ref.shape[0]]
     high_ref[...] = whole_ref[low_ref.shape[0] :]
+
+
+def exchange(block, way):
+    planes = lax.axis_size("depth")
+    pairs = []
+    for c in range(2 * X):
+        for d in range(planes):
+            step = way if d % 2 else -way
+            pairs.append((c * planes + d, (c // X * X + (c + step) % X) * planes + d))
+    return lax.ppermute(block, ("chan", "depth"), pairs)
+
+
+def half_kernel(low, whole_ref, out_ref):
+    out_ref[...] = whole_ref[pl.ds(0 if low else out_ref.shape[0], out_ref.shape[0]), :]
+
+
+def half(whole, low):
+    return pl.pallas_call(
+        functools.partial(half_kernel, low),
+        out_shape=jax.ShapeDtypeStruct((whole.shape[0] // 2, whole.shape[1]), F32),
+        compiler_params=LIMIT,
+        name="half",
+    )(whole)
+
+
+def spread_own(whole):
+    s1, s3 = exchange(whole, 1), exchange(whole, -1)
+    return s1, s3, exchange(half(s1, True), 1), exchange(half(s3, False), -1)
+
+
+def spread(whole, order):
+    part = jax.ShapeDtypeStruct((whole.shape[0] // 2, whole.shape[1]), F32)
+    low, high = pl.pallas_call(
+        divide_kernel,
+        out_shape=(part, part),
+        in_specs=[pl.BlockSpec(memory_space=pltpu.VMEM), pl.BlockSpec(memory_space=pl.ANY)],
+        compiler_params=LIMIT,
+        name="divide",
+    )(whole, order)
+    s1a, s3b = exchange(low, 1), exchange(high, -1)
+    s1b, s3a = exchange(high, 1), exchange(low, -1)
+    return s1a, s1b, s3b, s3a, exchange(s1a, 1), exchange(s3b, -1)
 
 
 def local(volume, kernel):
@@ -148,31 +190,17 @@
     shard, _, height, across = volume.shape
     half = channels // 2
     cells = shard * height
-    limit = pltpu.CompilerParams(vmem_limit_bytes=24 * 1024 * 1024)
     own = volume.reshape(cells, across)
     other = lax.ppermute(own, "chan", [(i, (i + X) % (2 * X)) for i in range(2 * X)])
-    s1, s3, s2 = [from_x(own, step) for step in (1, 3, 2)]
     weights = jax.ShapeDtypeStruct((9 * filters, 9 * half), BF16)
     last_weights = jax.ShapeDtypeStruct((9 * filters, 3 * half), BF16)
     near_taps, far_taps, last_taps = pl.pallas_call(
         taps_kernel,
         out_shape=(weights, weights, last_weights),
-        compiler_params=limit,
+        compiler_params=LIMIT,
         cost_estimate=pl.CostEstimate(flops=0, bytes_accessed=4_000_000, transcendentals=0),
         name="taps",
     )(kernel)
-
-    part = jax.ShapeDtypeStruct((cells // 2, across), F32)
-    low, high = pl.pallas_call(
-        divide_kernel,
-        out_shape=(part, part),
-        in_specs=[pl.BlockSpec(memory_space=pltpu.VMEM), pl.BlockSpec(memory_space=pl.ANY)],
-        compiler_params=limit,
-        name="divide",
-    )(other, last_taps)
-    t3a, t1b = from_x(low, 3), from_x(high, 1)
-    t3b, t1a = from_x(high, 3), from_x(low, 1)
-    t2a, t2b = from_x(t3a, 3), from_x(t1b, 1)
 
     def work(planes, part):
         return pl.CostEstimate(
@@ -187,18 +215,19 @@
         near_kernel,
         out_shape=total,
         scratch_shapes=[packed],
-        compiler_params=limit,
+        compiler_params=LIMIT,
         cost_estimate=work(3, 1),
         name="near",
-    )(own, s1, s2, s3, near_taps)
+    )(own, *spread_own(own), near_taps)
+    *most, t2a, t2b = spread(other, before)
     before = pl.pallas_call(
         far_kernel,
         out_shape=total,
         scratch_shapes=[packed],
-        compiler_params=limit,
+        compiler_params=LIMIT,
         cost_estimate=work(3, 1),
         name="far",
-    )(other, t1a, t1b, t3a, t3b, far_taps, before)
+    )(other, *most, far_taps, before)
 
     def last(name, *taps):
         part = jax.ShapeDtypeStruct((filters * height, across), F32)
@@ -209,7 +238,7 @@
                 pltpu.VMEM((3 * half, height * across), BF16),
                 pltpu.VMEM((len(taps) * filters, total.shape[1]), F32),
             ],
-            compiler_params=limit,
+            compiler_params=LIMIT,
             cost_estimate=work(len(taps), 0.25),
             name=name,
         )(t2a, t2b, last_taps, before)
@@ -219,7 +248,8 @@
     planes = lax.axis_size("depth")
     between = [(i, i + 1) for i in range(1, planes - 1, 2)]
     within = [(i, i + 1) for i in range(0, planes, 2)]
-    off = lax.ppermute(off, "depth", between + [(j, i) for i, j in between])
+    ends = [(0, 0), (planes - 1, planes - 1)]
+    off = lax.ppermute(off, "depth", between + [(j, i) for i, j in between] + ends)
     on = lax.ppermute(on, "depth", within + [(j, i) for i, j in within])
     return (mid + off + on).reshape(filters, 1, height, across)
 

time: 45.7 us -> 47.8 us (1.046)
  waiting for transfers between devices: 9.25 us -> 5.94 us
  starting transfers between devices: 27.4 us -> 30.1 us
  Pallas kernels: 6.18 us -> 8.84 us
    ppermute x10 -> x11, starting transfers between devices: 19.6 us -> 22.9 us  [the longest x10 13 us: exchange(): return lax.ppermute(block, ('chan', 'depth'), pairs)]
    ppermute x10 -> x11, waiting for transfers between devices: 9.24 us -> 5.93 us  [the longest x1 3.18 us: local(): lax.ppermute(off, 'depth', between + [(j, i) for i, j in between] + ends)]
    pallas_call x1, Pallas kernels: 0.92 us -> 3.55 us  [local(): pl.pallas_call(taps_kernel, out_shape=(weights, weights, last_weights), c...]
    ppermute x1, starting transfers between devices: 7.74 us -> 7.1 us  [local(): lax.ppermute(own, 'chan', [(i, (i + X) % (2 * X)) for i in range(2 * X)])]
  transfers between devices with their start and end apart: 12 -> 13, of which waited for: 3 -> 3; matrix products, arithmetic and copies ran while one was open for 0% -> 0% of each run, Pallas kernels for 12% -> 18%
where the time goes in v4:
time: 47.8 us; the launch traced here: 47 us
  starting transfers between devices  30.1 us (63%)
  Pallas kernels  8.84 us (18%)
  waiting for transfers between devices  5.94 us (12%)
  local copies, waits for them, and re-layouts  1.17 us (2%)
  other arithmetic  0.76 us (2%)
    ppermute x10, starting transfers between devices, exchange(): return lax.ppermute(block, ('chan', 'depth'), pairs)  13 us
    ppermute x1, starting transfers between devices, local(): lax.ppermute(off, 'depth', between + [(j, i) for i, j in between] + ends)  9.93 us
    ppermute x1, starting transfers between devices, local(): lax.ppermute(own, 'chan', [(i, (i + X) % (2 * X)) for i in range(2 * X)])  7.1 us
    pallas_call x1, Pallas kernels, local(): pl.pallas_call(taps_kernel, out_shape=(weights, weights, last_weights), c...  3.55 us
    ppermute x1, waiting for transfers between devices, local(): lax.ppermute(off, 'depth', between + [(j, i) for i, j in between] + ends)  3.18 us
    ppermute x10, waiting for transfers between devices, exchange(): return lax.ppermute(block, ('chan', 'depth'), pairs)  2.76 us
    pallas_call x1, Pallas kernels, local(): pl.pallas_call(near_kernel, out_shape=total, scratch_shapes=[packed], com...  1.99 us
    pallas_call x1, Pallas kernels, local(): pl.pallas_call(far_kernel, out_shape=total, scratch_shapes=[packed], comp...  1.91 us
  transfers between devices with their start and end apart: 13, of which 3 were waited for; matrix products, arithmetic and copies ran while one was open for 0% of the time, Pallas kernels for 18%

profile of v4, /device:TPU:1, one launch (start us, length us, event | category | flops | bytes accessed | tf_op | source)
XLA Modules:
  0.0 47.0 jit_solution(3140159513503968254)
XLA Ops:
  0.0 2.0 %collective-permute-start.1 = (f32[512,128]{1,0:T(8,128)}, f32[512,128]{1,0:T(8,128)S(1)}, u32[]{:S(2)}, u32[]{:S(2)}) collective-permute-start(f32[512,128]{1,0:T(8,128)} %bitcast.4), channel_id=1, source_target_pairs={{0,96},{1,33},{2,98},{3,35},{4,100},{5,37},{6,102},{7,39},{8,104},... | collective-permute-start | bytes 786440 | tf_op jit(solution)/shard_map/ppermute | solution.py:153
  2.0 1.3 %collective-permute-start.2 = (f32[512,128]{1,0:T(8,128)}, f32[512,128]{1,0:T(8,128)S(1)}, u32[]{:S(2)}, u32[]{:S(2)}) collective-permute-start(f32[512,128]{1,0:T(8,128)} %bitcast.5), channel_id=1, source_target_pairs={{0,32},{1,97},{2,34},{3,99},{4,36},{5,101},{6,38},{7,103},{8,40},{... | collective-permute-start | bytes 786440 | tf_op jit(solution)/shard_map/ppermute | solution.py:153
  3.3 7.1 %collective-permute-start = (f32[512,128]{1,0:T(8,128)}, f32[512,128]{1,0:T(8,128)S(1)}, u32[]{:S(2)}, u32[]{:S(2)}) collective-permute-start(f32[512,128]{1,0:T(8,128)} %bitcast.6), channel_id=1, source_target_pairs={{0,128},{32,160},{64,192},{96,224},{128,0},{160,32},{192,64},{224,... | collective-permute-start | bytes 786440 | tf_op jit(solution)/shard_map/ppermute | solution.py:194
  10.4 0.0 collective-permute-done.1.whole_ref.s1
  10.4 0.1 collective-permute-start.3
  10.5 0.0 collective-permute-done.2.whole_ref.s3
  10.6 2.7 %collective-permute-start.4 = (f32[256,128]{1,0:T(8,128)S(1)}, f32[256,128]{1,0:T(8,128)S(1)}, u32[]{:S(2)}, u32[]{:S(2)}) collective-permute-start(f32[256,128]{1,0:T(8,128)S(1)} %half.3), channel_id=1, source_target_pairs={{0,32},{1,97},{2,34},{3,99},{4,36},{5,101},{6,38},{7,103},{8,40},{... | collective-permute-start | bytes 393224 | tf_op jit(solution)/shard_map/ppermute | solution.py:153
  13.3 0.0 copy-start
  13.3 1.2 %copy-done = f32[3,3,3,32,256]{4,3,2,1,0:T(8,128)S(1)} copy-done((f32[3,3,3,32,256]{4,3,2,1,0:T(8,128)S(1)}, f32[3,3,3,32,256]{4,3,2,1,0:T(8,128)}, u32[]{:S(2)}) %copy-start) | copy-done | bytes 884760
  14.5 0.0 copy-start.1
  14.5 3.6 %taps.1 = (bf16[288,1152]{1,0:T(8,128)(2,1)S(1)}, bf16[288,1152]{1,0:T(8,128)(2,1)S(1)}, bf16[288,384]{1,0:T(8,128)(2,1)S(1)}) custom-call(f32[3,3,3,32,256]{4,3,2,1,0:T(8,128)S(1)} %copy-done), custom_call_target="tpu_custom_call" | custom-call | bytes 4000000 | tf_op jit(solution)/shard_map/taps/pallas_call | solution.py:197
  18.0 0.0 collective-permute-done.3.s2a
  18.0 0.0 collective-permute-done.4.s2b
  18.0 0.0 copy-done.1
  18.0 2.0 %near.1.order_ref.near_ref = f32[96,2304]{1,0:T(8,128)S(1)} custom-call(f32[512,128]{1,0:T(8,128)S(1)} %bitcast.7, f32[512,128]{1,0:T(8,128)S(1)} %collective-permute-done.1.whole_ref.s1, f32[512,128]{1,0:T(8,128)S(1)} %collective-permute-done.2.whole_ref.s3, f32[256,128]{1,0:T(8,128)S(1)} %collective-permute-done.3.s2a, ...), custom_call_target="tpu_custom_call" | custom-call | flops 1358954496 | bytes 3000000 | tf_op jit(solution)/shard_map/near/pallas_call | solution.py:214
  20.0 0.0 collective-permute-done.whole_ref.s0
  20.1 0.1 collective-permute-start.5
  20.2 2.7 %collective-permute-start.7 = (f32[256,128]{1,0:T(8,128)S(1)}, f32[256,128]{1,0:T(8,128)S(1)}, u32[]{:S(2)}, u32[]{:S(2)}) collective-permute-start(f32[256,128]{1,0:T(8,128)S(1)} %get-tuple-element.14), channel_id=1, source_target_pairs={{0,32},{1,97},{2,34},{3,99},{4,36},{5,101},{6,38},{7,103},{8,40},{... | collective-permute-start | bytes 393224 | tf_op jit(solution)/shard_map/ppermute | solution.py:153
  22.8 0.0 collective-permute-start.10
  22.9 1.4 %collective-permute-start.9 = (f32[256,128]{1,0:T(8,128)S(1)}, f32[256,128]{1,0:T(8,128)S(1)}, u32[]{:S(2)}, u32[]{:S(2)}) collective-permute-start(f32[256,128]{1,0:T(8,128)S(1)} %get-tuple-element.14), channel_id=1, source_target_pairs={{0,96},{1,33},{2,98},{3,35},{4,100},{5,37},{6,102},{7,39},{8,104},... | collective-permute-start | bytes 393224 | tf_op jit(solution)/shard_map/ppermute | solution.py:153
  24.3 0.9 %collective-permute-done.5.s1a = f32[256,128]{1,0:T(8,128)S(1)} collective-permute-done((f32[256,128]{1,0:T(8,128)S(1)}, f32[256,128]{1,0:T(8,128)S(1)}, u32[]{:S(2)}, u32[]{:S(2)}) %collective-permute-start.5) | collective-permute-done | bytes 131104 | tf_op jit(solution)/shard_map/ppermute | solution.py:153
  25.2 0.0 collective-permute-start.6
  25.2 0.0 collective-permute-done.7.s3b
  25.2 2.7 %collective-permute-start.8 = (f32[256,128]{1,0:T(8,128)S(1)}, f32[256,128]{1,0:T(8,128)S(1)}, u32[]{:S(2)}, u32[]{:S(2)}) collective-permute-start(f32[256,128]{1,0:T(8,128)S(1)} %collective-permute-done.7.s3b), channel_id=1, source_target_pairs={{0,32},{1,97},{2,34},{3,99},{4,36},{5,101},{6,38},{7,103},{8,40},{... | collective-permute-start | bytes 393224 | tf_op jit(solution)/shard_map/ppermute | solution.py:153
  27.9 0.0 collective-permute-done.10.s3a
  27.9 0.0 collective-permute-done.9.s1b
  27.9 1.9 %far.1.before_ref = f32[96,2304]{1,0:T(8,128)S(1)} custom-call(f32[512,128]{1,0:T(8,128)S(1)} %collective-permute-done.whole_ref.s0, f32[256,128]{1,0:T(8,128)S(1)} %collective-permute-done.5.s1a, f32[256,128]{1,0:T(8,128)S(1)} %collective-permute-done.9.s1b, f32[256,128]{1,0:T(8,128)S(1)} %collective-permute-done.7.s3b, ...), custom_call_target="tpu_custom_call" | custom-call | flops 1358954496 | bytes 3000000 | tf_op jit(solution)/shard_map/far/pallas_call | solution.py:223
  29.8 1.8 %collective-permute-done.6.s2a = f32[256,128]{1,0:T(8,128)S(1)} collective-permute-done((f32[256,128]{1,0:T(8,128)S(1)}, f32[256,128]{1,0:T(8,128)S(1)}, u32[]{:S(2)}, u32[]{:S(2)}) %collective-permute-start.6) | collective-permute-done | bytes 131104 | tf_op jit(solution)/shard_map/ppermute | solution.py:153
  31.6 0.0 collective-permute-done.8.s2b
  31.7 0.6 %off.1 = f32[512,128]{1,0:T(8,128)S(1)} custom-call(f32[256,128]{1,0:T(8,128)S(1)} %collective-permute-done.6.s2a, f32[256,128]{1,0:T(8,128)S(1)} %collective-permute-done.8.s2b, bf16[288,384]{1,0:T(8,128)(2,1)S(1)} %get-tuple-element.15.taps_ref, f32[96,2304]{1,0:T(8,128)S(1)} %far.1.before_ref), custom_call_target="tpu_custom_call" | custom-call | flops 113246208 | bytes 3000000 | tf_op jit(solution)/shard_map/off/pallas_call | solution.py:234
  32.2 9.9 %collective-permute-start.11 = (f32[512,128]{1,0:T(8,128)S(1)}, f32[512,128]{1,0:T(8,128)S(1)}, u32[]{:S(2)}, u32[]{:S(2)}) collective-permute-start(f32[512,128]{1,0:T(8,128)S(1)} %off.1), channel_id=1, source_target_pairs={{1,2},{3,4},{5,6},{7,8},{9,10},{11,12},{13,14},{15,16},{17,18},{19... | collective-permute-start | bytes 786440 | tf_op jit(solution)/shard_map/ppermute | solution.py:252
  42.2 0.8 %rest.1 = (f32[512,128]{1,0:T(8,128)S(1)}, f32[512,128]{1,0:T(8,128)S(1)}) custom-call(f32[256,128]{1,0:T(8,128)S(1)} %collective-permute-done.6.s2a, f32[256,128]{1,0:T(8,128)S(1)} %collective-permute-done.8.s2b, bf16[288,384]{1,0:T(8,128)(2,1)S(1)} %get-tuple-element.15.taps_ref, f32[96,2304]{1,0:T(8,128)S(1)} %far.1.before_ref), custom_call_target="tpu_custom_call" | custom-call | flops 226492416 | bytes 3000000 | tf_op jit(solution)/shard_map/rest/pallas_call | solution.py:234
  42.9 0.1 collective-permute-start.12
  43.0 3.2 %collective-permute-done.11 = f32[512,128]{1,0:T(8,128)S(1)} collective-permute-done((f32[512,128]{1,0:T(8,128)S(1)}, f32[512,128]{1,0:T(8,128)S(1)}, u32[]{:S(2)}, u32[]{:S(2)}) %collective-permute-start.11) | collective-permute-done | bytes 262176 | tf_op jit(solution)/shard_map/ppermute | solution.py:252
  46.2 0.0 collective-permute-done.12
  46.2 0.8 %add_add_fusion = f32[512,128]{1,0:T(8,128)} fusion(f32[512,128]{1,0:T(8,128)S(1)} %collective-permute-done.12, f32[512,128]{1,0:T(8,128)S(1)} %get-tuple-element.17, f32[512,128]{1,0:T(8,128)S(1)} %collective-permute-done.11), kind=kLoop, calls=%fused_computation | loop fusion | flops 131072 | bytes 1048576 | tf_op jit(solution)/shard_map/add | solution.py:254
  (3 shorter events, 0.0 us)
Async XLA Ops:
  0.0 10.4 %collective-permute-start.1 = (f32[512,128]{1,0:T(8,128)}, f32[512,128]{1,0:T(8,128)S(1)}, u32[]{:S(2)}, u32[]{:S(2)}) collective-permute-start(f32[512,128]{1,0:T(8,128)} %bitcast.4), channel_id=1, source_target_pairs={{0,96},{1,33},{2,98},{3,35},{4,100},{5,37},{6,102},{7,39},{8,104},... | collective-permute-start | bytes 786440 | tf_op jit(solution)/shard_map/ppermute | solution.py:153
  2.0 8.5 %collective-permute-start.2 = (f32[512,128]{1,0:T(8,128)}, f32[512,128]{1,0:T(8,128)S(1)}, u32[]{:S(2)}, u32[]{:S(2)}) collective-permute-start(f32[512,128]{1,0:T(8,128)} %bitcast.5), channel_id=1, source_target_pairs={{0,32},{1,97},{2,34},{3,99},{4,36},{5,101},{6,38},{7,103},{8,40},{... | collective-permute-start | bytes 786440 | tf_op jit(solution)/shard_map/ppermute | solution.py:153
  3.3 16.7 %collective-permute-start = (f32[512,128]{1,0:T(8,128)}, f32[512,128]{1,0:T(8,128)S(1)}, u32[]{:S(2)}, u32[]{:S(2)}) collective-permute-start(f32[512,128]{1,0:T(8,128)} %bitcast.6), channel_id=1, source_target_pairs={{0,128},{32,160},{64,192},{96,224},{128,0},{160,32},{192,64},{224,... | collective-permute-start | bytes 786440 | tf_op jit(solution)/shard_map/ppermute | solution.py:194
  10.4 7.6 %collective-permute-start.3 = (f32[256,128]{1,0:T(8,128)S(1)}, f32[256,128]{1,0:T(8,128)S(1)}, u32[]{:S(2)}, u32[]{:S(2)}) collective-permute-start(f32[256,128]{1,0:T(8,128)S(1)} %half.2), channel_id=1, source_target_pairs={{0,96},{1,33},{2,98},{3,35},{4,100},{5,37},{6,102},{7,39},{8,104},... | collective-permute-start | bytes 393224 | tf_op jit(solution)/shard_map/ppermute | solution.py:153
  10.6 7.5 %collective-permute-start.4 = (f32[256,128]{1,0:T(8,128)S(1)}, f32[256,128]{1,0:T(8,128)S(1)}, u32[]{:S(2)}, u32[]{:S(2)}) collective-permute-start(f32[256,128]{1,0:T(8,128)S(1)} %half.3), channel_id=1, source_target_pairs={{0,32},{1,97},{2,34},{3,99},{4,36},{5,101},{6,38},{7,103},{8,40},{... | collective-permute-start | bytes 393224 | tf_op jit(solution)/shard_map/ppermute | solution.py:153
  13.3 1.2 %copy-start = (f32[3,3,3,32,256]{4,3,2,1,0:T(8,128)S(1)}, f32[3,3,3,32,256]{4,3,2,1,0:T(8,128)}, u32[]{:S(2)}) copy-start(f32[3,3,3,32,256]{4,3,2,1,0:T(8,128)} %kernel_ref.1) | copy-start | bytes 2654212
  14.5 3.6 %copy-start.1 = (f32[32,1,16,128]{3,2,1,0:T(8,128)S(1)}, f32[32,1,16,128]{3,2,1,0:T(8,128)}, u32[]{:S(2)}) copy-start(f32[32,1,16,128]{3,2,1,0:T(8,128)} %param.2) | copy-start | bytes 786436
  20.1 5.1 %collective-permute-start.5 = (f32[256,128]{1,0:T(8,128)S(1)}, f32[256,128]{1,0:T(8,128)S(1)}, u32[]{:S(2)}, u32[]{:S(2)}) collective-permute-start(f32[256,128]{1,0:T(8,128)S(1)} %get-tuple-element.13), channel_id=1, source_target_pairs={{0,96},{1,33},{2,98},{3,35},{4,100},{5,37},{6,102},{7,39},{8,104},... | collective-permute-start | bytes 393224 | tf_op jit(solution)/shard_map/ppermute | solution.py:153
  20.2 5.0 %collective-permute-start.7 = (f32[256,128]{1,0:T(8,128)S(1)}, f32[256,128]{1,0:T(8,128)S(1)}, u32[]{:S(2)}, u32[]{:S(2)}) collective-permute-start(f32[256,128]{1,0:T(8,128)S(1)} %get-tuple-element.14), channel_id=1, source_target_pairs={{0,32},{1,97},{2,34},{3,99},{4,36},{5,101},{6,38},{7,103},{8,40},{... | collective-permute-start | bytes 393224 | tf_op jit(solution)/shard_map/ppermute | solution.py:153
  22.8 5.0 %collective-permute-start.10 = (f32[256,128]{1,0:T(8,128)S(1)}, f32[256,128]{1,0:T(8,128)S(1)}, u32[]{:S(2)}, u32[]{:S(2)}) collective-permute-start(f32[256,128]{1,0:T(8,128)S(1)} %get-tuple-element.13), channel_id=1, source_target_pairs={{0,32},{1,97},{2,34},{3,99},{4,36},{5,101},{6,38},{7,103},{8,40},{... | collective-permute-start | bytes 393224 | tf_op jit(solution)/shard_map/ppermute | solution.py:153
  22.9 5.0 %collective-permute-start.9 = (f32[256,128]{1,0:T(8,128)S(1)}, f32[256,128]{1,0:T(8,128)S(1)}, u32[]{:S(2)}, u32[]{:S(2)}) collective-permute-start(f32[256,128]{1,0:T(8,128)S(1)} %get-tuple-element.14), channel_id=1, source_target_pairs={{0,96},{1,33},{2,98},{3,35},{4,100},{5,37},{6,102},{7,39},{8,104},... | collective-permute-start | bytes 393224 | tf_op jit(solution)/shard_map/ppermute | solution.py:153
  25.2 6.5 %collective-permute-start.6 = (f32[256,128]{1,0:T(8,128)S(1)}, f32[256,128]{1,0:T(8,128)S(1)}, u32[]{:S(2)}, u32[]{:S(2)}) collective-permute-start(f32[256,128]{1,0:T(8,128)S(1)} %collective-permute-done.5.s1a), channel_id=1, source_target_pairs={{0,96},{1,33},{2,98},{3,35},{4,100},{5,37},{6,102},{7,39},{8,104},... | collective-permute-start | bytes 393224 | tf_op jit(solution)/shard_map/ppermute | solution.py:153
  25.2 6.5 %collective-permute-start.8 = (f32[256,128]{1,0:T(8,128)S(1)}, f32[256,128]{1,0:T(8,128)S(1)}, u32[]{:S(2)}, u32[]{:S(2)}) collective-permute-start(f32[256,128]{1,0:T(8,128)S(1)} %collective-permute-done.7.s3b), channel_id=1, source_target_pairs={{0,32},{1,97},{2,34},{3,99},{4,36},{5,101},{6,38},{7,103},{8,40},{... | collective-permute-start | bytes 393224 | tf_op jit(solution)/shard_map/ppermute | solution.py:153
  32.2 14.0 %collective-permute-start.11 = (f32[512,128]{1,0:T(8,128)S(1)}, f32[512,128]{1,0:T(8,128)S(1)}, u32[]{:S(2)}, u32[]{:S(2)}) collective-permute-start(f32[512,128]{1,0:T(8,128)S(1)} %off.1), channel_id=1, source_target_pairs={{1,2},{3,4},{5,6},{7,8},{9,10},{11,12},{13,14},{15,16},{17,18},{19... | collective-permute-start | bytes 786440 | tf_op jit(solution)/shard_map/ppermute | solution.py:252
  42.9 3.3 %collective-permute-start.12 = (f32[512,128]{1,0:T(8,128)S(1)}, f32[512,128]{1,0:T(8,128)S(1)}, u32[]{:S(2)}, u32[]{:S(2)}) collective-permute-start(f32[512,128]{1,0:T(8,128)S(1)} %get-tuple-element.18), channel_id=1, source_target_pairs={{0,1},{2,3},{4,5},{6,7},{8,9},{10,11},{12,13},{14,15},{16,17},{18,... | collective-permute-start | bytes 786440 | tf_op jit(solution)/shard_map/ppermute | solution.py:253

commit v5 on v4

--- a/solution.py
+++ b/solution.py
@@ -27,6 +27,7 @@
     shard = half // X
     turn = lax.rem((X - x) * shard, half)
     slot = lax.broadcasted_iota(jnp.int32, (filters, half), 1) // shard
+    swapped = ((slot == 1) | (slot == 3)) & (core == 1)
     for out_ref, row in ((near_ref, z), (far_ref, 1 - z)):
         columns = pl.ds(pl.multiple_of(row * half, half), half)
         for a, plane in enumerate((2 - 2 * core, 2 * core, 1)):
@@ -36,7 +37,7 @@
                 for e in range(3):
                     values = pltpu.roll(kernel_ref[plane, b, e, :, columns], turn, 1)
                     mirrored = pltpu.roll(values, half // 2, 1)
-                    high, low = split(jnp.where(slot % 2 * core == 1, mirrored, values))
+                    high, low = split(jnp.where(swapped, mirrored, values))
                     out_ref[rows, pl.ds(e * half, half)] = high
                     out_ref[rows, pl.ds((3 + e) * half, half)] = high
                     out_ref[rows, pl.ds((6 + e) * half, half)] = low
@@ -101,9 +102,9 @@
     accumulate(((s0,), (s1,), (s2a, s2b), (s3,)), taps_ref, cells, total)
 
 
-def far_kernel(s0, s1a, s1b, s3b, s3a, taps_ref, near_ref, total, cells):
+def far_kernel(s0, s1, s3, taps_ref, near_ref, total, cells):
     total[...] = near_ref[...]
-    accumulate(((s0,), (s1a, s1b), (), (s3a, s3b)), taps_ref, cells, total)
+    accumulate(((s0,), (s1,), (), (s3,)), taps_ref, cells, total)
 
 
 def last_kernel(planes, s2a, s2b, taps_ref, before_ref, *rest):
@@ -138,11 +139,6 @@
             out_ref[pl.ds(h, filters, stride=height), :] = values
 
 
-def divide_kernel(whole_ref, order_ref, low_ref, high_ref):
-    low_ref[...] = whole_ref[: low_ref.shape[0]]
-    high_ref[...] = whole_ref[low_ref.shape[0] :]
-
-
 def exchange(block, way):
     planes = lax.axis_size("depth")
     pairs = []
@@ -166,23 +162,9 @@
     )(whole)
 
 
-def spread_own(whole):
+def spread(whole):
     s1, s3 = exchange(whole, 1), exchange(whole, -1)
     return s1, s3, exchange(half(s1, True), 1), exchange(half(s3, False), -1)
-
-
-def spread(whole, order):
-    part = jax.ShapeDtypeStruct((whole.shape[0] // 2, whole.shape[1]), F32)
-    low, high = pl.pallas_call(
-        divide_kernel,
-        out_shape=(part, part),
-        in_specs=[pl.BlockSpec(memory_space=pltpu.VMEM), pl.BlockSpec(memory_space=pl.ANY)],
-        compiler_params=LIMIT,
-        name="divide",
-    )(whole, order)
-    s1a, s3b = exchange(low, 1), exchange(high, -1)
-    s1b, s3a = exchange(high, 1), exchange(low, -1)
-    return s1a, s1b, s3b, s3a, exchange(s1a, 1), exchange(s3b, -1)
 
 
 def local(volume, kernel):
@@ -216,16 +198,16 @@
         out_shape=total,
         scratch_shapes=[packed],
         compiler_params=LIMIT,
-        cost_estimate=work(3, 1),
+        cost_estimate=work(3, 4),
         name="near",
-    )(own, *spread_own(own), near_taps)
-    *most, t2a, t2b = spread(other, before)
+    )(own, *spread(own), near_taps)
+    *most, t2a, t2b = spread(other)
     before = pl.pallas_call(
         far_kernel,
         out_shape=total,
         scratch_shapes=[packed],
         compiler_params=LIMIT,
-        cost_estimate=work(3, 1),
+        cost_estimate=work(3, 4),
         name="far",
     )(other, *most, far_taps, before)
 
@@ -248,7 +230,7 @@
     planes = lax.axis_size("depth")
     between = [(i, i + 1) for i in range(1, planes - 1, 2)]
     within = [(i, i + 1) for i in range(0, planes, 2)]
-    ends = [(0, 0), (planes - 1, planes - 1)]
+    ends = [(0, planes - 1), (planes - 1, 0)]
     off = lax.ppermute(off, "depth", between + [(j, i) for i, j in between] + ends)
     on = lax.ppermute(on, "depth", within + [(j, i) for i, j in within])
     return (mid + off + on).reshape(filters, 1, height, across)

time: 47.8 us -> 48.5 us (1.015)
  the two profiles are of different devices: /device:TPU:1 before, /device:TPU:32 now
where the time goes in v5:
time: 48.5 us; the launch traced here: 48.4 us
  starting transfers between devices  20.1 us (41%)
  waiting for transfers between devices  17.5 us (36%)
  Pallas kernels  8.83 us (18%)
  local copies, waits for them, and re-layouts  1.17 us (2%)
  other arithmetic  0.75 us (2%)
    ppermute x8, starting transfers between devices, exchange(): return lax.ppermute(block, ('chan', 'depth'), pairs)  11.9 us
    ppermute x8, waiting for transfers between devices, exchange(): return lax.ppermute(block, ('chan', 'depth'), pairs)  8.23 us
    ppermute x1, starting transfers between devices, local(): lax.ppermute(own, 'chan', [(i, (i + X) % (2 * X)) for i in range(2 * X)])  6.29 us
    ppermute x1, waiting for transfers between devices, local(): lax.ppermute(off, 'depth', between + [(j, i) for i, j in between] + ends)  5.37 us
    ppermute x1, waiting for transfers between devices, local(): lax.ppermute(own, 'chan', [(i, (i + X) % (2 * X)) for i in range(2 * X)])  3.86 us
    pallas_call x1, Pallas kernels, local(): pl.pallas_call(taps_kernel, out_shape=(weights, weights, last_weights), c...  3.55 us
    pallas_call x1, Pallas kernels, local(): pl.pallas_call(near_kernel, out_shape=total, scratch_shapes=[packed], com...  1.99 us
    pallas_call x1, Pallas kernels, local(): pl.pallas_call(far_kernel, out_shape=total, scratch_shapes=[packed], comp...  1.91 us
  transfers between devices with their start and end apart: 11, of which 6 were waited for; matrix products, arithmetic and copies ran while one was open for 0% of the time, Pallas kernels for 17%

profile of v5, /device:TPU:32, one launch (start us, length us, event | category | flops | bytes accessed | tf_op | source)
XLA Modules:
  0.0 48.4 jit_solution(11690597041194057762)
XLA Ops:
  0.0 2.8 %collective-permute-start.5 = (f32[512,128]{1,0:T(8,128)}, f32[512,128]{1,0:T(8,128)S(1)}, u32[]{:S(2)}, u32[]{:S(2)}) collective-permute-start(f32[512,128]{1,0:T(8,128)} %bitcast.4), channel_id=1, source_target_pairs={{0,96},{1,33},{2,98},{3,35},{4,100},{5,37},{6,102},{7,39},{8,104},... | collective-permute-start | bytes 786440 | tf_op jit(solution)/shard_map/ppermute | solution.py:149
  2.8 0.0 collective-permute-start.6
  2.8 6.3 %collective-permute-start = (f32[512,128]{1,0:T(8,128)}, f32[512,128]{1,0:T(8,128)S(1)}, u32[]{:S(2)}, u32[]{:S(2)}) collective-permute-start(f32[512,128]{1,0:T(8,128)} %bitcast.6), channel_id=1, source_target_pairs={{0,128},{32,160},{64,192},{96,224},{128,0},{160,32},{192,64},{224,... | collective-permute-start | bytes 786440 | tf_op jit(solution)/shard_map/ppermute | solution.py:176
  9.1 0.3 collective-permute-done.5.whole_ref.s1
  9.3 3.2 %collective-permute-start.7 = (f32[256,128]{1,0:T(8,128)S(1)}, f32[256,128]{1,0:T(8,128)S(1)}, u32[]{:S(2)}, u32[]{:S(2)}) collective-permute-start(f32[256,128]{1,0:T(8,128)S(1)} %half.6), channel_id=1, source_target_pairs={{0,96},{1,33},{2,98},{3,35},{4,100},{5,37},{6,102},{7,39},{8,104},... | collective-permute-start | bytes 393224 | tf_op jit(solution)/shard_map/ppermute | solution.py:149
  12.5 0.0 collective-permute-done.6.whole_ref.s3
  12.5 0.1 collective-permute-start.8
  12.6 0.0 copy-start
  12.6 1.2 %copy-done = f32[3,3,3,32,256]{4,3,2,1,0:T(8,128)S(1)} copy-done((f32[3,3,3,32,256]{4,3,2,1,0:T(8,128)S(1)}, f32[3,3,3,32,256]{4,3,2,1,0:T(8,128)}, u32[]{:S(2)}) %copy-start) | copy-done | bytes 884760
  13.8 0.0 copy-start.1
  13.8 3.6 %taps.1 = (bf16[288,1152]{1,0:T(8,128)(2,1)S(1)}, bf16[288,1152]{1,0:T(8,128)(2,1)S(1)}, bf16[288,384]{1,0:T(8,128)(2,1)S(1)}) custom-call(f32[3,3,3,32,256]{4,3,2,1,0:T(8,128)S(1)} %copy-done), custom_call_target="tpu_custom_call" | custom-call | bytes 4000000 | tf_op jit(solution)/shard_map/taps/pallas_call | solution.py:179
  17.4 3.9 %collective-permute-done.s0 = f32[512,128]{1,0:T(8,128)S(1)} collective-permute-done((f32[512,128]{1,0:T(8,128)}, f32[512,128]{1,0:T(8,128)S(1)}, u32[]{:S(2)}, u32[]{:S(2)}) %collective-permute-start) | collective-permute-done | bytes 262176 | tf_op jit(solution)/shard_map/ppermute | solution.py:176
  21.2 1.5 %collective-permute-start.1 = (f32[512,128]{1,0:T(8,128)S(1)}, f32[512,128]{1,0:T(8,128)S(1)}, u32[]{:S(2)}, u32[]{:S(2)}) collective-permute-start(f32[512,128]{1,0:T(8,128)S(1)} %collective-permute-done.s0), channel_id=1, source_target_pairs={{0,96},{1,33},{2,98},{3,35},{4,100},{5,37},{6,102},{7,39},{8,104},... | collective-permute-start | bytes 786440 | tf_op jit(solution)/shard_map/ppermute | solution.py:149
  22.7 0.5 %collective-permute-start.3 = (f32[512,128]{1,0:T(8,128)S(1)}, f32[512,128]{1,0:T(8,128)S(1)}, u32[]{:S(2)}, u32[]{:S(2)}) collective-permute-start(f32[512,128]{1,0:T(8,128)S(1)} %collective-permute-done.s0), channel_id=1, source_target_pairs={{0,32},{1,97},{2,34},{3,99},{4,36},{5,101},{6,38},{7,103},{8,40},{... | collective-permute-start | bytes 786440 | tf_op jit(solution)/shard_map/ppermute | solution.py:149
  23.2 0.0 collective-permute-done.7.s2a
  23.3 0.0 collective-permute-done.8.s2b
  23.3 0.0 copy-done.1
  23.3 2.0 %near.1.near_ref = f32[96,2304]{1,0:T(8,128)S(1)} custom-call(f32[512,128]{1,0:T(8,128)S(1)} %bitcast.7, f32[512,128]{1,0:T(8,128)S(1)} %collective-permute-done.5.whole_ref.s1, f32[512,128]{1,0:T(8,128)S(1)} %collective-permute-done.6.whole_ref.s3, f32[256,128]{1,0:T(8,128)S(1)} %collective-permute-done.7.s2a, f32[256,128]{1,0:T(8,128)S(1)} %collective-permute-done.8.s2b, ...), custom_call_target="tpu_custom_call" | custom-call | flops 5435817984 | bytes 3000000 | tf_op jit(solution)/shard_map/near/pallas_call | solution.py:196
  25.3 3.7 %collective-permute-done.1.whole_ref.s1 = f32[512,128]{1,0:T(8,128)S(1)} collective-permute-done((f32[512,128]{1,0:T(8,128)S(1)}, f32[512,128]{1,0:T(8,128)S(1)}, u32[]{:S(2)}, u32[]{:S(2)}) %collective-permute-start.1) | collective-permute-done | bytes 262176 | tf_op jit(solution)/shard_map/ppermute | solution.py:149
  29.0 3.8 %collective-permute-start.2 = (f32[256,128]{1,0:T(8,128)S(1)}, f32[256,128]{1,0:T(8,128)S(1)}, u32[]{:S(2)}, u32[]{:S(2)}) collective-permute-start(f32[256,128]{1,0:T(8,128)S(1)} %half.4), channel_id=1, source_target_pairs={{0,96},{1,33},{2,98},{3,35},{4,100},{5,37},{6,102},{7,39},{8,104},... | collective-permute-start | bytes 393224 | tf_op jit(solution)/shard_map/ppermute | solution.py:149
  32.7 0.0 collective-permute-done.3.whole_ref.s3
  32.8 0.1 collective-permute-start.4
  32.9 1.9 %far.1.before_ref = f32[96,2304]{1,0:T(8,128)S(1)} custom-call(f32[512,128]{1,0:T(8,128)S(1)} %collective-permute-done.s0, f32[512,128]{1,0:T(8,128)S(1)} %collective-permute-done.1.whole_ref.s1, f32[512,128]{1,0:T(8,128)S(1)} %collective-permute-done.3.whole_ref.s3, bf16[288,1152]{1,0:T(8,128)(2,1)S(1)} %get-tuple-element.11.taps_ref, ...), custom_call_target="tpu_custom_call" | custom-call | flops 5435817984 | bytes 3000000 | tf_op jit(solution)/shard_map/far/pallas_call | solution.py:205
  34.8 0.6 %collective-permute-done.2.s2a = f32[256,128]{1,0:T(8,128)S(1)} collective-permute-done((f32[256,128]{1,0:T(8,128)S(1)}, f32[256,128]{1,0:T(8,128)S(1)}, u32[]{:S(2)}, u32[]{:S(2)}) %collective-permute-start.2) | collective-permute-done | bytes 131104 | tf_op jit(solution)/shard_map/ppermute | solution.py:149
  35.4 3.6 %collective-permute-done.4.s2b = f32[256,128]{1,0:T(8,128)S(1)} collective-permute-done((f32[256,128]{1,0:T(8,128)S(1)}, f32[256,128]{1,0:T(8,128)S(1)}, u32[]{:S(2)}, u32[]{:S(2)}) %collective-permute-start.4) | collective-permute-done | bytes 131104 | tf_op jit(solution)/shard_map/ppermute | solution.py:149
  39.0 0.6 %off.1 = f32[512,128]{1,0:T(8,128)S(1)} custom-call(f32[256,128]{1,0:T(8,128)S(1)} %collective-permute-done.2.s2a, f32[256,128]{1,0:T(8,128)S(1)} %collective-permute-done.4.s2b, bf16[288,384]{1,0:T(8,128)(2,1)S(1)} %get-tuple-element.10.taps_ref, f32[96,2304]{1,0:T(8,128)S(1)} %far.1.before_ref), custom_call_target="tpu_custom_call" | custom-call | flops 113246208 | bytes 3000000 | tf_op jit(solution)/shard_map/off/pallas_call | solution.py:216
  39.6 0.1 collective-permute-start.9
  39.7 0.8 %rest.1 = (f32[512,128]{1,0:T(8,128)S(1)}, f32[512,128]{1,0:T(8,128)S(1)}) custom-call(f32[256,128]{1,0:T(8,128)S(1)} %collective-permute-done.2.s2a, f32[256,128]{1,0:T(8,128)S(1)} %collective-permute-done.4.s2b, bf16[288,384]{1,0:T(8,128)(2,1)S(1)} %get-tuple-element.10.taps_ref, f32[96,2304]{1,0:T(8,128)S(1)} %far.1.before_ref), custom_call_target="tpu_custom_call" | custom-call | flops 226492416 | bytes 3000000 | tf_op jit(solution)/shard_map/rest/pallas_call | solution.py:216
  40.5 1.8 %collective-permute-start.10 = (f32[512,128]{1,0:T(8,128)S(1)}, f32[512,128]{1,0:T(8,128)S(1)}, u32[]{:S(2)}, u32[]{:S(2)}) collective-permute-start(f32[512,128]{1,0:T(8,128)S(1)} %get-tuple-element.14), channel_id=1, source_target_pairs={{0,1},{2,3},{4,5},{6,7},{8,9},{10,11},{12,13},{14,15},{16,17},{18,... | collective-permute-start | bytes 786440 | tf_op jit(solution)/shard_map/ppermute | solution.py:235
  42.2 5.4 %collective-permute-done.9 = f32[512,128]{1,0:T(8,128)S(1)} collective-permute-done((f32[512,128]{1,0:T(8,128)S(1)}, f32[512,128]{1,0:T(8,128)S(1)}, u32[]{:S(2)}, u32[]{:S(2)}) %collective-permute-start.9) | collective-permute-done | bytes 262176 | tf_op jit(solution)/shard_map/ppermute | solution.py:234
  47.6 0.0 collective-permute-done.10
  47.6 0.8 %add_add_fusion = f32[512,128]{1,0:T(8,128)} fusion(f32[512,128]{1,0:T(8,128)S(1)} %collective-permute-done.10, f32[512,128]{1,0:T(8,128)S(1)} %get-tuple-element.13, f32[512,128]{1,0:T(8,128)S(1)} %collective-permute-done.9), kind=kLoop, calls=%fused_computation | loop fusion | flops 131072 | bytes 1048576 | tf_op jit(solution)/shard_map/add | solution.py:236
  (4 shorter events, 0.0 us)
Async XLA Ops:
  0.0 9.3 %collective-permute-start.5 = (f32[512,128]{1,0:T(8,128)}, f32[512,128]{1,0:T(8,128)S(1)}, u32[]{:S(2)}, u32[]{:S(2)}) collective-permute-start(f32[512,128]{1,0:T(8,128)} %bitcast.4), channel_id=1, source_target_pairs={{0,96},{1,33},{2,98},{3,35},{4,100},{5,37},{6,102},{7,39},{8,104},... | collective-permute-start | bytes 786440 | tf_op jit(solution)/shard_map/ppermute | solution.py:149
  2.8 9.8 %collective-permute-start.6 = (f32[512,128]{1,0:T(8,128)}, f32[512,128]{1,0:T(8,128)S(1)}, u32[]{:S(2)}, u32[]{:S(2)}) collective-permute-start(f32[512,128]{1,0:T(8,128)} %bitcast.5), channel_id=1, source_target_pairs={{0,32},{1,97},{2,34},{3,99},{4,36},{5,101},{6,38},{7,103},{8,40},{... | collective-permute-start | bytes 786440 | tf_op jit(solution)/shard_map/ppermute | solution.py:149
  2.8 18.5 %collective-permute-start = (f32[512,128]{1,0:T(8,128)}, f32[512,128]{1,0:T(8,128)S(1)}, u32[]{:S(2)}, u32[]{:S(2)}) collective-permute-start(f32[512,128]{1,0:T(8,128)} %bitcast.6), channel_id=1, source_target_pairs={{0,128},{32,160},{64,192},{96,224},{128,0},{160,32},{192,64},{224,... | collective-permute-start | bytes 786440 | tf_op jit(solution)/shard_map/ppermute | solution.py:176
  9.3 13.9 %collective-permute-start.7 = (f32[256,128]{1,0:T(8,128)S(1)}, f32[256,128]{1,0:T(8,128)S(1)}, u32[]{:S(2)}, u32[]{:S(2)}) collective-permute-start(f32[256,128]{1,0:T(8,128)S(1)} %half.6), channel_id=1, source_target_pairs={{0,96},{1,33},{2,98},{3,35},{4,100},{5,37},{6,102},{7,39},{8,104},... | collective-permute-start | bytes 393224 | tf_op jit(solution)/shard_map/ppermute | solution.py:149
  12.5 10.7 %collective-permute-start.8 = (f32[256,128]{1,0:T(8,128)S(1)}, f32[256,128]{1,0:T(8,128)S(1)}, u32[]{:S(2)}, u32[]{:S(2)}) collective-permute-start(f32[256,128]{1,0:T(8,128)S(1)} %half.7), channel_id=1, source_target_pairs={{0,32},{1,97},{2,34},{3,99},{4,36},{5,101},{6,38},{7,103},{8,40},{... | collective-permute-start | bytes 393224 | tf_op jit(solution)/shard_map/ppermute | solution.py:149
  12.6 1.2 %copy-start = (f32[3,3,3,32,256]{4,3,2,1,0:T(8,128)S(1)}, f32[3,3,3,32,256]{4,3,2,1,0:T(8,128)}, u32[]{:S(2)}) copy-start(f32[3,3,3,32,256]{4,3,2,1,0:T(8,128)} %kernel_ref.1) | copy-start | bytes 2654212
  13.8 9.5 %copy-start.1 = (f32[32,1,16,128]{3,2,1,0:T(8,128)S(1)}, f32[32,1,16,128]{3,2,1,0:T(8,128)}, u32[]{:S(2)}) copy-start(f32[32,1,16,128]{3,2,1,0:T(8,128)} %param.2) | copy-start | bytes 786436
  21.2 7.7 %collective-permute-start.1 = (f32[512,128]{1,0:T(8,128)S(1)}, f32[512,128]{1,0:T(8,128)S(1)}, u32[]{:S(2)}, u32[]{:S(2)}) collective-permute-start(f32[512,128]{1,0:T(8,128)S(1)} %collective-permute-done.s0), channel_id=1, source_target_pairs={{0,96},{1,33},{2,98},{3,35},{4,100},{5,37},{6,102},{7,39},{8,104},... | collective-permute-start | bytes 786440 | tf_op jit(solution)/shard_map/ppermute | solution.py:149
  22.7 10.0 %collective-permute-start.3 = (f32[512,128]{1,0:T(8,128)S(1)}, f32[512,128]{1,0:T(8,128)S(1)}, u32[]{:S(2)}, u32[]{:S(2)}) collective-permute-start(f32[512,128]{1,0:T(8,128)S(1)} %collective-permute-done.s0), channel_id=1, source_target_pairs={{0,32},{1,97},{2,34},{3,99},{4,36},{5,101},{6,38},{7,103},{8,40},{... | collective-permute-start | bytes 786440 | tf_op jit(solution)/shard_map/ppermute | solution.py:149
  29.0 6.4 %collective-permute-start.2 = (f32[256,128]{1,0:T(8,128)S(1)}, f32[256,128]{1,0:T(8,128)S(1)}, u32[]{:S(2)}, u32[]{:S(2)}) collective-permute-start(f32[256,128]{1,0:T(8,128)S(1)} %half.4), channel_id=1, source_target_pairs={{0,96},{1,33},{2,98},{3,35},{4,100},{5,37},{6,102},{7,39},{8,104},... | collective-permute-start | bytes 393224 | tf_op jit(solution)/shard_map/ppermute | solution.py:149
  32.8 6.3 %collective-permute-start.4 = (f32[256,128]{1,0:T(8,128)S(1)}, f32[256,128]{1,0:T(8,128)S(1)}, u32[]{:S(2)}, u32[]{:S(2)}) collective-permute-start(f32[256,128]{1,0:T(8,128)S(1)} %half.5), channel_id=1, source_target_pairs={{0,32},{1,97},{2,34},{3,99},{4,36},{5,101},{6,38},{7,103},{8,40},{... | collective-permute-start | bytes 393224 | tf_op jit(solution)/shard_map/ppermute | solution.py:149
  39.6 8.0 %collective-permute-start.9 = (f32[512,128]{1,0:T(8,128)S(1)}, f32[512,128]{1,0:T(8,128)S(1)}, u32[]{:S(2)}, u32[]{:S(2)}) collective-permute-start(f32[512,128]{1,0:T(8,128)S(1)} %off.1), channel_id=1, source_target_pairs={{1,2},{3,4},{5,6},{7,8},{9,10},{11,12},{13,14},{15,16},{17,18},{19... | collective-permute-start | bytes 786440 | tf_op jit(solution)/shard_map/ppermute | solution.py:234
  40.5 7.1 %collective-permute-start.10 = (f32[512,128]{1,0:T(8,128)S(1)}, f32[512,128]{1,0:T(8,128)S(1)}, u32[]{:S(2)}, u32[]{:S(2)}) collective-permute-start(f32[512,128]{1,0:T(8,128)S(1)} %get-tuple-element.14), channel_id=1, source_target_pairs={{0,1},{2,3},{4,5},{6,7},{8,9},{10,11},{12,13},{14,15},{16,17},{18,... | collective-permute-start | bytes 786440 | tf_op jit(solution)/shard_map/ppermute | solution.py:235

commit v6 on v3

--- a/solution.py
+++ b/solution.py
@@ -126,11 +126,14 @@
             preferred_element_type=F32,
         )
         scatter(products, total, filters, start, across)
+    depth = lax.axis_index("depth")
+    edge = (depth == 0) | (depth == lax.axis_size("depth") - 1)
     for a, out_ref in enumerate(out_refs):
         for h in range(height):
-            out_ref[pl.ds(h, filters, stride=height), :] = total[
-                pl.ds(a * filters, filters), pl.ds((h + 1) * across, across)
-            ]
+            values = total[pl.ds(a * filters, filters), pl.ds((h + 1) * across, across)]
+            if planes[a] == 0:
+                values = jnp.where(edge, 0.0, values)
+            out_ref[pl.ds(h, filters, stride=height), :] = values
 
 
 def from_x(block, step):
@@ -219,7 +222,8 @@
     planes = lax.axis_size("depth")
     between = [(i, i + 1) for i in range(1, planes - 1, 2)]
     within = [(i, i + 1) for i in range(0, planes, 2)]
-    off = lax.ppermute(off, "depth", between + [(j, i) for i, j in between])
+    ends = [(0, planes - 1), (planes - 1, 0)]
+    off = lax.ppermute(off, "depth", between + [(j, i) for i, j in between] + ends)
     on = lax.ppermute(on, "depth", within + [(j, i) for i, j in within])
     return (mid + off + on).reshape(filters, 1, height, across)
 

time: 45.7 us -> 45.7 us (level)
  the two profiles are of different devices: /device:TPU:1 before, /device:TPU:6 now
where the time goes in v6:
time: 45.7 us; the launch traced here: 45.6 us
  starting transfers between devices  21.5 us (47%)
  waiting for transfers between devices  15.9 us (35%)
  Pallas kernels  6.18 us (14%)
  local copies, waits for them, and re-layouts  1.17 us (3%)
  other arithmetic  0.75 us (2%)
    ppermute x9, starting transfers between devices, from_x(): return lax.ppermute(block, 'chan', pairs)  11.4 us
    ppermute x9, waiting for transfers between devices, from_x(): return lax.ppermute(block, 'chan', pairs)  8.24 us
    ppermute x1, starting transfers between devices, local(): lax.ppermute(own, 'chan', [(i, (i + X) % (2 * X)) for i in range(2 * X)])  7.19 us
    ppermute x1, waiting for transfers between devices, local(): lax.ppermute(off, 'depth', between + [(j, i) for i, j in between] + ends)  6.12 us
    ppermute x1, starting transfers between devices, local(): lax.ppermute(off, 'depth', between + [(j, i) for i, j in between] + ends)  2.81 us
    pallas_call x1, Pallas kernels, local(): pl.pallas_call(near_kernel, out_shape=total, scratch_shapes=[packed], com...  1.99 us
    pallas_call x1, Pallas kernels, local(): pl.pallas_call(far_kernel, out_shape=total, scratch_shapes=[packed], comp...  1.91 us
    ppermute x1, waiting for transfers between devices, local(): lax.ppermute(own, 'chan', [(i, (i + X) % (2 * X)) for i in range(2 * X)])  1.5 us
  transfers between devices with their start and end apart: 12, of which 5 were waited for; matrix products, arithmetic and copies ran while one was open for 0% of the time, Pallas kernels for 12%

profile of v6, /device:TPU:6, one launch (start us, length us, event | category | flops | bytes accessed | tf_op | source)
XLA Modules:
  0.0 45.6 jit_solution(4934021003682935163)
XLA Ops:
  0.0 7.2 %collective-permute-start = (f32[512,128]{1,0:T(8,128)}, f32[512,128]{1,0:T(8,128)S(1)}, u32[]{:S(2)}, u32[]{:S(2)}) collective-permute-start(f32[512,128]{1,0:T(8,128)} %bitcast.4), channel_id=1, source_target_pairs={{0,128},{32,160},{64,192},{96,224},{128,0},{160,32},{192,64},{224,... | collective-permute-start | bytes 786440 | tf_op jit(solution)/shard_map/ppermute | solution.py:156
  7.2 0.8 %collective-permute-start.7 = (f32[512,128]{1,0:T(8,128)}, f32[512,128]{1,0:T(8,128)S(1)}, u32[]{:S(2)}, u32[]{:S(2)}) collective-permute-start(f32[512,128]{1,0:T(8,128)} %bitcast.5), channel_id=1, source_target_pairs={{0,96},{32,0},{64,32},{96,64},{128,224},{160,128},{192,160},{224,1... | collective-permute-start | bytes 786440 | tf_op jit(solution)/shard_map/ppermute | solution.py:141
  8.0 1.1 %collective-permute-start.8 = (f32[512,128]{1,0:T(8,128)}, f32[512,128]{1,0:T(8,128)S(1)}, u32[]{:S(2)}, u32[]{:S(2)}) collective-permute-start(f32[512,128]{1,0:T(8,128)} %bitcast.6), channel_id=1, source_target_pairs={{0,64},{32,96},{64,0},{96,32},{128,192},{160,224},{192,128},{224,1... | collective-permute-start | bytes 786440 | tf_op jit(solution)/shard_map/ppermute | solution.py:141
  9.1 2.1 %collective-permute-start.9 = (f32[512,128]{1,0:T(8,128)}, f32[512,128]{1,0:T(8,128)S(1)}, u32[]{:S(2)}, u32[]{:S(2)}) collective-permute-start(f32[512,128]{1,0:T(8,128)} %bitcast.7), channel_id=1, source_target_pairs={{0,32},{32,64},{64,96},{96,0},{128,160},{160,192},{192,224},{224,1... | collective-permute-start | bytes 786440 | tf_op jit(solution)/shard_map/ppermute | solution.py:141
  11.2 0.0 copy-start
  11.2 1.2 %copy-done = f32[3,3,3,32,256]{4,3,2,1,0:T(8,128)S(1)} copy-done((f32[3,3,3,32,256]{4,3,2,1,0:T(8,128)S(1)}, f32[3,3,3,32,256]{4,3,2,1,0:T(8,128)}, u32[]{:S(2)}) %copy-start) | copy-done | bytes 884760
  12.4 0.9 %taps.1 = (bf16[288,1152]{1,0:T(8,128)(2,1)S(1)}, bf16[288,1152]{1,0:T(8,128)(2,1)S(1)}, bf16[288,384]{1,0:T(8,128)(2,1)S(1)}) custom-call(f32[3,3,3,32,256]{4,3,2,1,0:T(8,128)S(1)} %copy-done), custom_call_target="tpu_custom_call" | custom-call | bytes 4000000 | tf_op jit(solution)/shard_map/taps/pallas_call | solution.py:160
  13.3 0.0 copy-start.1
  13.3 1.5 %collective-permute-done.whole_ref.s0 = f32[512,128]{1,0:T(8,128)S(1)} collective-permute-done((f32[512,128]{1,0:T(8,128)}, f32[512,128]{1,0:T(8,128)S(1)}, u32[]{:S(2)}, u32[]{:S(2)}) %collective-permute-start) | collective-permute-done | bytes 262176 | tf_op jit(solution)/shard_map/ppermute | solution.py:156
  14.9 0.6 %collective-permute-start.1 = (f32[256,128]{1,0:T(8,128)S(1)}, f32[256,128]{1,0:T(8,128)S(1)}, u32[]{:S(2)}, u32[]{:S(2)}) collective-permute-start(f32[256,128]{1,0:T(8,128)S(1)} %get-tuple-element.13), channel_id=1, source_target_pairs={{0,32},{32,64},{64,96},{96,0},{128,160},{160,192},{192,224},{224,1... | collective-permute-start | bytes 393224 | tf_op jit(solution)/shard_map/ppermute | solution.py:141
  15.4 1.5 %collective-permute-start.3 = (f32[256,128]{1,0:T(8,128)S(1)}, f32[256,128]{1,0:T(8,128)S(1)}, u32[]{:S(2)}, u32[]{:S(2)}) collective-permute-start(f32[256,128]{1,0:T(8,128)S(1)} %get-tuple-element.14), channel_id=1, source_target_pairs={{0,96},{32,0},{64,32},{96,64},{128,224},{160,128},{192,160},{224,1... | collective-permute-start | bytes 393224 | tf_op jit(solution)/shard_map/ppermute | solution.py:141
  17.0 6.2 %collective-permute-done.7.s1 = f32[512,128]{1,0:T(8,128)S(1)} collective-permute-done((f32[512,128]{1,0:T(8,128)}, f32[512,128]{1,0:T(8,128)S(1)}, u32[]{:S(2)}, u32[]{:S(2)}) %collective-permute-start.7) | collective-permute-done | bytes 262176 | tf_op jit(solution)/shard_map/ppermute | solution.py:141
  23.1 0.0 collective-permute-start.5
  23.1 0.0 collective-permute-done.8.s2
  23.1 3.2 %collective-permute-start.6 = (f32[256,128]{1,0:T(8,128)S(1)}, f32[256,128]{1,0:T(8,128)S(1)}, u32[]{:S(2)}, u32[]{:S(2)}) collective-permute-start(f32[256,128]{1,0:T(8,128)S(1)} %get-tuple-element.14), channel_id=1, source_target_pairs={{0,32},{32,64},{64,96},{96,0},{128,160},{160,192},{192,224},{224,1... | collective-permute-start | bytes 393224 | tf_op jit(solution)/shard_map/ppermute | solution.py:141
  26.4 0.5 %collective-permute-done.1.s3a = f32[256,128]{1,0:T(8,128)S(1)} collective-permute-done((f32[256,128]{1,0:T(8,128)S(1)}, f32[256,128]{1,0:T(8,128)S(1)}, u32[]{:S(2)}, u32[]{:S(2)}) %collective-permute-start.1) | collective-permute-done | bytes 131104 | tf_op jit(solution)/shard_map/ppermute | solution.py:141
  26.8 1.3 %collective-permute-start.2 = (f32[256,128]{1,0:T(8,128)S(1)}, f32[256,128]{1,0:T(8,128)S(1)}, u32[]{:S(2)}, u32[]{:S(2)}) collective-permute-start(f32[256,128]{1,0:T(8,128)S(1)} %collective-permute-done.1.s3a), channel_id=1, source_target_pairs={{0,32},{32,64},{64,96},{96,0},{128,160},{160,192},{192,224},{224,1... | collective-permute-start | bytes 393224 | tf_op jit(solution)/shard_map/ppermute | solution.py:141
  28.1 0.0 collective-permute-done.3.s1b
  28.2 0.7 %collective-permute-start.4 = (f32[256,128]{1,0:T(8,128)S(1)}, f32[256,128]{1,0:T(8,128)S(1)}, u32[]{:S(2)}, u32[]{:S(2)}) collective-permute-start(f32[256,128]{1,0:T(8,128)S(1)} %collective-permute-done.3.s1b), channel_id=1, source_target_pairs={{0,96},{32,0},{64,32},{96,64},{128,224},{160,128},{192,160},{224,1... | collective-permute-start | bytes 393224 | tf_op jit(solution)/shard_map/ppermute | solution.py:141
  28.9 0.0 collective-permute-done.9.s3
  28.9 0.0 copy-done.1
  28.9 2.0 %near.1.near_ref = f32[96,2304]{1,0:T(8,128)S(1)} custom-call(f32[512,128]{1,0:T(8,128)S(1)} %bitcast.8, f32[512,128]{1,0:T(8,128)S(1)} %collective-permute-done.7.s1, f32[512,128]{1,0:T(8,128)S(1)} %collective-permute-done.8.s2, f32[512,128]{1,0:T(8,128)S(1)} %collective-permute-done.9.s3, bf16[288,1152]{1,0:T(8,128)(2,1)S(1)} %get-tuple-element.16.taps_ref), custom_call_target="tpu_custom_call" | custom-call | flops 1358954496 | bytes 3000000 | tf_op jit(solution)/shard_map/near/pallas_call | solution.py:189
  30.9 0.0 collective-permute-done.5.s1a
  30.9 0.0 collective-permute-done.6.s3b
  30.9 1.9 %far.1.before_ref = f32[96,2304]{1,0:T(8,128)S(1)} custom-call(f32[512,128]{1,0:T(8,128)S(1)} %collective-permute-done.whole_ref.s0, f32[256,128]{1,0:T(8,128)S(1)} %collective-permute-done.5.s1a, f32[256,128]{1,0:T(8,128)S(1)} %collective-permute-done.3.s1b, f32[256,128]{1,0:T(8,128)S(1)} %collective-permute-done.1.s3a, ...), custom_call_target="tpu_custom_call" | custom-call | flops 1358954496 | bytes 3000000 | tf_op jit(solution)/shard_map/far/pallas_call | solution.py:197
  32.8 0.0 collective-permute-done.2.s2a
  32.8 1.6 %collective-permute-done.4.s2b = f32[256,128]{1,0:T(8,128)S(1)} collective-permute-done((f32[256,128]{1,0:T(8,128)S(1)}, f32[256,128]{1,0:T(8,128)S(1)}, u32[]{:S(2)}, u32[]{:S(2)}) %collective-permute-start.4) | collective-permute-done | bytes 131104 | tf_op jit(solution)/shard_map/ppermute | solution.py:141
  34.4 0.6 %off.1 = f32[512,128]{1,0:T(8,128)S(1)} custom-call(f32[256,128]{1,0:T(8,128)S(1)} %collective-permute-done.2.s2a, f32[256,128]{1,0:T(8,128)S(1)} %collective-permute-done.4.s2b, bf16[288,384]{1,0:T(8,128)(2,1)S(1)} %get-tuple-element.12.order_ref.taps_ref, f32[96,2304]{1,0:T(8,128)S(1)} %far.1.before_ref), custom_call_target="tpu_custom_call" | custom-call | flops 113246208 | bytes 3000000 | tf_op jit(solution)/shard_map/off/pallas_call | solution.py:208
  35.0 2.8 %collective-permute-start.10 = (f32[512,128]{1,0:T(8,128)S(1)}, f32[512,128]{1,0:T(8,128)S(1)}, u32[]{:S(2)}, u32[]{:S(2)}) collective-permute-start(f32[512,128]{1,0:T(8,128)S(1)} %off.1), channel_id=1, source_target_pairs={{1,2},{3,4},{5,6},{7,8},{9,10},{11,12},{13,14},{15,16},{17,18},{19... | collective-permute-start | bytes 786440 | tf_op jit(solution)/shard_map/ppermute | solution.py:226
  37.8 0.7 %rest.1 = (f32[512,128]{1,0:T(8,128)S(1)}, f32[512,128]{1,0:T(8,128)S(1)}) custom-call(f32[256,128]{1,0:T(8,128)S(1)} %collective-permute-done.2.s2a, f32[256,128]{1,0:T(8,128)S(1)} %collective-permute-done.4.s2b, bf16[288,384]{1,0:T(8,128)(2,1)S(1)} %get-tuple-element.12.order_ref.taps_ref, f32[96,2304]{1,0:T(8,128)S(1)} %far.1.before_ref), custom_call_target="tpu_custom_call" | custom-call | flops 226492416 | bytes 3000000 | tf_op jit(solution)/shard_map/rest/pallas_call | solution.py:208
  38.6 0.1 collective-permute-start.11
  38.7 6.1 %collective-permute-done.10 = f32[512,128]{1,0:T(8,128)S(1)} collective-permute-done((f32[512,128]{1,0:T(8,128)S(1)}, f32[512,128]{1,0:T(8,128)S(1)}, u32[]{:S(2)}, u32[]{:S(2)}) %collective-permute-start.10) | collective-permute-done | bytes 262176 | tf_op jit(solution)/shard_map/ppermute | solution.py:226
  44.8 0.0 collective-permute-done.11
  44.8 0.8 %add_add_fusion = f32[512,128]{1,0:T(8,128)} fusion(f32[512,128]{1,0:T(8,128)S(1)} %collective-permute-done.11, f32[512,128]{1,0:T(8,128)S(1)} %get-tuple-element.17, f32[512,128]{1,0:T(8,128)S(1)} %collective-permute-done.10), kind=kLoop, calls=%fused_computation | loop fusion | flops 131072 | bytes 1048576 | tf_op jit(solution)/shard_map/add | solution.py:228
  (1 shorter events, 0.0 us)
Async XLA Ops:
  0.0 14.8 %collective-permute-start = (f32[512,128]{1,0:T(8,128)}, f32[512,128]{1,0:T(8,128)S(1)}, u32[]{:S(2)}, u32[]{:S(2)}) collective-permute-start(f32[512,128]{1,0:T(8,128)} %bitcast.4), channel_id=1, source_target_pairs={{0,128},{32,160},{64,192},{96,224},{128,0},{160,32},{192,64},{224,... | collective-permute-start | bytes 786440 | tf_op jit(solution)/shard_map/ppermute | solution.py:156
  7.2 15.9 %collective-permute-start.7 = (f32[512,128]{1,0:T(8,128)}, f32[512,128]{1,0:T(8,128)S(1)}, u32[]{:S(2)}, u32[]{:S(2)}) collective-permute-start(f32[512,128]{1,0:T(8,128)} %bitcast.5), channel_id=1, source_target_pairs={{0,96},{32,0},{64,32},{96,64},{128,224},{160,128},{192,160},{224,1... | collective-permute-start | bytes 786440 | tf_op jit(solution)/shard_map/ppermute | solution.py:141
  8.0 15.1 %collective-permute-start.8 = (f32[512,128]{1,0:T(8,128)}, f32[512,128]{1,0:T(8,128)S(1)}, u32[]{:S(2)}, u32[]{:S(2)}) collective-permute-start(f32[512,128]{1,0:T(8,128)} %bitcast.6), channel_id=1, source_target_pairs={{0,64},{32,96},{64,0},{96,32},{128,192},{160,224},{192,128},{224,1... | collective-permute-start | bytes 786440 | tf_op jit(solution)/shard_map/ppermute | solution.py:141
  9.1 19.7 %collective-permute-start.9 = (f32[512,128]{1,0:T(8,128)}, f32[512,128]{1,0:T(8,128)S(1)}, u32[]{:S(2)}, u32[]{:S(2)}) collective-permute-start(f32[512,128]{1,0:T(8,128)} %bitcast.7), channel_id=1, source_target_pairs={{0,32},{32,64},{64,96},{96,0},{128,160},{160,192},{192,224},{224,1... | collective-permute-start | bytes 786440 | tf_op jit(solution)/shard_map/ppermute | solution.py:141
  11.2 1.2 %copy-start = (f32[3,3,3,32,256]{4,3,2,1,0:T(8,128)S(1)}, f32[3,3,3,32,256]{4,3,2,1,0:T(8,128)}, u32[]{:S(2)}) copy-start(f32[3,3,3,32,256]{4,3,2,1,0:T(8,128)} %kernel_ref.1) | copy-start | bytes 2654212
  13.3 15.5 %copy-start.1 = (f32[32,1,16,128]{3,2,1,0:T(8,128)S(1)}, f32[32,1,16,128]{3,2,1,0:T(8,128)}, u32[]{:S(2)}) copy-start(f32[32,1,16,128]{3,2,1,0:T(8,128)} %param.2) | copy-start | bytes 786436
  14.9 12.0 %collective-permute-start.1 = (f32[256,128]{1,0:T(8,128)S(1)}, f32[256,128]{1,0:T(8,128)S(1)}, u32[]{:S(2)}, u32[]{:S(2)}) collective-permute-start(f32[256,128]{1,0:T(8,128)S(1)} %get-tuple-element.13), channel_id=1, source_target_pairs={{0,32},{32,64},{64,96},{96,0},{128,160},{160,192},{192,224},{224,1... | collective-permute-start | bytes 393224 | tf_op jit(solution)/shard_map/ppermute | solution.py:141
  15.4 12.7 %collective-permute-start.3 = (f32[256,128]{1,0:T(8,128)S(1)}, f32[256,128]{1,0:T(8,128)S(1)}, u32[]{:S(2)}, u32[]{:S(2)}) collective-permute-start(f32[256,128]{1,0:T(8,128)S(1)} %get-tuple-element.14), channel_id=1, source_target_pairs={{0,96},{32,0},{64,32},{96,64},{128,224},{160,128},{192,160},{224,1... | collective-permute-start | bytes 393224 | tf_op jit(solution)/shard_map/ppermute | solution.py:141
  23.1 7.7 %collective-permute-start.5 = (f32[256,128]{1,0:T(8,128)S(1)}, f32[256,128]{1,0:T(8,128)S(1)}, u32[]{:S(2)}, u32[]{:S(2)}) collective-permute-start(f32[256,128]{1,0:T(8,128)S(1)} %get-tuple-element.13), channel_id=1, source_target_pairs={{0,96},{32,0},{64,32},{96,64},{128,224},{160,128},{192,160},{224,1... | collective-permute-start | bytes 393224 | tf_op jit(solution)/shard_map/ppermute | solution.py:141
  23.1 7.7 %collective-permute-start.6 = (f32[256,128]{1,0:T(8,128)S(1)}, f32[256,128]{1,0:T(8,128)S(1)}, u32[]{:S(2)}, u32[]{:S(2)}) collective-permute-start(f32[256,128]{1,0:T(8,128)S(1)} %get-tuple-element.14), channel_id=1, source_target_pairs={{0,32},{32,64},{64,96},{96,0},{128,160},{160,192},{192,224},{224,1... | collective-permute-start | bytes 393224 | tf_op jit(solution)/shard_map/ppermute | solution.py:141
  26.8 6.0 %collective-permute-start.2 = (f32[256,128]{1,0:T(8,128)S(1)}, f32[256,128]{1,0:T(8,128)S(1)}, u32[]{:S(2)}, u32[]{:S(2)}) collective-permute-start(f32[256,128]{1,0:T(8,128)S(1)} %collective-permute-done.1.s3a), channel_id=1, source_target_pairs={{0,32},{32,64},{64,96},{96,0},{128,160},{160,192},{192,224},{224,1... | collective-permute-start | bytes 393224 | tf_op jit(solution)/shard_map/ppermute | solution.py:141
  28.2 6.3 %collective-permute-start.4 = (f32[256,128]{1,0:T(8,128)S(1)}, f32[256,128]{1,0:T(8,128)S(1)}, u32[]{:S(2)}, u32[]{:S(2)}) collective-permute-start(f32[256,128]{1,0:T(8,128)S(1)} %collective-permute-done.3.s1b), channel_id=1, source_target_pairs={{0,96},{32,0},{64,32},{96,64},{128,224},{160,128},{192,160},{224,1... | collective-permute-start | bytes 393224 | tf_op jit(solution)/shard_map/ppermute | solution.py:141
  35.0 9.8 %collective-permute-start.10 = (f32[512,128]{1,0:T(8,128)S(1)}, f32[512,128]{1,0:T(8,128)S(1)}, u32[]{:S(2)}, u32[]{:S(2)}) collective-permute-start(f32[512,128]{1,0:T(8,128)S(1)} %off.1), channel_id=1, source_target_pairs={{1,2},{3,4},{5,6},{7,8},{9,10},{11,12},{13,14},{15,16},{17,18},{19... | collective-permute-start | bytes 786440 | tf_op jit(solution)/shard_map/ppermute | solution.py:226
  38.6 6.2 %collective-permute-start.11 = (f32[512,128]{1,0:T(8,128)S(1)}, f32[512,128]{1,0:T(8,128)S(1)}, u32[]{:S(2)}, u32[]{:S(2)}) collective-permute-start(f32[512,128]{1,0:T(8,128)S(1)} %get-tuple-element.18), channel_id=1, source_target_pairs={{0,1},{2,3},{4,5},{6,7},{8,9},{10,11},{12,13},{14,15},{16,17},{18,... | collective-permute-start | bytes 786440 | tf_op jit(solution)/shard_map/ppermute | solution.py:227

commit v7 on v6

--- a/solution.py
+++ b/solution.py
@@ -222,8 +222,11 @@
     planes = lax.axis_size("depth")
     between = [(i, i + 1) for i in range(1, planes - 1, 2)]
     within = [(i, i + 1) for i in range(0, planes, 2)]
-    ends = [(0, planes - 1), (planes - 1, 0)]
-    off = lax.ppermute(off, "depth", between + [(j, i) for i, j in between] + ends)
+    pairs = []
+    for c in range(2 * X):
+        pairs += [(c * planes + i, c * planes + j) for k, l in between for i, j in ((k, l), (l, k))]
+        pairs += [(c * planes + d, (c ^ 1) * planes + d) for d in (0, planes - 1)]
+    off = lax.ppermute(off, ("chan", "depth"), pairs)
     on = lax.ppermute(on, "depth", within + [(j, i) for i, j in within])
     return (mid + off + on).reshape(filters, 1, height, across)
 

time: 45.7 us -> 43.9 us (0.961)
  the two profiles are of different devices: /device:TPU:6 before, /device:TPU:1 now
where the time goes in v7:
time: 43.9 us; the launch traced here: 43.4 us
  starting transfers between devices  25.6 us (58%)
  waiting for transfers between devices  9.56 us (22%)
  Pallas kernels  6.18 us (14%)
  local copies, waits for them, and re-layouts  1.17 us (3%)
  other arithmetic  0.75 us (2%)
    ppermute x9, starting transfers between devices, from_x(): return lax.ppermute(block, 'chan', pairs)  15.4 us
    ppermute x1, starting transfers between devices, local(): lax.ppermute(own, 'chan', [(i, (i + X) % (2 * X)) for i in range(2 * X)])  7.74 us
    ppermute x9, waiting for transfers between devices, from_x(): return lax.ppermute(block, 'chan', pairs)  6.07 us
    ppermute x1, waiting for transfers between devices, local(): off = lax.ppermute(off, ('chan', 'depth'), pairs)  3.49 us
    ppermute x1, starting transfers between devices, local(): off = lax.ppermute(off, ('chan', 'depth'), pairs)  2.38 us
    pallas_call x1, Pallas kernels, local(): pl.pallas_call(near_kernel, out_shape=total, scratch_shapes=[packed], com...  1.99 us
    pallas_call x1, Pallas kernels, local(): pl.pallas_call(far_kernel, out_shape=total, scratch_shapes=[packed], comp...  1.91 us
    pallas_call x2, Pallas kernels, last(): pl.pallas_call(functools.partial(last_kernel, taps), out_shape=[part] * l...  1.34 us
  transfers between devices with their start and end apart: 12, of which 3 were waited for; matrix products, arithmetic and copies ran while one was open for 0% of the time, Pallas kernels for 13%

profile of v7, /device:TPU:1, one launch (start us, length us, event | category | flops | bytes accessed | tf_op | source)
XLA Modules:
  0.0 43.4 jit_solution(8816786981387685922)
XLA Ops:
  0.0 7.7 %collective-permute-start = (f32[512,128]{1,0:T(8,128)}, f32[512,128]{1,0:T(8,128)S(1)}, u32[]{:S(2)}, u32[]{:S(2)}) collective-permute-start(f32[512,128]{1,0:T(8,128)} %bitcast.4), channel_id=1, source_target_pairs={{0,128},{32,160},{64,192},{96,224},{128,0},{160,32},{192,64},{224,... | collective-permute-start | bytes 786440 | tf_op jit(solution)/shard_map/ppermute | solution.py:156
  7.7 2.5 %collective-permute-start.7 = (f32[512,128]{1,0:T(8,128)}, f32[512,128]{1,0:T(8,128)S(1)}, u32[]{:S(2)}, u32[]{:S(2)}) collective-permute-start(f32[512,128]{1,0:T(8,128)} %bitcast.5), channel_id=1, source_target_pairs={{0,96},{32,0},{64,32},{96,64},{128,224},{160,128},{192,160},{224,1... | collective-permute-start | bytes 786440 | tf_op jit(solution)/shard_map/ppermute | solution.py:141
  10.2 0.5 %collective-permute-start.8 = (f32[512,128]{1,0:T(8,128)}, f32[512,128]{1,0:T(8,128)S(1)}, u32[]{:S(2)}, u32[]{:S(2)}) collective-permute-start(f32[512,128]{1,0:T(8,128)} %bitcast.6), channel_id=1, source_target_pairs={{0,64},{32,96},{64,0},{96,32},{128,192},{160,224},{192,128},{224,1... | collective-permute-start | bytes 786440 | tf_op jit(solution)/shard_map/ppermute | solution.py:141
  10.7 0.6 %collective-permute-start.9 = (f32[512,128]{1,0:T(8,128)}, f32[512,128]{1,0:T(8,128)S(1)}, u32[]{:S(2)}, u32[]{:S(2)}) collective-permute-start(f32[512,128]{1,0:T(8,128)} %bitcast.7), channel_id=1, source_target_pairs={{0,32},{32,64},{64,96},{96,0},{128,160},{160,192},{192,224},{224,1... | collective-permute-start | bytes 786440 | tf_op jit(solution)/shard_map/ppermute | solution.py:141
  11.3 0.0 copy-start
  11.3 1.2 %copy-done = f32[3,3,3,32,256]{4,3,2,1,0:T(8,128)S(1)} copy-done((f32[3,3,3,32,256]{4,3,2,1,0:T(8,128)S(1)}, f32[3,3,3,32,256]{4,3,2,1,0:T(8,128)}, u32[]{:S(2)}) %copy-start) | copy-done | bytes 884760
  12.5 0.9 %taps.1 = (bf16[288,1152]{1,0:T(8,128)(2,1)S(1)}, bf16[288,1152]{1,0:T(8,128)(2,1)S(1)}, bf16[288,384]{1,0:T(8,128)(2,1)S(1)}) custom-call(f32[3,3,3,32,256]{4,3,2,1,0:T(8,128)S(1)} %copy-done), custom_call_target="tpu_custom_call" | custom-call | bytes 4000000 | tf_op jit(solution)/shard_map/taps/pallas_call | solution.py:160
  13.4 0.0 copy-start.1
  13.5 0.0 collective-permute-done.whole_ref.s0
  13.5 2.8 %collective-permute-start.1 = (f32[256,128]{1,0:T(8,128)S(1)}, f32[256,128]{1,0:T(8,128)S(1)}, u32[]{:S(2)}, u32[]{:S(2)}) collective-permute-start(f32[256,128]{1,0:T(8,128)S(1)} %get-tuple-element.13), channel_id=1, source_target_pairs={{0,32},{32,64},{64,96},{96,0},{128,160},{160,192},{192,224},{224,1... | collective-permute-start | bytes 393224 | tf_op jit(solution)/shard_map/ppermute | solution.py:141
  16.3 1.4 %collective-permute-start.3 = (f32[256,128]{1,0:T(8,128)S(1)}, f32[256,128]{1,0:T(8,128)S(1)}, u32[]{:S(2)}, u32[]{:S(2)}) collective-permute-start(f32[256,128]{1,0:T(8,128)S(1)} %get-tuple-element.14), channel_id=1, source_target_pairs={{0,96},{32,0},{64,32},{96,64},{128,224},{160,128},{192,160},{224,1... | collective-permute-start | bytes 393224 | tf_op jit(solution)/shard_map/ppermute | solution.py:141
  17.6 0.0 collective-permute-done.7.s1
  17.6 2.1 %collective-permute-start.5 = (f32[256,128]{1,0:T(8,128)S(1)}, f32[256,128]{1,0:T(8,128)S(1)}, u32[]{:S(2)}, u32[]{:S(2)}) collective-permute-start(f32[256,128]{1,0:T(8,128)S(1)} %get-tuple-element.13), channel_id=1, source_target_pairs={{0,96},{32,0},{64,32},{96,64},{128,224},{160,128},{192,160},{224,1... | collective-permute-start | bytes 393224 | tf_op jit(solution)/shard_map/ppermute | solution.py:141
  19.8 0.0 collective-permute-done.8.s2
  19.8 2.8 %collective-permute-start.6 = (f32[256,128]{1,0:T(8,128)S(1)}, f32[256,128]{1,0:T(8,128)S(1)}, u32[]{:S(2)}, u32[]{:S(2)}) collective-permute-start(f32[256,128]{1,0:T(8,128)S(1)} %get-tuple-element.14), channel_id=1, source_target_pairs={{0,32},{32,64},{64,96},{96,0},{128,160},{160,192},{192,224},{224,1... | collective-permute-start | bytes 393224 | tf_op jit(solution)/shard_map/ppermute | solution.py:141
  22.6 6.0 %collective-permute-done.1.s3a = f32[256,128]{1,0:T(8,128)S(1)} collective-permute-done((f32[256,128]{1,0:T(8,128)S(1)}, f32[256,128]{1,0:T(8,128)S(1)}, u32[]{:S(2)}, u32[]{:S(2)}) %collective-permute-start.1) | collective-permute-done | bytes 131104 | tf_op jit(solution)/shard_map/ppermute | solution.py:141
  28.6 0.0 collective-permute-start.2
  28.6 0.0 collective-permute-done.3.s1b
  28.6 2.7 %collective-permute-start.4 = (f32[256,128]{1,0:T(8,128)S(1)}, f32[256,128]{1,0:T(8,128)S(1)}, u32[]{:S(2)}, u32[]{:S(2)}) collective-permute-start(f32[256,128]{1,0:T(8,128)S(1)} %collective-permute-done.3.s1b), channel_id=1, source_target_pairs={{0,96},{32,0},{64,32},{96,64},{128,224},{160,128},{192,160},{224,1... | collective-permute-start | bytes 393224 | tf_op jit(solution)/shard_map/ppermute | solution.py:141
  31.3 0.0 collective-permute-done.9.s3
  31.3 0.0 copy-done.1
  31.3 2.0 %near.1.near_ref = f32[96,2304]{1,0:T(8,128)S(1)} custom-call(f32[512,128]{1,0:T(8,128)S(1)} %bitcast.8, f32[512,128]{1,0:T(8,128)S(1)} %collective-permute-done.7.s1, f32[512,128]{1,0:T(8,128)S(1)} %collective-permute-done.8.s2, f32[512,128]{1,0:T(8,128)S(1)} %collective-permute-done.9.s3, bf16[288,1152]{1,0:T(8,128)(2,1)S(1)} %get-tuple-element.16.taps_ref), custom_call_target="tpu_custom_call" | custom-call | flops 1358954496 | bytes 3000000 | tf_op jit(solution)/shard_map/near/pallas_call | solution.py:189
  33.3 0.0 collective-permute-done.5.s1a
  33.3 0.0 collective-permute-done.6.s3b
  33.3 1.9 %far.1.before_ref = f32[96,2304]{1,0:T(8,128)S(1)} custom-call(f32[512,128]{1,0:T(8,128)S(1)} %collective-permute-done.whole_ref.s0, f32[256,128]{1,0:T(8,128)S(1)} %collective-permute-done.5.s1a, f32[256,128]{1,0:T(8,128)S(1)} %collective-permute-done.3.s1b, f32[256,128]{1,0:T(8,128)S(1)} %collective-permute-done.1.s3a, ...), custom_call_target="tpu_custom_call" | custom-call | flops 1358954496 | bytes 3000000 | tf_op jit(solution)/shard_map/far/pallas_call | solution.py:197
  35.2 0.1 collective-permute-done.2.s2a
  35.3 0.0 collective-permute-done.4.s2b
  35.3 0.6 %off.1 = f32[512,128]{1,0:T(8,128)S(1)} custom-call(f32[256,128]{1,0:T(8,128)S(1)} %collective-permute-done.2.s2a, f32[256,128]{1,0:T(8,128)S(1)} %collective-permute-done.4.s2b, bf16[288,384]{1,0:T(8,128)(2,1)S(1)} %get-tuple-element.12.order_ref.taps_ref, f32[96,2304]{1,0:T(8,128)S(1)} %far.1.before_ref), custom_call_target="tpu_custom_call" | custom-call | flops 113246208 | bytes 3000000 | tf_op jit(solution)/shard_map/off/pallas_call | solution.py:208
  35.9 2.4 %collective-permute-start.10 = (f32[512,128]{1,0:T(8,128)S(1)}, f32[512,128]{1,0:T(8,128)S(1)}, u32[]{:S(2)}, u32[]{:S(2)}) collective-permute-start(f32[512,128]{1,0:T(8,128)S(1)} %off.1), channel_id=1, source_target_pairs={{1,2},{2,1},{3,4},{4,3},{5,6},{6,5},{7,8},{8,7},{9,10},{10,9},{11,... | collective-permute-start | bytes 786440 | tf_op jit(solution)/shard_map/ppermute | solution.py:229
  38.3 0.7 %rest.1 = (f32[512,128]{1,0:T(8,128)S(1)}, f32[512,128]{1,0:T(8,128)S(1)}) custom-call(f32[256,128]{1,0:T(8,128)S(1)} %collective-permute-done.2.s2a, f32[256,128]{1,0:T(8,128)S(1)} %collective-permute-done.4.s2b, bf16[288,384]{1,0:T(8,128)(2,1)S(1)} %get-tuple-element.12.order_ref.taps_ref, f32[96,2304]{1,0:T(8,128)S(1)} %far.1.before_ref), custom_call_target="tpu_custom_call" | custom-call | flops 226492416 | bytes 3000000 | tf_op jit(solution)/shard_map/rest/pallas_call | solution.py:208
  39.0 0.1 collective-permute-start.11
  39.1 3.5 %collective-permute-done.10 = f32[512,128]{1,0:T(8,128)S(1)} collective-permute-done((f32[512,128]{1,0:T(8,128)S(1)}, f32[512,128]{1,0:T(8,128)S(1)}, u32[]{:S(2)}, u32[]{:S(2)}) %collective-permute-start.10) | collective-permute-done | bytes 262176 | tf_op jit(solution)/shard_map/ppermute | solution.py:229
  42.6 0.0 collective-permute-done.11
  42.6 0.8 %add_add_fusion = f32[512,128]{1,0:T(8,128)} fusion(f32[512,128]{1,0:T(8,128)S(1)} %collective-permute-done.11, f32[512,128]{1,0:T(8,128)S(1)} %get-tuple-element.17, f32[512,128]{1,0:T(8,128)S(1)} %collective-permute-done.10), kind=kLoop, calls=%fused_computation | loop fusion | flops 131072 | bytes 1048576 | tf_op jit(solution)/shard_map/add | solution.py:231
  (1 shorter events, 0.0 us)
Async XLA Ops:
  0.0 13.5 %collective-permute-start = (f32[512,128]{1,0:T(8,128)}, f32[512,128]{1,0:T(8,128)S(1)}, u32[]{:S(2)}, u32[]{:S(2)}) collective-permute-start(f32[512,128]{1,0:T(8,128)} %bitcast.4), channel_id=1, source_target_pairs={{0,128},{32,160},{64,192},{96,224},{128,0},{160,32},{192,64},{224,... | collective-permute-start | bytes 786440 | tf_op jit(solution)/shard_map/ppermute | solution.py:156
  7.7 9.9 %collective-permute-start.7 = (f32[512,128]{1,0:T(8,128)}, f32[512,128]{1,0:T(8,128)S(1)}, u32[]{:S(2)}, u32[]{:S(2)}) collective-permute-start(f32[512,128]{1,0:T(8,128)} %bitcast.5), channel_id=1, source_target_pairs={{0,96},{32,0},{64,32},{96,64},{128,224},{160,128},{192,160},{224,1... | collective-permute-start | bytes 786440 | tf_op jit(solution)/shard_map/ppermute | solution.py:141
  10.2 9.6 %collective-permute-start.8 = (f32[512,128]{1,0:T(8,128)}, f32[512,128]{1,0:T(8,128)S(1)}, u32[]{:S(2)}, u32[]{:S(2)}) collective-permute-start(f32[512,128]{1,0:T(8,128)} %bitcast.6), channel_id=1, source_target_pairs={{0,64},{32,96},{64,0},{96,32},{128,192},{160,224},{192,128},{224,1... | collective-permute-start | bytes 786440 | tf_op jit(solution)/shard_map/ppermute | solution.py:141
  10.7 20.5 %collective-permute-start.9 = (f32[512,128]{1,0:T(8,128)}, f32[512,128]{1,0:T(8,128)S(1)}, u32[]{:S(2)}, u32[]{:S(2)}) collective-permute-start(f32[512,128]{1,0:T(8,128)} %bitcast.7), channel_id=1, source_target_pairs={{0,32},{32,64},{64,96},{96,0},{128,160},{160,192},{192,224},{224,1... | collective-permute-start | bytes 786440 | tf_op jit(solution)/shard_map/ppermute | solution.py:141
  11.3 1.2 %copy-start = (f32[3,3,3,32,256]{4,3,2,1,0:T(8,128)S(1)}, f32[3,3,3,32,256]{4,3,2,1,0:T(8,128)}, u32[]{:S(2)}) copy-start(f32[3,3,3,32,256]{4,3,2,1,0:T(8,128)} %kernel_ref.1) | copy-start | bytes 2654212
  13.4 17.8 %copy-start.1 = (f32[32,1,16,128]{3,2,1,0:T(8,128)S(1)}, f32[32,1,16,128]{3,2,1,0:T(8,128)}, u32[]{:S(2)}) copy-start(f32[32,1,16,128]{3,2,1,0:T(8,128)} %param.2) | copy-start | bytes 786436
  13.5 15.1 %collective-permute-start.1 = (f32[256,128]{1,0:T(8,128)S(1)}, f32[256,128]{1,0:T(8,128)S(1)}, u32[]{:S(2)}, u32[]{:S(2)}) collective-permute-start(f32[256,128]{1,0:T(8,128)S(1)} %get-tuple-element.13), channel_id=1, source_target_pairs={{0,32},{32,64},{64,96},{96,0},{128,160},{160,192},{192,224},{224,1... | collective-permute-start | bytes 393224 | tf_op jit(solution)/shard_map/ppermute | solution.py:141
  16.3 12.3 %collective-permute-start.3 = (f32[256,128]{1,0:T(8,128)S(1)}, f32[256,128]{1,0:T(8,128)S(1)}, u32[]{:S(2)}, u32[]{:S(2)}) collective-permute-start(f32[256,128]{1,0:T(8,128)S(1)} %get-tuple-element.14), channel_id=1, source_target_pairs={{0,96},{32,0},{64,32},{96,64},{128,224},{160,128},{192,160},{224,1... | collective-permute-start | bytes 393224 | tf_op jit(solution)/shard_map/ppermute | solution.py:141
  17.6 15.6 %collective-permute-start.5 = (f32[256,128]{1,0:T(8,128)S(1)}, f32[256,128]{1,0:T(8,128)S(1)}, u32[]{:S(2)}, u32[]{:S(2)}) collective-permute-start(f32[256,128]{1,0:T(8,128)S(1)} %get-tuple-element.13), channel_id=1, source_target_pairs={{0,96},{32,0},{64,32},{96,64},{128,224},{160,128},{192,160},{224,1... | collective-permute-start | bytes 393224 | tf_op jit(solution)/shard_map/ppermute | solution.py:141
  19.8 13.5 %collective-permute-start.6 = (f32[256,128]{1,0:T(8,128)S(1)}, f32[256,128]{1,0:T(8,128)S(1)}, u32[]{:S(2)}, u32[]{:S(2)}) collective-permute-start(f32[256,128]{1,0:T(8,128)S(1)} %get-tuple-element.14), channel_id=1, source_target_pairs={{0,32},{32,64},{64,96},{96,0},{128,160},{160,192},{192,224},{224,1... | collective-permute-start | bytes 393224 | tf_op jit(solution)/shard_map/ppermute | solution.py:141
  28.6 6.7 %collective-permute-start.2 = (f32[256,128]{1,0:T(8,128)S(1)}, f32[256,128]{1,0:T(8,128)S(1)}, u32[]{:S(2)}, u32[]{:S(2)}) collective-permute-start(f32[256,128]{1,0:T(8,128)S(1)} %collective-permute-done.1.s3a), channel_id=1, source_target_pairs={{0,32},{32,64},{64,96},{96,0},{128,160},{160,192},{192,224},{224,1... | collective-permute-start | bytes 393224 | tf_op jit(solution)/shard_map/ppermute | solution.py:141
  28.6 6.7 %collective-permute-start.4 = (f32[256,128]{1,0:T(8,128)S(1)}, f32[256,128]{1,0:T(8,128)S(1)}, u32[]{:S(2)}, u32[]{:S(2)}) collective-permute-start(f32[256,128]{1,0:T(8,128)S(1)} %collective-permute-done.3.s1b), channel_id=1, source_target_pairs={{0,96},{32,0},{64,32},{96,64},{128,224},{160,128},{192,160},{224,1... | collective-permute-start | bytes 393224 | tf_op jit(solution)/shard_map/ppermute | solution.py:141
  35.9 6.7 %collective-permute-start.10 = (f32[512,128]{1,0:T(8,128)S(1)}, f32[512,128]{1,0:T(8,128)S(1)}, u32[]{:S(2)}, u32[]{:S(2)}) collective-permute-start(f32[512,128]{1,0:T(8,128)S(1)} %off.1), channel_id=1, source_target_pairs={{1,2},{2,1},{3,4},{4,3},{5,6},{6,5},{7,8},{8,7},{9,10},{10,9},{11,... | collective-permute-start | bytes 786440 | tf_op jit(solution)/shard_map/ppermute | solution.py:229
  39.0 3.6 %collective-permute-start.11 = (f32[512,128]{1,0:T(8,128)S(1)}, f32[512,128]{1,0:T(8,128)S(1)}, u32[]{:S(2)}, u32[]{:S(2)}) collective-permute-start(f32[512,128]{1,0:T(8,128)S(1)} %get-tuple-element.18), channel_id=1, source_target_pairs={{0,1},{2,3},{4,5},{6,7},{8,9},{10,11},{12,13},{14,15},{16,17},{18,... | collective-permute-start | bytes 786440 | tf_op jit(solution)/shard_map/ppermute | solution.py:230

commit v8 on v7

--- a/solution.py
+++ b/solution.py
@@ -9,6 +9,7 @@
 
 X = 4
 ROWS = 2
+LIMIT = pltpu.CompilerParams(vmem_limit_bytes=24 * 1024 * 1024)
 F32, BF16 = jnp.float32, jnp.bfloat16
 
 
@@ -25,7 +26,7 @@
     half = kernel_ref.shape[4] // 2
     shard = half // X
     turn = lax.rem((X - x) * shard, half)
-    slot = lax.broadcasted_iota(jnp.int32, (filters, half), 1) // shard
+    unit = lax.broadcasted_iota(jnp.int32, (filters, half), 1) // (shard // 2)
     for out_ref, row in ((near_ref, z), (far_ref, 1 - z)):
         columns = pl.ds(pl.multiple_of(row * half, half), half)
         for a, plane in enumerate((2 - 2 * core, 2 * core, 1)):
@@ -44,8 +45,10 @@
                     for tile in range(last_ref.shape[1] // half):
                         result = jnp.zeros((filters, half), F32)
                         for k, values in enumerate(blocks[tile * X : tile * X + X]):
-                            placed = pltpu.roll(values, (k + X - 2) % X * shard, 1)
-                            result = jnp.where(slot == k, placed, result)
+                            low = pltpu.roll(values, (k + X - 1) % X * shard, 1)
+                            high = pltpu.roll(values, (k + X - 3) % X * shard, 1)
+                            result = jnp.where(unit == 2 * k, low, result)
+                            result = jnp.where(unit == 2 * k + 1, high, result)
                         last_ref[rows, pl.ds(tile * half, half)] = result.astype(BF16)
 
 
@@ -61,22 +64,18 @@
             cells[pl.ds(row, channels), pl.ds(h * across, across)] = part
 
 
-def accumulate(shards, taps_ref, cells, total):
+def accumulate(shards, unused, taps_ref, cells, total):
     across = shards[0][0].shape[1]
     height = cells.shape[1] // across
     half = cells.shape[0] // 6
-    channels = half // X
-    for k, refs in enumerate(shards):
-        if not refs:
-            for e in range(6):
-                rows = pl.ds(e * half + k * channels, channels)
-                cells[rows, :] = jnp.zeros((channels, cells.shape[1]), BF16)
+    for place, channels in unused:
+        for e in range(6):
+            cells[pl.ds(e * half + place, channels), :] = jnp.zeros((channels, cells.shape[1]), BF16)
     for start in range(0, height, ROWS):
         for h in range(start, start + ROWS):
-            for k, refs in enumerate(shards):
-                for j, ref in enumerate(refs):
-                    row = k * channels + j * channels // len(refs)
-                    pack(ref, cells, h, height, [(e * half + row, (3 + e) * half + row) for e in range(3)])
+            for ref, place in shards:
+                rows = [(e * half + place, (3 + e) * half + place) for e in range(3)]
+                pack(ref, cells, h, height, rows)
         wide = pl.ds(start * across, ROWS * across)
         products = jnp.dot(
             taps_ref[:, : 6 * half], cells[:, wide], preferred_element_type=F32
@@ -95,20 +94,29 @@
 
 
 def near_kernel(s0, s1, s2, s3, taps_ref, total, cells):
+    n = taps_ref.shape[1] // 9 // X
     total[...] = jnp.zeros_like(total)
-    accumulate(((s0,), (s1,), (s2,), (s3,)), taps_ref, cells, total)
-
-
-def far_kernel(s0, s1a, s1b, s3a, s3b, taps_ref, near_ref, total, cells):
+    accumulate(((s0, 0), (s1, n), (s2, 2 * n), (s3, 3 * n)), (), taps_ref, cells, total)
+
+
+def far_kernel(s0, s1b, s2a, s2b, s3a, taps_ref, near_ref, total, cells):
+    n = taps_ref.shape[1] // 9 // X
+    m = n // 2
     total[...] = near_ref[...]
-    accumulate(((s0,), (s1a, s1b), (), (s3a, s3b)), taps_ref, cells, total)
-
-
-def last_kernel(planes, s2a, s2b, taps_ref, before_ref, *rest):
+    accumulate(
+        ((s0, 0), (s1b, n + m), (s2a, 2 * n), (s2b, 2 * n + m), (s3a, 3 * n)),
+        ((n, m), (3 * n + m, m)),
+        taps_ref,
+        cells,
+        total,
+    )
+
+
+def last_kernel(planes, low, high, taps_ref, before_ref, *rest):
     *out_refs, cells, total = rest
-    across = s2a.shape[1]
+    across = low.shape[1]
     height = cells.shape[1] // across
-    part = s2a.shape[0] // height
+    part = low.shape[0] // height
     channels = 2 * part
     filters = before_ref.shape[0] // 3
     first = planes[0] * filters
@@ -117,7 +125,7 @@
     cells[pl.ds(9 * channels, unused), :] = jnp.zeros((unused, cells.shape[1]), BF16)
     for start in range(0, height, ROWS):
         for h in range(start, start + ROWS):
-            for j, ref in enumerate((s2a, s2b)):
+            for j, ref in enumerate((low, high)):
                 rows = [[(3 * t + e) * channels + j * part for t in range(3)] for e in range(3)]
                 pack(ref, cells, h, height, rows)
         products = jnp.dot(
@@ -146,12 +154,25 @@
     high_ref[...] = whole_ref[low_ref.shape[0] :]
 
 
+def copy_kernel(one_ref, order_ref, out_ref):
+    out_ref[...] = one_ref[...]
+
+
+def behind(one, order):
+    return pl.pallas_call(
+        copy_kernel,
+        out_shape=jax.ShapeDtypeStruct(one.shape, one.dtype),
+        in_specs=[pl.BlockSpec(memory_space=pltpu.VMEM), pl.BlockSpec(memory_space=pl.ANY)],
+        compiler_params=LIMIT,
+        name="behind",
+    )(one, order)
+
+
 def local(volume, kernel):
     filters, channels = kernel.shape[3], kernel.shape[4]
     shard, _, height, across = volume.shape
     half = channels // 2
     cells = shard * height
-    limit = pltpu.CompilerParams(vmem_limit_bytes=24 * 1024 * 1024)
     own = volume.reshape(cells, across)
     other = lax.ppermute(own, "chan", [(i, (i + X) % (2 * X)) for i in range(2 * X)])
     s1, s3, s2 = [from_x(own, step) for step in (1, 3, 2)]
@@ -160,7 +181,7 @@
     near_taps, far_taps, last_taps = pl.pallas_call(
         taps_kernel,
         out_shape=(weights, weights, last_weights),
-        compiler_params=limit,
+        compiler_params=LIMIT,
         cost_estimate=pl.CostEstimate(flops=0, bytes_accessed=4_000_000, transcendentals=0),
         name="taps",
     )(kernel)
@@ -170,12 +191,12 @@
         divide_kernel,
         out_shape=(part, part),
         in_specs=[pl.BlockSpec(memory_space=pltpu.VMEM), pl.BlockSpec(memory_space=pl.ANY)],
-        compiler_params=limit,
+        compiler_params=LIMIT,
         name="divide",
     )(other, last_taps)
     t3a, t1b = from_x(low, 3), from_x(high, 1)
-    t3b, t1a = from_x(high, 3), from_x(low, 1)
     t2a, t2b = from_x(t3a, 3), from_x(t1b, 1)
+    t3b, t1a = from_x(behind(high, t1b), 3), from_x(behind(low, t3a), 1)
 
     def work(planes, part):
         return pl.CostEstimate(
@@ -190,7 +211,7 @@
         near_kernel,
         out_shape=total,
         scratch_shapes=[packed],
-        compiler_params=limit,
+        compiler_params=LIMIT,
         cost_estimate=work(3, 1),
         name="near",
     )(own, s1, s2, s3, near_taps)
@@ -198,10 +219,10 @@
         far_kernel,
         out_shape=total,
         scratch_shapes=[packed],
-        compiler_params=limit,
+        compiler_params=LIMIT,
         cost_estimate=work(3, 1),
         name="far",
-    )(other, t1a, t1b, t3a, t3b, far_taps, before)
+    )(other, t1b, t2a, t2b, t3a, far_taps, before)
 
     def last(name, *taps):
         part = jax.ShapeDtypeStruct((filters * height, across), F32)
@@ -212,13 +233,12 @@
                 pltpu.VMEM((3 * half, height * across), BF16),
                 pltpu.VMEM((len(taps) * filters, total.shape[1]), F32),
             ],
-            compiler_params=limit,
+            compiler_params=LIMIT,
             cost_estimate=work(len(taps), 0.25),
             name=name,
-        )(t2a, t2b, last_taps, before)
-
-    (off,) = last("off", 0)
-    on, mid = last("rest", 1, 2)
+        )(t1a, t3b, last_taps, before)
+
+    off, on, mid = last("last", 0, 1, 2)
     planes = lax.axis_size("depth")
     between = [(i, i + 1) for i in range(1, planes - 1, 2)]
     within = [(i, i + 1) for i in range(0, planes, 2)]

time: 43.9 us -> 44.6 us (1.016)
  waiting for transfers between devices: 9.56 us -> 12.4 us
  starting transfers between devices: 25.6 us -> 23.7 us
    ppermute x9, starting transfers between devices: 15.4 us -> 12.2 us  [from_x(): return lax.ppermute(block, 'chan', pairs)]
    ppermute x9, waiting for transfers between devices: 6.07 us -> 8.05 us  [from_x(): return lax.ppermute(block, 'chan', pairs)]
    ppermute x1, starting transfers between devices: 2.38 us -> 3.76 us  [local(): off = lax.ppermute(off, ('chan', 'depth'), pairs)]
    ppermute x1, waiting for transfers between devices: 3.49 us -> 4.35 us  [local(): off = lax.ppermute(off, ('chan', 'depth'), pairs)]
    pallas_call x2 -> x1, Pallas kernels: 1.34 us -> 1.01 us  [last(): pl.pallas_call(functools.partial(last_kernel, taps), out_shape=[part] * l...]
  transfers between devices with their start and end apart: 12 -> 12, of which waited for: 3 -> 2; matrix products, arithmetic and copies ran while one was open for 0% -> 0% of each run, Pallas kernels for 13% -> 11%
where the time goes in v8:
time: 44.6 us; the launch traced here: 44.2 us
  starting transfers between devices  23.7 us (53%)
  waiting for transfers between devices  12.4 us (28%)
  Pallas kernels  6.05 us (14%)
  local copies, waits for them, and re-layouts  1.17 us (3%)
  other arithmetic  0.74 us (2%)
    ppermute x9, starting transfers between devices, from_x(): return lax.ppermute(block, 'chan', pairs)  12.2 us
    ppermute x9, waiting for transfers between devices, from_x(): return lax.ppermute(block, 'chan', pairs)  8.05 us
    ppermute x1, starting transfers between devices, local(): lax.ppermute(own, 'chan', [(i, (i + X) % (2 * X)) for i in range(2 * X)])  7.74 us
    ppermute x1, waiting for transfers between devices, local(): off = lax.ppermute(off, ('chan', 'depth'), pairs)  4.35 us
    ppermute x1, starting transfers between devices, local(): off = lax.ppermute(off, ('chan', 'depth'), pairs)  3.76 us
    pallas_call x1, Pallas kernels, local(): pl.pallas_call(near_kernel, out_shape=total, scratch_shapes=[packed], com...  1.99 us
    pallas_call x1, Pallas kernels, local(): pl.pallas_call(far_kernel, out_shape=total, scratch_shapes=[packed], comp...  1.89 us
    unnamed x4, local copies, waits for them, and re-layouts  1.17 us
  transfers between devices with their start and end apart: 12, of which 2 were waited for; matrix products, arithmetic and copies ran while one was open for 0% of the time, Pallas kernels for 11%

profile of v8, /device:TPU:1, one launch (start us, length us, event | category | flops | bytes accessed | tf_op | source)
XLA Modules:
  0.0 44.2 jit_solution(925289541908028414)
XLA Ops:
  0.0 7.7 %collective-permute-start = (f32[512,128]{1,0:T(8,128)}, f32[512,128]{1,0:T(8,128)S(1)}, u32[]{:S(2)}, u32[]{:S(2)}) collective-permute-start(f32[512,128]{1,0:T(8,128)} %bitcast.4), channel_id=1, source_target_pairs={{0,128},{32,160},{64,192},{96,224},{128,0},{160,32},{192,64},{224,... | collective-permute-start | bytes 786440 | tf_op jit(solution)/shard_map/ppermute | solution.py:177
  7.7 1.2 %collective-permute-start.9 = (f32[512,128]{1,0:T(8,128)}, f32[512,128]{1,0:T(8,128)S(1)}, u32[]{:S(2)}, u32[]{:S(2)}) collective-permute-start(f32[512,128]{1,0:T(8,128)} %bitcast.5), channel_id=1, source_target_pairs={{0,32},{32,64},{64,96},{96,0},{128,160},{160,192},{192,224},{224,1... | collective-permute-start | bytes 786440 | tf_op jit(solution)/shard_map/ppermute | solution.py:149
  9.0 2.5 %collective-permute-start.8 = (f32[512,128]{1,0:T(8,128)}, f32[512,128]{1,0:T(8,128)S(1)}, u32[]{:S(2)}, u32[]{:S(2)}) collective-permute-start(f32[512,128]{1,0:T(8,128)} %bitcast.6), channel_id=1, source_target_pairs={{0,64},{32,96},{64,0},{96,32},{128,192},{160,224},{192,128},{224,1... | collective-permute-start | bytes 786440 | tf_op jit(solution)/shard_map/ppermute | solution.py:149
  11.4 1.2 %collective-permute-start.7 = (f32[512,128]{1,0:T(8,128)}, f32[512,128]{1,0:T(8,128)S(1)}, u32[]{:S(2)}, u32[]{:S(2)}) collective-permute-start(f32[512,128]{1,0:T(8,128)} %bitcast.7), channel_id=1, source_target_pairs={{0,96},{32,0},{64,32},{96,64},{128,224},{160,128},{192,160},{224,1... | collective-permute-start | bytes 786440 | tf_op jit(solution)/shard_map/ppermute | solution.py:149
  12.6 0.0 copy-start
  12.6 1.2 %copy-done = f32[3,3,3,32,256]{4,3,2,1,0:T(8,128)S(1)} copy-done((f32[3,3,3,32,256]{4,3,2,1,0:T(8,128)S(1)}, f32[3,3,3,32,256]{4,3,2,1,0:T(8,128)}, u32[]{:S(2)}) %copy-start) | copy-done | bytes 884760
  13.7 1.1 %taps.1 = (bf16[288,1152]{1,0:T(8,128)(2,1)S(1)}, bf16[288,1152]{1,0:T(8,128)(2,1)S(1)}, bf16[288,384]{1,0:T(8,128)(2,1)S(1)}) custom-call(f32[3,3,3,32,256]{4,3,2,1,0:T(8,128)S(1)} %copy-done), custom_call_target="tpu_custom_call" | custom-call | bytes 4000000 | tf_op jit(solution)/shard_map/taps/pallas_call | solution.py:181
  14.8 0.0 collective-permute-done.whole_ref.s0
  14.9 1.4 %collective-permute-start.1 = (f32[256,128]{1,0:T(8,128)S(1)}, f32[256,128]{1,0:T(8,128)S(1)}, u32[]{:S(2)}, u32[]{:S(2)}) collective-permute-start(f32[256,128]{1,0:T(8,128)S(1)} %get-tuple-element.14.one_ref), channel_id=1, source_target_pairs={{0,32},{32,64},{64,96},{96,0},{128,160},{160,192},{192,224},{224,1... | collective-permute-start | bytes 393224 | tf_op jit(solution)/shard_map/ppermute | solution.py:149
  16.3 1.4 %collective-permute-start.3 = (f32[256,128]{1,0:T(8,128)S(1)}, f32[256,128]{1,0:T(8,128)S(1)}, u32[]{:S(2)}, u32[]{:S(2)}) collective-permute-start(f32[256,128]{1,0:T(8,128)S(1)} %get-tuple-element.15.one_ref), channel_id=1, source_target_pairs={{0,96},{32,0},{64,32},{96,64},{128,224},{160,128},{192,160},{224,1... | collective-permute-start | bytes 393224 | tf_op jit(solution)/shard_map/ppermute | solution.py:149
  17.6 8.0 %collective-permute-done.1.order_ref.s3a = f32[256,128]{1,0:T(8,128)S(1)} collective-permute-done((f32[256,128]{1,0:T(8,128)S(1)}, f32[256,128]{1,0:T(8,128)S(1)}, u32[]{:S(2)}, u32[]{:S(2)}) %collective-permute-start.1) | collective-permute-done | bytes 131104 | tf_op jit(solution)/shard_map/ppermute | solution.py:149
  25.7 0.0 collective-permute-start.5
  25.7 0.0 collective-permute-done.3.order_ref.s1b
  25.7 3.1 %collective-permute-start.6 = (f32[256,128]{1,0:T(8,128)S(1)}, f32[256,128]{1,0:T(8,128)S(1)}, u32[]{:S(2)}, u32[]{:S(2)}) collective-permute-start(f32[256,128]{1,0:T(8,128)S(1)} %collective-permute-done.3.order_ref.s1b), channel_id=1, source_target_pairs={{0,96},{32,0},{64,32},{96,64},{128,224},{160,128},{192,160},{224,1... | collective-permute-start | bytes 393224 | tf_op jit(solution)/shard_map/ppermute | solution.py:149
  28.8 0.0 copy-start.1
  28.8 0.0 collective-permute-done.9.s3
  28.8 0.1 collective-permute-start.2
  28.9 0.0 collective-permute-done.8.s2
  28.9 1.4 %collective-permute-start.4 = (f32[256,128]{1,0:T(8,128)S(1)}, f32[256,128]{1,0:T(8,128)S(1)}, u32[]{:S(2)}, u32[]{:S(2)}) collective-permute-start(f32[256,128]{1,0:T(8,128)S(1)} %behind.3), channel_id=1, source_target_pairs={{0,32},{32,64},{64,96},{96,0},{128,160},{160,192},{192,224},{224,1... | collective-permute-start | bytes 393224 | tf_op jit(solution)/shard_map/ppermute | solution.py:149
  30.4 0.0 collective-permute-done.7.s1
  30.4 0.0 copy-done.1
  30.4 2.0 %near.1.near_ref = f32[96,2304]{1,0:T(8,128)S(1)} custom-call(f32[512,128]{1,0:T(8,128)S(1)} %bitcast.8, f32[512,128]{1,0:T(8,128)S(1)} %collective-permute-done.7.s1, f32[512,128]{1,0:T(8,128)S(1)} %collective-permute-done.8.s2, f32[512,128]{1,0:T(8,128)S(1)} %collective-permute-done.9.s3, bf16[288,1152]{1,0:T(8,128)(2,1)S(1)} %get-tuple-element.17.taps_ref), custom_call_target="tpu_custom_call" | custom-call | flops 1358954496 | bytes 3000000 | tf_op jit(solution)/shard_map/near/pallas_call | solution.py:210
  32.4 0.0 collective-permute-done.5.s2a
  32.4 0.0 collective-permute-done.6.s2b
  32.4 1.9 %far.1.before_ref = f32[96,2304]{1,0:T(8,128)S(1)} custom-call(f32[512,128]{1,0:T(8,128)S(1)} %collective-permute-done.whole_ref.s0, f32[256,128]{1,0:T(8,128)S(1)} %collective-permute-done.3.order_ref.s1b, f32[256,128]{1,0:T(8,128)S(1)} %collective-permute-done.5.s2a, f32[256,128]{1,0:T(8,128)S(1)} %collective-permute-done.6.s2b, ...), custom_call_target="tpu_custom_call" | custom-call | flops 1358954496 | bytes 3000000 | tf_op jit(solution)/shard_map/far/pallas_call | solution.py:218
  34.3 0.0 collective-permute-done.2.low
  34.3 0.0 collective-permute-done.4.high
  34.3 1.0 %last.1 = (f32[512,128]{1,0:T(8,128)S(1)}, f32[512,128]{1,0:T(8,128)S(1)}, f32[512,128]{1,0:T(8,128)S(1)}) custom-call(f32[256,128]{1,0:T(8,128)S(1)} %collective-permute-done.2.low, f32[256,128]{1,0:T(8,128)S(1)} %collective-permute-done.4.high, bf16[288,384]{1,0:T(8,128)(2,1)S(1)} %get-tuple-element.13.order_ref.taps_ref, f32[96,2304]{1,0:T(8,128)S(1)} %far.1.before_ref), custom_call_target="tpu_custom_call" | custom-call | flops 339738624 | bytes 3000000 | tf_op jit(solution)/shard_map/last/pallas_call | solution.py:229
  35.4 3.8 %collective-permute-start.10 = (f32[512,128]{1,0:T(8,128)S(1)}, f32[512,128]{1,0:T(8,128)S(1)}, u32[]{:S(2)}, u32[]{:S(2)}) collective-permute-start(f32[512,128]{1,0:T(8,128)S(1)} %get-tuple-element.19), channel_id=1, source_target_pairs={{1,2},{2,1},{3,4},{4,3},{5,6},{6,5},{7,8},{8,7},{9,10},{10,9},{11,... | collective-permute-start | bytes 786440 | tf_op jit(solution)/shard_map/ppermute | solution.py:249
  39.1 0.0 collective-permute-start.11
  39.1 4.3 %collective-permute-done.10 = f32[512,128]{1,0:T(8,128)S(1)} collective-permute-done((f32[512,128]{1,0:T(8,128)S(1)}, f32[512,128]{1,0:T(8,128)S(1)}, u32[]{:S(2)}, u32[]{:S(2)}) %collective-permute-start.10) | collective-permute-done | bytes 262176 | tf_op jit(solution)/shard_map/ppermute | solution.py:249
  43.5 0.0 collective-permute-done.11
  43.5 0.7 %add_add_fusion = f32[512,128]{1,0:T(8,128)} fusion(f32[512,128]{1,0:T(8,128)S(1)} %collective-permute-done.11, f32[512,128]{1,0:T(8,128)S(1)} %get-tuple-element.18, f32[512,128]{1,0:T(8,128)S(1)} %collective-permute-done.10), kind=kLoop, calls=%fused_computation | loop fusion | flops 131072 | bytes 1048576 | tf_op jit(solution)/shard_map/add | solution.py:251
  (3 shorter events, 0.0 us)
Async XLA Ops:
  0.0 14.8 %collective-permute-start = (f32[512,128]{1,0:T(8,128)}, f32[512,128]{1,0:T(8,128)S(1)}, u32[]{:S(2)}, u32[]{:S(2)}) collective-permute-start(f32[512,128]{1,0:T(8,128)} %bitcast.4), channel_id=1, source_target_pairs={{0,128},{32,160},{64,192},{96,224},{128,0},{160,32},{192,64},{224,... | collective-permute-start | bytes 786440 | tf_op jit(solution)/shard_map/ppermute | solution.py:177
  7.7 21.1 %collective-permute-start.9 = (f32[512,128]{1,0:T(8,128)}, f32[512,128]{1,0:T(8,128)S(1)}, u32[]{:S(2)}, u32[]{:S(2)}) collective-permute-start(f32[512,128]{1,0:T(8,128)} %bitcast.5), channel_id=1, source_target_pairs={{0,32},{32,64},{64,96},{96,0},{128,160},{160,192},{192,224},{224,1... | collective-permute-start | bytes 786440 | tf_op jit(solution)/shard_map/ppermute | solution.py:149
  9.0 20.0 %collective-permute-start.8 = (f32[512,128]{1,0:T(8,128)}, f32[512,128]{1,0:T(8,128)S(1)}, u32[]{:S(2)}, u32[]{:S(2)}) collective-permute-start(f32[512,128]{1,0:T(8,128)} %bitcast.6), channel_id=1, source_target_pairs={{0,64},{32,96},{64,0},{96,32},{128,192},{160,224},{192,128},{224,1... | collective-permute-start | bytes 786440 | tf_op jit(solution)/shard_map/ppermute | solution.py:149
  11.4 19.0 %collective-permute-start.7 = (f32[512,128]{1,0:T(8,128)}, f32[512,128]{1,0:T(8,128)S(1)}, u32[]{:S(2)}, u32[]{:S(2)}) collective-permute-start(f32[512,128]{1,0:T(8,128)} %bitcast.7), channel_id=1, source_target_pairs={{0,96},{32,0},{64,32},{96,64},{128,224},{160,128},{192,160},{224,1... | collective-permute-start | bytes 786440 | tf_op jit(solution)/shard_map/ppermute | solution.py:149
  12.6 1.2 %copy-start = (f32[3,3,3,32,256]{4,3,2,1,0:T(8,128)S(1)}, f32[3,3,3,32,256]{4,3,2,1,0:T(8,128)}, u32[]{:S(2)}) copy-start(f32[3,3,3,32,256]{4,3,2,1,0:T(8,128)} %kernel_ref.1) | copy-start | bytes 2654212
  14.9 10.8 %collective-permute-start.1 = (f32[256,128]{1,0:T(8,128)S(1)}, f32[256,128]{1,0:T(8,128)S(1)}, u32[]{:S(2)}, u32[]{:S(2)}) collective-permute-start(f32[256,128]{1,0:T(8,128)S(1)} %get-tuple-element.14.one_ref), channel_id=1, source_target_pairs={{0,32},{32,64},{64,96},{96,0},{128,160},{160,192},{192,224},{224,1... | collective-permute-start | bytes 393224 | tf_op jit(solution)/shard_map/ppermute | solution.py:149
  16.3 9.4 %collective-permute-start.3 = (f32[256,128]{1,0:T(8,128)S(1)}, f32[256,128]{1,0:T(8,128)S(1)}, u32[]{:S(2)}, u32[]{:S(2)}) collective-permute-start(f32[256,128]{1,0:T(8,128)S(1)} %get-tuple-element.15.one_ref), channel_id=1, source_target_pairs={{0,96},{32,0},{64,32},{96,64},{128,224},{160,128},{192,160},{224,1... | collective-permute-start | bytes 393224 | tf_op jit(solution)/shard_map/ppermute | solution.py:149
  25.7 6.7 %collective-permute-start.5 = (f32[256,128]{1,0:T(8,128)S(1)}, f32[256,128]{1,0:T(8,128)S(1)}, u32[]{:S(2)}, u32[]{:S(2)}) collective-permute-start(f32[256,128]{1,0:T(8,128)S(1)} %collective-permute-done.1.order_ref.s3a), channel_id=1, source_target_pairs={{0,32},{32,64},{64,96},{96,0},{128,160},{160,192},{192,224},{224,1... | collective-permute-start | bytes 393224 | tf_op jit(solution)/shard_map/ppermute | solution.py:149
  25.7 6.7 %collective-permute-start.6 = (f32[256,128]{1,0:T(8,128)S(1)}, f32[256,128]{1,0:T(8,128)S(1)}, u32[]{:S(2)}, u32[]{:S(2)}) collective-permute-start(f32[256,128]{1,0:T(8,128)S(1)} %collective-permute-done.3.order_ref.s1b), channel_id=1, source_target_pairs={{0,96},{32,0},{64,32},{96,64},{128,224},{160,128},{192,160},{224,1... | collective-permute-start | bytes 393224 | tf_op jit(solution)/shard_map/ppermute | solution.py:149
  28.8 1.6 %copy-start.1 = (f32[32,1,16,128]{3,2,1,0:T(8,128)S(1)}, f32[32,1,16,128]{3,2,1,0:T(8,128)}, u32[]{:S(2)}) copy-start(f32[32,1,16,128]{3,2,1,0:T(8,128)} %param.2) | copy-start | bytes 786436
  28.8 5.5 %collective-permute-start.2 = (f32[256,128]{1,0:T(8,128)S(1)}, f32[256,128]{1,0:T(8,128)S(1)}, u32[]{:S(2)}, u32[]{:S(2)}) collective-permute-start(f32[256,128]{1,0:T(8,128)S(1)} %behind.2), channel_id=1, source_target_pairs={{0,96},{32,0},{64,32},{96,64},{128,224},{160,128},{192,160},{224,1... | collective-permute-start | bytes 393224 | tf_op jit(solution)/shard_map/ppermute | solution.py:149
  28.9 5.4 %collective-permute-start.4 = (f32[256,128]{1,0:T(8,128)S(1)}, f32[256,128]{1,0:T(8,128)S(1)}, u32[]{:S(2)}, u32[]{:S(2)}) collective-permute-start(f32[256,128]{1,0:T(8,128)S(1)} %behind.3), channel_id=1, source_target_pairs={{0,32},{32,64},{64,96},{96,0},{128,160},{160,192},{192,224},{224,1... | collective-permute-start | bytes 393224 | tf_op jit(solution)/shard_map/ppermute | solution.py:149
  35.4 8.1 %collective-permute-start.10 = (f32[512,128]{1,0:T(8,128)S(1)}, f32[512,128]{1,0:T(8,128)S(1)}, u32[]{:S(2)}, u32[]{:S(2)}) collective-permute-start(f32[512,128]{1,0:T(8,128)S(1)} %get-tuple-element.19), channel_id=1, source_target_pairs={{1,2},{2,1},{3,4},{4,3},{5,6},{6,5},{7,8},{8,7},{9,10},{10,9},{11,... | collective-permute-start | bytes 786440 | tf_op jit(solution)/shard_map/ppermute | solution.py:249
  39.1 4.4 %collective-permute-start.11 = (f32[512,128]{1,0:T(8,128)S(1)}, f32[512,128]{1,0:T(8,128)S(1)}, u32[]{:S(2)}, u32[]{:S(2)}) collective-permute-start(f32[512,128]{1,0:T(8,128)S(1)} %get-tuple-element.20), channel_id=1, source_target_pairs={{0,1},{2,3},{4,5},{6,7},{8,9},{10,11},{12,13},{14,15},{16,17},{18,... | collective-permute-start | bytes 786440 | tf_op jit(solution)/shard_map/ppermute | solution.py:250

commit v9 on v8

--- a/solution.py
+++ b/solution.py
@@ -195,8 +195,6 @@
         name="divide",
     )(other, last_taps)
     t3a, t1b = from_x(low, 3), from_x(high, 1)
-    t2a, t2b = from_x(t3a, 3), from_x(t1b, 1)
-    t3b, t1a = from_x(behind(high, t1b), 3), from_x(behind(low, t3a), 1)
 
     def work(planes, part):
         return pl.CostEstimate(
@@ -215,6 +213,8 @@
         cost_estimate=work(3, 1),
         name="near",
     )(own, s1, s2, s3, near_taps)
+    t2a, t2b = from_x(behind(t3a, before), 3), from_x(behind(t1b, before), 1)
+    t3b, t1a = from_x(behind(high, t1b), 3), from_x(behind(low, t3a), 1)
     before = pl.pallas_call(
         far_kernel,
         out_shape=total,

time: 44.6 us -> 45.4 us (1.018)
  starting transfers between devices: 23.7 us -> 24.4 us
  transfers between devices with their start and end apart: 12 -> 12, of which waited for: 2 -> 6; matrix products, arithmetic and copies ran while one was open for 0% -> 0% of each run, Pallas kernels for 11% -> 11%
where the time goes in v9:
time: 45.4 us; the launch traced here: 45.3 us
  starting transfers between devices  24.4 us (54%)
  waiting for transfers between devices  12.8 us (28%)
  Pallas kernels  6.07 us (13%)
  local copies, waits for them, and re-layouts  1.17 us (3%)
  other arithmetic  0.74 us (2%)
    ppermute x9, starting transfers between devices, from_x(): return lax.ppermute(block, 'chan', pairs)  12.5 us
    ppermute x9, waiting for transfers between devices, from_x(): return lax.ppermute(block, 'chan', pairs)  8.46 us
    ppermute x1, starting transfers between devices, local(): lax.ppermute(own, 'chan', [(i, (i + X) % (2 * X)) for i in range(2 * X)])  7.74 us
    ppermute x1, waiting for transfers between devices, local(): off = lax.ppermute(off, ('chan', 'depth'), pairs)  4.35 us
    ppermute x1, starting transfers between devices, local(): off = lax.ppermute(off, ('chan', 'depth'), pairs)  4.17 us
    pallas_call x1, Pallas kernels, local(): pl.pallas_call(near_kernel, out_shape=total, scratch_shapes=[packed], com...  1.99 us
    pallas_call x1, Pallas kernels, local(): pl.pallas_call(far_kernel, out_shape=total, scratch_shapes=[packed], comp...  1.9 us
    unnamed x4, local copies, waits for them, and re-layouts  1.17 us
  transfers between devices with their start and end apart: 12, of which 6 were waited for; matrix products, arithmetic and copies ran while one was open for 0% of the time, Pallas kernels for 11%

profile of v9, /device:TPU:1, one launch (start us, length us, event | category | flops | bytes accessed | tf_op | source)
XLA Modules:
  0.0 45.3 jit_solution(18425421883051573080)
XLA Ops:
  0.0 7.7 %collective-permute-start = (f32[512,128]{1,0:T(8,128)}, f32[512,128]{1,0:T(8,128)S(1)}, u32[]{:S(2)}, u32[]{:S(2)}) collective-permute-start(f32[512,128]{1,0:T(8,128)} %bitcast.4), channel_id=1, source_target_pairs={{0,128},{32,160},{64,192},{96,224},{128,0},{160,32},{192,64},{224,... | collective-permute-start | bytes 786440 | tf_op jit(solution)/shard_map/ppermute | solution.py:177
  7.7 1.2 %collective-permute-start.7 = (f32[512,128]{1,0:T(8,128)}, f32[512,128]{1,0:T(8,128)S(1)}, u32[]{:S(2)}, u32[]{:S(2)}) collective-permute-start(f32[512,128]{1,0:T(8,128)} %bitcast.5), channel_id=1, source_target_pairs={{0,32},{32,64},{64,96},{96,0},{128,160},{160,192},{192,224},{224,1... | collective-permute-start | bytes 786440 | tf_op jit(solution)/shard_map/ppermute | solution.py:149
  9.0 2.5 %collective-permute-start.6 = (f32[512,128]{1,0:T(8,128)}, f32[512,128]{1,0:T(8,128)S(1)}, u32[]{:S(2)}, u32[]{:S(2)}) collective-permute-start(f32[512,128]{1,0:T(8,128)} %bitcast.6), channel_id=1, source_target_pairs={{0,64},{32,96},{64,0},{96,32},{128,192},{160,224},{192,128},{224,1... | collective-permute-start | bytes 786440 | tf_op jit(solution)/shard_map/ppermute | solution.py:149
  11.4 1.2 %collective-permute-start.5 = (f32[512,128]{1,0:T(8,128)}, f32[512,128]{1,0:T(8,128)S(1)}, u32[]{:S(2)}, u32[]{:S(2)}) collective-permute-start(f32[512,128]{1,0:T(8,128)} %bitcast.7), channel_id=1, source_target_pairs={{0,96},{32,0},{64,32},{96,64},{128,224},{160,128},{192,160},{224,1... | collective-permute-start | bytes 786440 | tf_op jit(solution)/shard_map/ppermute | solution.py:149
  12.6 0.0 copy-start
  12.6 1.2 %copy-done = f32[3,3,3,32,256]{4,3,2,1,0:T(8,128)S(1)} copy-done((f32[3,3,3,32,256]{4,3,2,1,0:T(8,128)S(1)}, f32[3,3,3,32,256]{4,3,2,1,0:T(8,128)}, u32[]{:S(2)}) %copy-start) | copy-done | bytes 884760
  13.7 1.1 %taps.1 = (bf16[288,1152]{1,0:T(8,128)(2,1)S(1)}, bf16[288,1152]{1,0:T(8,128)(2,1)S(1)}, bf16[288,384]{1,0:T(8,128)(2,1)S(1)}) custom-call(f32[3,3,3,32,256]{4,3,2,1,0:T(8,128)S(1)} %copy-done), custom_call_target="tpu_custom_call" | custom-call | bytes 4000000 | tf_op jit(solution)/shard_map/taps/pallas_call | solution.py:181
  14.8 0.0 copy-start.1
  14.9 0.0 collective-permute-done.whole_ref.s0
  14.9 1.4 %collective-permute-start.1 = (f32[256,128]{1,0:T(8,128)S(1)}, f32[256,128]{1,0:T(8,128)S(1)}, u32[]{:S(2)}, u32[]{:S(2)}) collective-permute-start(f32[256,128]{1,0:T(8,128)S(1)} %get-tuple-element.14.one_ref), channel_id=1, source_target_pairs={{0,32},{32,64},{64,96},{96,0},{128,160},{160,192},{192,224},{224,1... | collective-permute-start | bytes 393224 | tf_op jit(solution)/shard_map/ppermute | solution.py:149
  16.3 1.4 %collective-permute-start.3 = (f32[256,128]{1,0:T(8,128)S(1)}, f32[256,128]{1,0:T(8,128)S(1)}, u32[]{:S(2)}, u32[]{:S(2)}) collective-permute-start(f32[256,128]{1,0:T(8,128)S(1)} %get-tuple-element.15.one_ref), channel_id=1, source_target_pairs={{0,96},{32,0},{64,32},{96,64},{128,224},{160,128},{192,160},{224,1... | collective-permute-start | bytes 393224 | tf_op jit(solution)/shard_map/ppermute | solution.py:149
  17.7 0.0 collective-permute-done.7.s3
  17.7 5.0 %collective-permute-done.6.s2 = f32[512,128]{1,0:T(8,128)S(1)} collective-permute-done((f32[512,128]{1,0:T(8,128)}, f32[512,128]{1,0:T(8,128)S(1)}, u32[]{:S(2)}, u32[]{:S(2)}) %collective-permute-start.6) | collective-permute-done | bytes 262176 | tf_op jit(solution)/shard_map/ppermute | solution.py:149
  22.7 0.0 collective-permute-done.5.s1
  22.7 0.0 copy-done.1
  22.7 2.0 %near.1.order_ref.near_ref = f32[96,2304]{1,0:T(8,128)S(1)} custom-call(f32[512,128]{1,0:T(8,128)S(1)} %bitcast.8, f32[512,128]{1,0:T(8,128)S(1)} %collective-permute-done.5.s1, f32[512,128]{1,0:T(8,128)S(1)} %collective-permute-done.6.s2, f32[512,128]{1,0:T(8,128)S(1)} %collective-permute-done.7.s3, bf16[288,1152]{1,0:T(8,128)(2,1)S(1)} %get-tuple-element.16.taps_ref), custom_call_target="tpu_custom_call" | custom-call | flops 1358954496 | bytes 3000000 | tf_op jit(solution)/shard_map/near/pallas_call | solution.py:208
  24.7 1.0 %collective-permute-done.1.order_ref.one_ref.s3a = f32[256,128]{1,0:T(8,128)S(1)} collective-permute-done((f32[256,128]{1,0:T(8,128)S(1)}, f32[256,128]{1,0:T(8,128)S(1)}, u32[]{:S(2)}, u32[]{:S(2)}) %collective-permute-start.1) | collective-permute-done | bytes 131104 | tf_op jit(solution)/shard_map/ppermute | solution.py:149
  25.7 0.7 %collective-permute-start.8 = (f32[256,128]{1,0:T(8,128)S(1)}, f32[256,128]{1,0:T(8,128)S(1)}, u32[]{:S(2)}, u32[]{:S(2)}) collective-permute-start(f32[256,128]{1,0:T(8,128)S(1)} %behind.6), channel_id=1, source_target_pairs={{0,32},{32,64},{64,96},{96,0},{128,160},{160,192},{192,224},{224,1... | collective-permute-start | bytes 393224 | tf_op jit(solution)/shard_map/ppermute | solution.py:149
  26.4 0.0 collective-permute-done.3.order_ref.one_ref.s1b
  26.4 2.4 %collective-permute-start.9 = (f32[256,128]{1,0:T(8,128)S(1)}, f32[256,128]{1,0:T(8,128)S(1)}, u32[]{:S(2)}, u32[]{:S(2)}) collective-permute-start(f32[256,128]{1,0:T(8,128)S(1)} %behind.7), channel_id=1, source_target_pairs={{0,96},{32,0},{64,32},{96,64},{128,224},{160,128},{192,160},{224,1... | collective-permute-start | bytes 393224 | tf_op jit(solution)/shard_map/ppermute | solution.py:149
  28.9 0.8 %collective-permute-start.2 = (f32[256,128]{1,0:T(8,128)S(1)}, f32[256,128]{1,0:T(8,128)S(1)}, u32[]{:S(2)}, u32[]{:S(2)}) collective-permute-start(f32[256,128]{1,0:T(8,128)S(1)} %behind.4), channel_id=1, source_target_pairs={{0,96},{32,0},{64,32},{96,64},{128,224},{160,128},{192,160},{224,1... | collective-permute-start | bytes 393224 | tf_op jit(solution)/shard_map/ppermute | solution.py:149
  29.7 1.0 %collective-permute-start.4 = (f32[256,128]{1,0:T(8,128)S(1)}, f32[256,128]{1,0:T(8,128)S(1)}, u32[]{:S(2)}, u32[]{:S(2)}) collective-permute-start(f32[256,128]{1,0:T(8,128)S(1)} %behind.5), channel_id=1, source_target_pairs={{0,32},{32,64},{64,96},{96,0},{128,160},{160,192},{192,224},{224,1... | collective-permute-start | bytes 393224 | tf_op jit(solution)/shard_map/ppermute | solution.py:149
  30.7 0.1 collective-permute-done.8.s2a
  30.8 0.0 collective-permute-done.9.s2b
  30.8 1.9 %far.1.before_ref = f32[96,2304]{1,0:T(8,128)S(1)} custom-call(f32[512,128]{1,0:T(8,128)S(1)} %collective-permute-done.whole_ref.s0, f32[256,128]{1,0:T(8,128)S(1)} %collective-permute-done.3.order_ref.one_ref.s1b, f32[256,128]{1,0:T(8,128)S(1)} %collective-permute-done.8.s2a, f32[256,128]{1,0:T(8,128)S(1)} %collective-permute-done.9.s2b, ...), custom_call_target="tpu_custom_call" | custom-call | flops 1358954496 | bytes 3000000 | tf_op jit(solution)/shard_map/far/pallas_call | solution.py:218
  32.7 1.5 %collective-permute-done.2.low = f32[256,128]{1,0:T(8,128)S(1)} collective-permute-done((f32[256,128]{1,0:T(8,128)S(1)}, f32[256,128]{1,0:T(8,128)S(1)}, u32[]{:S(2)}, u32[]{:S(2)}) %collective-permute-start.2) | collective-permute-done | bytes 131104 | tf_op jit(solution)/shard_map/ppermute | solution.py:149
  34.2 0.8 %collective-permute-done.4.high = f32[256,128]{1,0:T(8,128)S(1)} collective-permute-done((f32[256,128]{1,0:T(8,128)S(1)}, f32[256,128]{1,0:T(8,128)S(1)}, u32[]{:S(2)}, u32[]{:S(2)}) %collective-permute-start.4) | collective-permute-done | bytes 131104 | tf_op jit(solution)/shard_map/ppermute | solution.py:149
  35.0 1.0 %last.1 = (f32[512,128]{1,0:T(8,128)S(1)}, f32[512,128]{1,0:T(8,128)S(1)}, f32[512,128]{1,0:T(8,128)S(1)}) custom-call(f32[256,128]{1,0:T(8,128)S(1)} %collective-permute-done.2.low, f32[256,128]{1,0:T(8,128)S(1)} %collective-permute-done.4.high, bf16[288,384]{1,0:T(8,128)(2,1)S(1)} %get-tuple-element.13.order_ref.taps_ref, f32[96,2304]{1,0:T(8,128)S(1)} %far.1.before_ref), custom_call_target="tpu_custom_call" | custom-call | flops 339738624 | bytes 3000000 | tf_op jit(solution)/shard_map/last/pallas_call | solution.py:229
  36.1 4.2 %collective-permute-start.10 = (f32[512,128]{1,0:T(8,128)S(1)}, f32[512,128]{1,0:T(8,128)S(1)}, u32[]{:S(2)}, u32[]{:S(2)}) collective-permute-start(f32[512,128]{1,0:T(8,128)S(1)} %get-tuple-element.19), channel_id=1, source_target_pairs={{1,2},{2,1},{3,4},{4,3},{5,6},{6,5},{7,8},{8,7},{9,10},{10,9},{11,... | collective-permute-start | bytes 786440 | tf_op jit(solution)/shard_map/ppermute | solution.py:249
  40.2 0.0 collective-permute-start.11
  40.2 4.3 %collective-permute-done.10 = f32[512,128]{1,0:T(8,128)S(1)} collective-permute-done((f32[512,128]{1,0:T(8,128)S(1)}, f32[512,128]{1,0:T(8,128)S(1)}, u32[]{:S(2)}, u32[]{:S(2)}) %collective-permute-start.10) | collective-permute-done | bytes 262176 | tf_op jit(solution)/shard_map/ppermute | solution.py:249
  44.6 0.0 collective-permute-done.11
  44.6 0.7 %add_add_fusion = f32[512,128]{1,0:T(8,128)} fusion(f32[512,128]{1,0:T(8,128)S(1)} %collective-permute-done.11, f32[512,128]{1,0:T(8,128)S(1)} %get-tuple-element.18, f32[512,128]{1,0:T(8,128)S(1)} %collective-permute-done.10), kind=kLoop, calls=%fused_computation | loop fusion | flops 131072 | bytes 1048576 | tf_op jit(solution)/shard_map/add | solution.py:251
  (5 shorter events, 0.1 us)
Async XLA Ops:
  0.0 14.9 %collective-permute-start = (f32[512,128]{1,0:T(8,128)}, f32[512,128]{1,0:T(8,128)S(1)}, u32[]{:S(2)}, u32[]{:S(2)}) collective-permute-start(f32[512,128]{1,0:T(8,128)} %bitcast.4), channel_id=1, source_target_pairs={{0,128},{32,160},{64,192},{96,224},{128,0},{160,32},{192,64},{224,... | collective-permute-start | bytes 786440 | tf_op jit(solution)/shard_map/ppermute | solution.py:177
  7.7 9.9 %collective-permute-start.7 = (f32[512,128]{1,0:T(8,128)}, f32[512,128]{1,0:T(8,128)S(1)}, u32[]{:S(2)}, u32[]{:S(2)}) collective-permute-start(f32[512,128]{1,0:T(8,128)} %bitcast.5), channel_id=1, source_target_pairs={{0,32},{32,64},{64,96},{96,0},{128,160},{160,192},{192,224},{224,1... | collective-permute-start | bytes 786440 | tf_op jit(solution)/shard_map/ppermute | solution.py:149
  9.0 13.7 %collective-permute-start.6 = (f32[512,128]{1,0:T(8,128)}, f32[512,128]{1,0:T(8,128)S(1)}, u32[]{:S(2)}, u32[]{:S(2)}) collective-permute-start(f32[512,128]{1,0:T(8,128)} %bitcast.6), channel_id=1, source_target_pairs={{0,64},{32,96},{64,0},{96,32},{128,192},{160,224},{192,128},{224,1... | collective-permute-start | bytes 786440 | tf_op jit(solution)/shard_map/ppermute | solution.py:149
  11.4 11.3 %collective-permute-start.5 = (f32[512,128]{1,0:T(8,128)}, f32[512,128]{1,0:T(8,128)S(1)}, u32[]{:S(2)}, u32[]{:S(2)}) collective-permute-start(f32[512,128]{1,0:T(8,128)} %bitcast.7), channel_id=1, source_target_pairs={{0,96},{32,0},{64,32},{96,64},{128,224},{160,128},{192,160},{224,1... | collective-permute-start | bytes 786440 | tf_op jit(solution)/shard_map/ppermute | solution.py:149
  12.6 1.2 %copy-start = (f32[3,3,3,32,256]{4,3,2,1,0:T(8,128)S(1)}, f32[3,3,3,32,256]{4,3,2,1,0:T(8,128)}, u32[]{:S(2)}) copy-start(f32[3,3,3,32,256]{4,3,2,1,0:T(8,128)} %kernel_ref.1) | copy-start | bytes 2654212
  14.8 7.8 %copy-start.1 = (f32[32,1,16,128]{3,2,1,0:T(8,128)S(1)}, f32[32,1,16,128]{3,2,1,0:T(8,128)}, u32[]{:S(2)}) copy-start(f32[32,1,16,128]{3,2,1,0:T(8,128)} %param.2) | copy-start | bytes 786436
  14.9 10.8 %collective-permute-start.1 = (f32[256,128]{1,0:T(8,128)S(1)}, f32[256,128]{1,0:T(8,128)S(1)}, u32[]{:S(2)}, u32[]{:S(2)}) collective-permute-start(f32[256,128]{1,0:T(8,128)S(1)} %get-tuple-element.14.one_ref), channel_id=1, source_target_pairs={{0,32},{32,64},{64,96},{96,0},{128,160},{160,192},{192,224},{224,1... | collective-permute-start | bytes 393224 | tf_op jit(solution)/shard_map/ppermute | solution.py:149
  16.3 10.1 %collective-permute-start.3 = (f32[256,128]{1,0:T(8,128)S(1)}, f32[256,128]{1,0:T(8,128)S(1)}, u32[]{:S(2)}, u32[]{:S(2)}) collective-permute-start(f32[256,128]{1,0:T(8,128)S(1)} %get-tuple-element.15.one_ref), channel_id=1, source_target_pairs={{0,96},{32,0},{64,32},{96,64},{128,224},{160,128},{192,160},{224,1... | collective-permute-start | bytes 393224 | tf_op jit(solution)/shard_map/ppermute | solution.py:149
  25.7 5.1 %collective-permute-start.8 = (f32[256,128]{1,0:T(8,128)S(1)}, f32[256,128]{1,0:T(8,128)S(1)}, u32[]{:S(2)}, u32[]{:S(2)}) collective-permute-start(f32[256,128]{1,0:T(8,128)S(1)} %behind.6), channel_id=1, source_target_pairs={{0,32},{32,64},{64,96},{96,0},{128,160},{160,192},{192,224},{224,1... | collective-permute-start | bytes 393224 | tf_op jit(solution)/shard_map/ppermute | solution.py:149
  26.4 4.4 %collective-permute-start.9 = (f32[256,128]{1,0:T(8,128)S(1)}, f32[256,128]{1,0:T(8,128)S(1)}, u32[]{:S(2)}, u32[]{:S(2)}) collective-permute-start(f32[256,128]{1,0:T(8,128)S(1)} %behind.7), channel_id=1, source_target_pairs={{0,96},{32,0},{64,32},{96,64},{128,224},{160,128},{192,160},{224,1... | collective-permute-start | bytes 393224 | tf_op jit(solution)/shard_map/ppermute | solution.py:149
  28.9 5.3 %collective-permute-start.2 = (f32[256,128]{1,0:T(8,128)S(1)}, f32[256,128]{1,0:T(8,128)S(1)}, u32[]{:S(2)}, u32[]{:S(2)}) collective-permute-start(f32[256,128]{1,0:T(8,128)S(1)} %behind.4), channel_id=1, source_target_pairs={{0,96},{32,0},{64,32},{96,64},{128,224},{160,128},{192,160},{224,1... | collective-permute-start | bytes 393224 | tf_op jit(solution)/shard_map/ppermute | solution.py:149
  29.7 5.3 %collective-permute-start.4 = (f32[256,128]{1,0:T(8,128)S(1)}, f32[256,128]{1,0:T(8,128)S(1)}, u32[]{:S(2)}, u32[]{:S(2)}) collective-permute-start(f32[256,128]{1,0:T(8,128)S(1)} %behind.5), channel_id=1, source_target_pairs={{0,32},{32,64},{64,96},{96,0},{128,160},{160,192},{192,224},{224,1... | collective-permute-start | bytes 393224 | tf_op jit(solution)/shard_map/ppermute | solution.py:149
  36.1 8.5 %collective-permute-start.10 = (f32[512,128]{1,0:T(8,128)S(1)}, f32[512,128]{1,0:T(8,128)S(1)}, u32[]{:S(2)}, u32[]{:S(2)}) collective-permute-start(f32[512,128]{1,0:T(8,128)S(1)} %get-tuple-element.19), channel_id=1, source_target_pairs={{1,2},{2,1},{3,4},{4,3},{5,6},{6,5},{7,8},{8,7},{9,10},{10,9},{11,... | collective-permute-start | bytes 786440 | tf_op jit(solution)/shard_map/ppermute | solution.py:249
  40.2 4.4 %collective-permute-start.11 = (f32[512,128]{1,0:T(8,128)S(1)}, f32[512,128]{1,0:T(8,128)S(1)}, u32[]{:S(2)}, u32[]{:S(2)}) collective-permute-start(f32[512,128]{1,0:T(8,128)S(1)} %get-tuple-element.20), channel_id=1, source_target_pairs={{0,1},{2,3},{4,5},{6,7},{8,9},{10,11},{12,13},{14,15},{16,17},{18,... | collective-permute-start | bytes 786440 | tf_op jit(solution)/shard_map/ppermute | solution.py:250

commit v10 on v7

--- a/solution.py
+++ b/solution.py
@@ -199,7 +199,7 @@
         out_shape=total,
         scratch_shapes=[packed],
         compiler_params=limit,
-        cost_estimate=work(3, 1),
+        cost_estimate=work(3, 4),
         name="far",
     )(other, t1a, t1b, t3a, t3b, far_taps, before)
 

time: 43.9 us -> 43.9 us (level)
  transfers between devices with their start and end apart: 12 -> 12, of which waited for: 3 -> 4; matrix products, arithmetic and copies ran while one was open for 0% -> 0% of each run, Pallas kernels for 13% -> 13%
where the time goes in v10:
time: 43.9 us; the launch traced here: 43.4 us
  starting transfers between devices  25.6 us (58%)
  waiting for transfers between devices  9.58 us (22%)
  Pallas kernels  6.17 us (14%)
  local copies, waits for them, and re-layouts  1.17 us (3%)
  other arithmetic  0.75 us (2%)
    ppermute x9, starting transfers between devices, from_x(): return lax.ppermute(block, 'chan', pairs)  15.4 us
    ppermute x1, starting transfers between devices, local(): lax.ppermute(own, 'chan', [(i, (i + X) % (2 * X)) for i in range(2 * X)])  7.74 us
    ppermute x9, waiting for transfers between devices, from_x(): return lax.ppermute(block, 'chan', pairs)  6.08 us
    ppermute x1, waiting for transfers between devices, local(): off = lax.ppermute(off, ('chan', 'depth'), pairs)  3.49 us
    ppermute x1, starting transfers between devices, local(): off = lax.ppermute(off, ('chan', 'depth'), pairs)  2.38 us
    pallas_call x1, Pallas kernels, local(): pl.pallas_call(near_kernel, out_shape=total, scratch_shapes=[packed], com...  1.99 us
    pallas_call x1, Pallas kernels, local(): pl.pallas_call(far_kernel, out_shape=total, scratch_shapes=[packed], comp...  1.91 us
    pallas_call x2, Pallas kernels, last(): pl.pallas_call(functools.partial(last_kernel, taps), out_shape=[part] * l...  1.34 us
  transfers between devices with their start and end apart: 12, of which 4 were waited for; matrix products, arithmetic and copies ran while one was open for 0% of the time, Pallas kernels for 13%

profile of v10, /device:TPU:1, one launch (start us, length us, event | category | flops | bytes accessed | tf_op | source)
XLA Modules:
  0.0 43.4 jit_solution(14310484663138655488)
XLA Ops:
  0.0 7.7 %collective-permute-start = (f32[512,128]{1,0:T(8,128)}, f32[512,128]{1,0:T(8,128)S(1)}, u32[]{:S(2)}, u32[]{:S(2)}) collective-permute-start(f32[512,128]{1,0:T(8,128)} %bitcast.4), channel_id=1, source_target_pairs={{0,128},{32,160},{64,192},{96,224},{128,0},{160,32},{192,64},{224,... | collective-permute-start | bytes 786440 | tf_op jit(solution)/shard_map/ppermute | solution.py:156
  7.7 2.5 %collective-permute-start.7 = (f32[512,128]{1,0:T(8,128)}, f32[512,128]{1,0:T(8,128)S(1)}, u32[]{:S(2)}, u32[]{:S(2)}) collective-permute-start(f32[512,128]{1,0:T(8,128)} %bitcast.5), channel_id=1, source_target_pairs={{0,96},{32,0},{64,32},{96,64},{128,224},{160,128},{192,160},{224,1... | collective-permute-start | bytes 786440 | tf_op jit(solution)/shard_map/ppermute | solution.py:141
  10.2 0.5 %collective-permute-start.8 = (f32[512,128]{1,0:T(8,128)}, f32[512,128]{1,0:T(8,128)S(1)}, u32[]{:S(2)}, u32[]{:S(2)}) collective-permute-start(f32[512,128]{1,0:T(8,128)} %bitcast.6), channel_id=1, source_target_pairs={{0,64},{32,96},{64,0},{96,32},{128,192},{160,224},{192,128},{224,1... | collective-permute-start | bytes 786440 | tf_op jit(solution)/shard_map/ppermute | solution.py:141
  10.7 0.6 %collective-permute-start.9 = (f32[512,128]{1,0:T(8,128)}, f32[512,128]{1,0:T(8,128)S(1)}, u32[]{:S(2)}, u32[]{:S(2)}) collective-permute-start(f32[512,128]{1,0:T(8,128)} %bitcast.7), channel_id=1, source_target_pairs={{0,32},{32,64},{64,96},{96,0},{128,160},{160,192},{192,224},{224,1... | collective-permute-start | bytes 786440 | tf_op jit(solution)/shard_map/ppermute | solution.py:141
  11.3 0.0 copy-start
  11.3 1.2 %copy-done = f32[3,3,3,32,256]{4,3,2,1,0:T(8,128)S(1)} copy-done((f32[3,3,3,32,256]{4,3,2,1,0:T(8,128)S(1)}, f32[3,3,3,32,256]{4,3,2,1,0:T(8,128)}, u32[]{:S(2)}) %copy-start) | copy-done | bytes 884760
  12.5 0.9 %taps.1 = (bf16[288,1152]{1,0:T(8,128)(2,1)S(1)}, bf16[288,1152]{1,0:T(8,128)(2,1)S(1)}, bf16[288,384]{1,0:T(8,128)(2,1)S(1)}) custom-call(f32[3,3,3,32,256]{4,3,2,1,0:T(8,128)S(1)} %copy-done), custom_call_target="tpu_custom_call" | custom-call | bytes 4000000 | tf_op jit(solution)/shard_map/taps/pallas_call | solution.py:160
  13.4 0.0 copy-start.1
  13.5 0.0 collective-permute-done.whole_ref.s0
  13.5 2.8 %collective-permute-start.1 = (f32[256,128]{1,0:T(8,128)S(1)}, f32[256,128]{1,0:T(8,128)S(1)}, u32[]{:S(2)}, u32[]{:S(2)}) collective-permute-start(f32[256,128]{1,0:T(8,128)S(1)} %get-tuple-element.13), channel_id=1, source_target_pairs={{0,32},{32,64},{64,96},{96,0},{128,160},{160,192},{192,224},{224,1... | collective-permute-start | bytes 393224 | tf_op jit(solution)/shard_map/ppermute | solution.py:141
  16.3 1.4 %collective-permute-start.3 = (f32[256,128]{1,0:T(8,128)S(1)}, f32[256,128]{1,0:T(8,128)S(1)}, u32[]{:S(2)}, u32[]{:S(2)}) collective-permute-start(f32[256,128]{1,0:T(8,128)S(1)} %get-tuple-element.14), channel_id=1, source_target_pairs={{0,96},{32,0},{64,32},{96,64},{128,224},{160,128},{192,160},{224,1... | collective-permute-start | bytes 393224 | tf_op jit(solution)/shard_map/ppermute | solution.py:141
  17.6 0.0 collective-permute-done.7.s1
  17.6 2.1 %collective-permute-start.5 = (f32[256,128]{1,0:T(8,128)S(1)}, f32[256,128]{1,0:T(8,128)S(1)}, u32[]{:S(2)}, u32[]{:S(2)}) collective-permute-start(f32[256,128]{1,0:T(8,128)S(1)} %get-tuple-element.13), channel_id=1, source_target_pairs={{0,96},{32,0},{64,32},{96,64},{128,224},{160,128},{192,160},{224,1... | collective-permute-start | bytes 393224 | tf_op jit(solution)/shard_map/ppermute | solution.py:141
  19.8 0.0 collective-permute-done.8.s2
  19.8 2.8 %collective-permute-start.6 = (f32[256,128]{1,0:T(8,128)S(1)}, f32[256,128]{1,0:T(8,128)S(1)}, u32[]{:S(2)}, u32[]{:S(2)}) collective-permute-start(f32[256,128]{1,0:T(8,128)S(1)} %get-tuple-element.14), channel_id=1, source_target_pairs={{0,32},{32,64},{64,96},{96,0},{128,160},{160,192},{192,224},{224,1... | collective-permute-start | bytes 393224 | tf_op jit(solution)/shard_map/ppermute | solution.py:141
  22.6 3.2 %collective-permute-done.9.s3 = f32[512,128]{1,0:T(8,128)S(1)} collective-permute-done((f32[512,128]{1,0:T(8,128)}, f32[512,128]{1,0:T(8,128)S(1)}, u32[]{:S(2)}, u32[]{:S(2)}) %collective-permute-start.9) | collective-permute-done | bytes 262176 | tf_op jit(solution)/shard_map/ppermute | solution.py:141
  25.8 0.0 copy-done.1
  25.8 2.0 %near.1.near_ref = f32[96,2304]{1,0:T(8,128)S(1)} custom-call(f32[512,128]{1,0:T(8,128)S(1)} %bitcast.8, f32[512,128]{1,0:T(8,128)S(1)} %collective-permute-done.7.s1, f32[512,128]{1,0:T(8,128)S(1)} %collective-permute-done.8.s2, f32[512,128]{1,0:T(8,128)S(1)} %collective-permute-done.9.s3, bf16[288,1152]{1,0:T(8,128)(2,1)S(1)} %get-tuple-element.16.taps_ref), custom_call_target="tpu_custom_call" | custom-call | flops 1358954496 | bytes 3000000 | tf_op jit(solution)/shard_map/near/pallas_call | solution.py:189
  27.8 0.8 %collective-permute-done.1.s3a = f32[256,128]{1,0:T(8,128)S(1)} collective-permute-done((f32[256,128]{1,0:T(8,128)S(1)}, f32[256,128]{1,0:T(8,128)S(1)}, u32[]{:S(2)}, u32[]{:S(2)}) %collective-permute-start.1) | collective-permute-done | bytes 131104 | tf_op jit(solution)/shard_map/ppermute | solution.py:141
  28.6 0.0 collective-permute-start.2
  28.6 0.0 collective-permute-done.3.s1b
  28.6 2.7 %collective-permute-start.4 = (f32[256,128]{1,0:T(8,128)S(1)}, f32[256,128]{1,0:T(8,128)S(1)}, u32[]{:S(2)}, u32[]{:S(2)}) collective-permute-start(f32[256,128]{1,0:T(8,128)S(1)} %collective-permute-done.3.s1b), channel_id=1, source_target_pairs={{0,96},{32,0},{64,32},{96,64},{128,224},{160,128},{192,160},{224,1... | collective-permute-start | bytes 393224 | tf_op jit(solution)/shard_map/ppermute | solution.py:141
  31.3 0.0 collective-permute-done.5.s1a
  31.3 0.0 collective-permute-done.6.s3b
  31.3 1.9 %far.1.before_ref = f32[96,2304]{1,0:T(8,128)S(1)} custom-call(f32[512,128]{1,0:T(8,128)S(1)} %collective-permute-done.whole_ref.s0, f32[256,128]{1,0:T(8,128)S(1)} %collective-permute-done.5.s1a, f32[256,128]{1,0:T(8,128)S(1)} %collective-permute-done.3.s1b, f32[256,128]{1,0:T(8,128)S(1)} %collective-permute-done.1.s3a, ...), custom_call_target="tpu_custom_call" | custom-call | flops 5435817984 | bytes 3000000 | tf_op jit(solution)/shard_map/far/pallas_call | solution.py:197
  33.2 2.1 %collective-permute-done.2.s2a = f32[256,128]{1,0:T(8,128)S(1)} collective-permute-done((f32[256,128]{1,0:T(8,128)S(1)}, f32[256,128]{1,0:T(8,128)S(1)}, u32[]{:S(2)}, u32[]{:S(2)}) %collective-permute-start.2) | collective-permute-done | bytes 131104 | tf_op jit(solution)/shard_map/ppermute | solution.py:141
  35.3 0.0 collective-permute-done.4.s2b
  35.3 0.6 %off.1 = f32[512,128]{1,0:T(8,128)S(1)} custom-call(f32[256,128]{1,0:T(8,128)S(1)} %collective-permute-done.2.s2a, f32[256,128]{1,0:T(8,128)S(1)} %collective-permute-done.4.s2b, bf16[288,384]{1,0:T(8,128)(2,1)S(1)} %get-tuple-element.12.order_ref.taps_ref, f32[96,2304]{1,0:T(8,128)S(1)} %far.1.before_ref), custom_call_target="tpu_custom_call" | custom-call | flops 113246208 | bytes 3000000 | tf_op jit(solution)/shard_map/off/pallas_call | solution.py:208
  35.9 2.4 %collective-permute-start.10 = (f32[512,128]{1,0:T(8,128)S(1)}, f32[512,128]{1,0:T(8,128)S(1)}, u32[]{:S(2)}, u32[]{:S(2)}) collective-permute-start(f32[512,128]{1,0:T(8,128)S(1)} %off.1), channel_id=1, source_target_pairs={{1,2},{2,1},{3,4},{4,3},{5,6},{6,5},{7,8},{8,7},{9,10},{10,9},{11,... | collective-permute-start | bytes 786440 | tf_op jit(solution)/shard_map/ppermute | solution.py:229
  38.3 0.7 %rest.1 = (f32[512,128]{1,0:T(8,128)S(1)}, f32[512,128]{1,0:T(8,128)S(1)}) custom-call(f32[256,128]{1,0:T(8,128)S(1)} %collective-permute-done.2.s2a, f32[256,128]{1,0:T(8,128)S(1)} %collective-permute-done.4.s2b, bf16[288,384]{1,0:T(8,128)(2,1)S(1)} %get-tuple-element.12.order_ref.taps_ref, f32[96,2304]{1,0:T(8,128)S(1)} %far.1.before_ref), custom_call_target="tpu_custom_call" | custom-call | flops 226492416 | bytes 3000000 | tf_op jit(solution)/shard_map/rest/pallas_call | solution.py:208
  39.0 0.1 collective-permute-start.11
  39.1 3.5 %collective-permute-done.10 = f32[512,128]{1,0:T(8,128)S(1)} collective-permute-done((f32[512,128]{1,0:T(8,128)S(1)}, f32[512,128]{1,0:T(8,128)S(1)}, u32[]{:S(2)}, u32[]{:S(2)}) %collective-permute-start.10) | collective-permute-done | bytes 262176 | tf_op jit(solution)/shard_map/ppermute | solution.py:229
  42.6 0.0 collective-permute-done.11
  42.6 0.8 %add_add_fusion = f32[512,128]{1,0:T(8,128)} fusion(f32[512,128]{1,0:T(8,128)S(1)} %collective-permute-done.11, f32[512,128]{1,0:T(8,128)S(1)} %get-tuple-element.17, f32[512,128]{1,0:T(8,128)S(1)} %collective-permute-done.10), kind=kLoop, calls=%fused_computation | loop fusion | flops 131072 | bytes 1048576 | tf_op jit(solution)/shard_map/add | solution.py:231
  (1 shorter events, 0.0 us)
Async XLA Ops:
  0.0 13.5 %collective-permute-start = (f32[512,128]{1,0:T(8,128)}, f32[512,128]{1,0:T(8,128)S(1)}, u32[]{:S(2)}, u32[]{:S(2)}) collective-permute-start(f32[512,128]{1,0:T(8,128)} %bitcast.4), channel_id=1, source_target_pairs={{0,128},{32,160},{64,192},{96,224},{128,0},{160,32},{192,64},{224,... | collective-permute-start | bytes 786440 | tf_op jit(solution)/shard_map/ppermute | solution.py:156
  7.7 9.9 %collective-permute-start.7 = (f32[512,128]{1,0:T(8,128)}, f32[512,128]{1,0:T(8,128)S(1)}, u32[]{:S(2)}, u32[]{:S(2)}) collective-permute-start(f32[512,128]{1,0:T(8,128)} %bitcast.5), channel_id=1, source_target_pairs={{0,96},{32,0},{64,32},{96,64},{128,224},{160,128},{192,160},{224,1... | collective-permute-start | bytes 786440 | tf_op jit(solution)/shard_map/ppermute | solution.py:141
  10.2 9.6 %collective-permute-start.8 = (f32[512,128]{1,0:T(8,128)}, f32[512,128]{1,0:T(8,128)S(1)}, u32[]{:S(2)}, u32[]{:S(2)}) collective-permute-start(f32[512,128]{1,0:T(8,128)} %bitcast.6), channel_id=1, source_target_pairs={{0,64},{32,96},{64,0},{96,32},{128,192},{160,224},{192,128},{224,1... | collective-permute-start | bytes 786440 | tf_op jit(solution)/shard_map/ppermute | solution.py:141
  10.7 15.0 %collective-permute-start.9 = (f32[512,128]{1,0:T(8,128)}, f32[512,128]{1,0:T(8,128)S(1)}, u32[]{:S(2)}, u32[]{:S(2)}) collective-permute-start(f32[512,128]{1,0:T(8,128)} %bitcast.7), channel_id=1, source_target_pairs={{0,32},{32,64},{64,96},{96,0},{128,160},{160,192},{192,224},{224,1... | collective-permute-start | bytes 786440 | tf_op jit(solution)/shard_map/ppermute | solution.py:141
  11.3 1.2 %copy-start = (f32[3,3,3,32,256]{4,3,2,1,0:T(8,128)S(1)}, f32[3,3,3,32,256]{4,3,2,1,0:T(8,128)}, u32[]{:S(2)}) copy-start(f32[3,3,3,32,256]{4,3,2,1,0:T(8,128)} %kernel_ref.1) | copy-start | bytes 2654212
  13.4 12.3 %copy-start.1 = (f32[32,1,16,128]{3,2,1,0:T(8,128)S(1)}, f32[32,1,16,128]{3,2,1,0:T(8,128)}, u32[]{:S(2)}) copy-start(f32[32,1,16,128]{3,2,1,0:T(8,128)} %param.2) | copy-start | bytes 786436
  13.5 15.1 %collective-permute-start.1 = (f32[256,128]{1,0:T(8,128)S(1)}, f32[256,128]{1,0:T(8,128)S(1)}, u32[]{:S(2)}, u32[]{:S(2)}) collective-permute-start(f32[256,128]{1,0:T(8,128)S(1)} %get-tuple-element.13), channel_id=1, source_target_pairs={{0,32},{32,64},{64,96},{96,0},{128,160},{160,192},{192,224},{224,1... | collective-permute-start | bytes 393224 | tf_op jit(solution)/shard_map/ppermute | solution.py:141
  16.3 12.3 %collective-permute-start.3 = (f32[256,128]{1,0:T(8,128)S(1)}, f32[256,128]{1,0:T(8,128)S(1)}, u32[]{:S(2)}, u32[]{:S(2)}) collective-permute-start(f32[256,128]{1,0:T(8,128)S(1)} %get-tuple-element.14), channel_id=1, source_target_pairs={{0,96},{32,0},{64,32},{96,64},{128,224},{160,128},{192,160},{224,1... | collective-permute-start | bytes 393224 | tf_op jit(solution)/shard_map/ppermute | solution.py:141
  17.6 13.6 %collective-permute-start.5 = (f32[256,128]{1,0:T(8,128)S(1)}, f32[256,128]{1,0:T(8,128)S(1)}, u32[]{:S(2)}, u32[]{:S(2)}) collective-permute-start(f32[256,128]{1,0:T(8,128)S(1)} %get-tuple-element.13), channel_id=1, source_target_pairs={{0,96},{32,0},{64,32},{96,64},{128,224},{160,128},{192,160},{224,1... | collective-permute-start | bytes 393224 | tf_op jit(solution)/shard_map/ppermute | solution.py:141
  19.8 11.5 %collective-permute-start.6 = (f32[256,128]{1,0:T(8,128)S(1)}, f32[256,128]{1,0:T(8,128)S(1)}, u32[]{:S(2)}, u32[]{:S(2)}) collective-permute-start(f32[256,128]{1,0:T(8,128)S(1)} %get-tuple-element.14), channel_id=1, source_target_pairs={{0,32},{32,64},{64,96},{96,0},{128,160},{160,192},{192,224},{224,1... | collective-permute-start | bytes 393224 | tf_op jit(solution)/shard_map/ppermute | solution.py:141
  28.6 6.7 %collective-permute-start.2 = (f32[256,128]{1,0:T(8,128)S(1)}, f32[256,128]{1,0:T(8,128)S(1)}, u32[]{:S(2)}, u32[]{:S(2)}) collective-permute-start(f32[256,128]{1,0:T(8,128)S(1)} %collective-permute-done.1.s3a), channel_id=1, source_target_pairs={{0,32},{32,64},{64,96},{96,0},{128,160},{160,192},{192,224},{224,1... | collective-permute-start | bytes 393224 | tf_op jit(solution)/shard_map/ppermute | solution.py:141
  28.6 6.7 %collective-permute-start.4 = (f32[256,128]{1,0:T(8,128)S(1)}, f32[256,128]{1,0:T(8,128)S(1)}, u32[]{:S(2)}, u32[]{:S(2)}) collective-permute-start(f32[256,128]{1,0:T(8,128)S(1)} %collective-permute-done.3.s1b), channel_id=1, source_target_pairs={{0,96},{32,0},{64,32},{96,64},{128,224},{160,128},{192,160},{224,1... | collective-permute-start | bytes 393224 | tf_op jit(solution)/shard_map/ppermute | solution.py:141
  35.9 6.7 %collective-permute-start.10 = (f32[512,128]{1,0:T(8,128)S(1)}, f32[512,128]{1,0:T(8,128)S(1)}, u32[]{:S(2)}, u32[]{:S(2)}) collective-permute-start(f32[512,128]{1,0:T(8,128)S(1)} %off.1), channel_id=1, source_target_pairs={{1,2},{2,1},{3,4},{4,3},{5,6},{6,5},{7,8},{8,7},{9,10},{10,9},{11,... | collective-permute-start | bytes 786440 | tf_op jit(solution)/shard_map/ppermute | solution.py:229
  39.0 3.6 %collective-permute-start.11 = (f32[512,128]{1,0:T(8,128)S(1)}, f32[512,128]{1,0:T(8,128)S(1)}, u32[]{:S(2)}, u32[]{:S(2)}) collective-permute-start(f32[512,128]{1,0:T(8,128)S(1)} %get-tuple-element.18), channel_id=1, source_target_pairs={{0,1},{2,3},{4,5},{6,7},{8,9},{10,11},{12,13},{14,15},{16,17},{18,... | collective-permute-start | bytes 786440 | tf_op jit(solution)/shard_map/ppermute | solution.py:230

commit v11 on v10

--- a/solution.py
+++ b/solution.py
@@ -8,7 +8,7 @@
 from jax.sharding import PartitionSpec as P
 
 X = 4
-ROWS = 2
+ROWS = 4
 F32, BF16 = jnp.float32, jnp.bfloat16
 
 

time: 43.9 us -> 43.9 us (level)
  no operation moved by 1% of the time
where the time goes in v11:
time: 43.9 us; the launch traced here: 43.4 us
  starting transfers between devices  25.6 us (58%)
  waiting for transfers between devices  9.58 us (22%)
  Pallas kernels  6.17 us (14%)
  local copies, waits for them, and re-layouts  1.17 us (3%)
  other arithmetic  0.75 us (2%)
    ppermute x9, starting transfers between devices, from_x(): return lax.ppermute(block, 'chan', pairs)  15.4 us
    ppermute x1, starting transfers between devices, local(): lax.ppermute(own, 'chan', [(i, (i + X) % (2 * X)) for i in range(2 * X)])  7.74 us
    ppermute x9, waiting for transfers between devices, from_x(): return lax.ppermute(block, 'chan', pairs)  6.08 us
    ppermute x1, waiting for transfers between devices, local(): off = lax.ppermute(off, ('chan', 'depth'), pairs)  3.49 us
    ppermute x1, starting transfers between devices, local(): off = lax.ppermute(off, ('chan', 'depth'), pairs)  2.38 us
    pallas_call x1, Pallas kernels, local(): pl.pallas_call(near_kernel, out_shape=total, scratch_shapes=[packed], com...  1.99 us
    pallas_call x1, Pallas kernels, local(): pl.pallas_call(far_kernel, out_shape=total, scratch_shapes=[packed], comp...  1.91 us
    pallas_call x2, Pallas kernels, last(): pl.pallas_call(functools.partial(last_kernel, taps), out_shape=[part] * l...  1.34 us
  transfers between devices with their start and end apart: 12, of which 4 were waited for; matrix products, arithmetic and copies ran while one was open for 0% of the time, Pallas kernels for 13%

profile of v11, /device:TPU:1, one launch (start us, length us, event | category | flops | bytes accessed | tf_op | source)
XLA Modules:
  0.0 43.4 jit_solution(2402848023297945993)
XLA Ops:
  0.0 7.7 %collective-permute-start = (f32[512,128]{1,0:T(8,128)}, f32[512,128]{1,0:T(8,128)S(1)}, u32[]{:S(2)}, u32[]{:S(2)}) collective-permute-start(f32[512,128]{1,0:T(8,128)} %bitcast.4), channel_id=1, source_target_pairs={{0,128},{32,160},{64,192},{96,224},{128,0},{160,32},{192,64},{224,... | collective-permute-start | bytes 786440 | tf_op jit(solution)/shard_map/ppermute | solution.py:156
  7.7 2.5 %collective-permute-start.7 = (f32[512,128]{1,0:T(8,128)}, f32[512,128]{1,0:T(8,128)S(1)}, u32[]{:S(2)}, u32[]{:S(2)}) collective-permute-start(f32[512,128]{1,0:T(8,128)} %bitcast.5), channel_id=1, source_target_pairs={{0,96},{32,0},{64,32},{96,64},{128,224},{160,128},{192,160},{224,1... | collective-permute-start | bytes 786440 | tf_op jit(solution)/shard_map/ppermute | solution.py:141
  10.2 0.5 %collective-permute-start.8 = (f32[512,128]{1,0:T(8,128)}, f32[512,128]{1,0:T(8,128)S(1)}, u32[]{:S(2)}, u32[]{:S(2)}) collective-permute-start(f32[512,128]{1,0:T(8,128)} %bitcast.6), channel_id=1, source_target_pairs={{0,64},{32,96},{64,0},{96,32},{128,192},{160,224},{192,128},{224,1... | collective-permute-start | bytes 786440 | tf_op jit(solution)/shard_map/ppermute | solution.py:141
  10.7 0.6 %collective-permute-start.9 = (f32[512,128]{1,0:T(8,128)}, f32[512,128]{1,0:T(8,128)S(1)}, u32[]{:S(2)}, u32[]{:S(2)}) collective-permute-start(f32[512,128]{1,0:T(8,128)} %bitcast.7), channel_id=1, source_target_pairs={{0,32},{32,64},{64,96},{96,0},{128,160},{160,192},{192,224},{224,1... | collective-permute-start | bytes 786440 | tf_op jit(solution)/shard_map/ppermute | solution.py:141
  11.3 0.0 copy-start
  11.3 1.2 %copy-done = f32[3,3,3,32,256]{4,3,2,1,0:T(8,128)S(1)} copy-done((f32[3,3,3,32,256]{4,3,2,1,0:T(8,128)S(1)}, f32[3,3,3,32,256]{4,3,2,1,0:T(8,128)}, u32[]{:S(2)}) %copy-start) | copy-done | bytes 884760
  12.5 0.9 %taps.1 = (bf16[288,1152]{1,0:T(8,128)(2,1)S(1)}, bf16[288,1152]{1,0:T(8,128)(2,1)S(1)}, bf16[288,384]{1,0:T(8,128)(2,1)S(1)}) custom-call(f32[3,3,3,32,256]{4,3,2,1,0:T(8,128)S(1)} %copy-done), custom_call_target="tpu_custom_call" | custom-call | bytes 4000000 | tf_op jit(solution)/shard_map/taps/pallas_call | solution.py:160
  13.4 0.0 copy-start.1
  13.5 0.0 collective-permute-done.whole_ref.s0
  13.5 2.8 %collective-permute-start.1 = (f32[256,128]{1,0:T(8,128)S(1)}, f32[256,128]{1,0:T(8,128)S(1)}, u32[]{:S(2)}, u32[]{:S(2)}) collective-permute-start(f32[256,128]{1,0:T(8,128)S(1)} %get-tuple-element.13), channel_id=1, source_target_pairs={{0,32},{32,64},{64,96},{96,0},{128,160},{160,192},{192,224},{224,1... | collective-permute-start | bytes 393224 | tf_op jit(solution)/shard_map/ppermute | solution.py:141
  16.3 1.4 %collective-permute-start.3 = (f32[256,128]{1,0:T(8,128)S(1)}, f32[256,128]{1,0:T(8,128)S(1)}, u32[]{:S(2)}, u32[]{:S(2)}) collective-permute-start(f32[256,128]{1,0:T(8,128)S(1)} %get-tuple-element.14), channel_id=1, source_target_pairs={{0,96},{32,0},{64,32},{96,64},{128,224},{160,128},{192,160},{224,1... | collective-permute-start | bytes 393224 | tf_op jit(solution)/shard_map/ppermute | solution.py:141
  17.6 0.0 collective-permute-done.7.s1
  17.6 2.1 %collective-permute-start.5 = (f32[256,128]{1,0:T(8,128)S(1)}, f32[256,128]{1,0:T(8,128)S(1)}, u32[]{:S(2)}, u32[]{:S(2)}) collective-permute-start(f32[256,128]{1,0:T(8,128)S(1)} %get-tuple-element.13), channel_id=1, source_target_pairs={{0,96},{32,0},{64,32},{96,64},{128,224},{160,128},{192,160},{224,1... | collective-permute-start | bytes 393224 | tf_op jit(solution)/shard_map/ppermute | solution.py:141
  19.8 0.0 collective-permute-done.8.s2
  19.8 2.8 %collective-permute-start.6 = (f32[256,128]{1,0:T(8,128)S(1)}, f32[256,128]{1,0:T(8,128)S(1)}, u32[]{:S(2)}, u32[]{:S(2)}) collective-permute-start(f32[256,128]{1,0:T(8,128)S(1)} %get-tuple-element.14), channel_id=1, source_target_pairs={{0,32},{32,64},{64,96},{96,0},{128,160},{160,192},{192,224},{224,1... | collective-permute-start | bytes 393224 | tf_op jit(solution)/shard_map/ppermute | solution.py:141
  22.6 3.2 %collective-permute-done.9.s3 = f32[512,128]{1,0:T(8,128)S(1)} collective-permute-done((f32[512,128]{1,0:T(8,128)}, f32[512,128]{1,0:T(8,128)S(1)}, u32[]{:S(2)}, u32[]{:S(2)}) %collective-permute-start.9) | collective-permute-done | bytes 262176 | tf_op jit(solution)/shard_map/ppermute | solution.py:141
  25.8 0.0 copy-done.1
  25.8 2.0 %near.1.near_ref = f32[96,2304]{1,0:T(8,128)S(1)} custom-call(f32[512,128]{1,0:T(8,128)S(1)} %bitcast.8, f32[512,128]{1,0:T(8,128)S(1)} %collective-permute-done.7.s1, f32[512,128]{1,0:T(8,128)S(1)} %collective-permute-done.8.s2, f32[512,128]{1,0:T(8,128)S(1)} %collective-permute-done.9.s3, bf16[288,1152]{1,0:T(8,128)(2,1)S(1)} %get-tuple-element.16.taps_ref), custom_call_target="tpu_custom_call" | custom-call | flops 1358954496 | bytes 3000000 | tf_op jit(solution)/shard_map/near/pallas_call | solution.py:189
  27.8 0.8 %collective-permute-done.1.s3a = f32[256,128]{1,0:T(8,128)S(1)} collective-permute-done((f32[256,128]{1,0:T(8,128)S(1)}, f32[256,128]{1,0:T(8,128)S(1)}, u32[]{:S(2)}, u32[]{:S(2)}) %collective-permute-start.1) | collective-permute-done | bytes 131104 | tf_op jit(solution)/shard_map/ppermute | solution.py:141
  28.6 0.0 collective-permute-start.2
  28.6 0.0 collective-permute-done.3.s1b
  28.6 2.7 %collective-permute-start.4 = (f32[256,128]{1,0:T(8,128)S(1)}, f32[256,128]{1,0:T(8,128)S(1)}, u32[]{:S(2)}, u32[]{:S(2)}) collective-permute-start(f32[256,128]{1,0:T(8,128)S(1)} %collective-permute-done.3.s1b), channel_id=1, source_target_pairs={{0,96},{32,0},{64,32},{96,64},{128,224},{160,128},{192,160},{224,1... | collective-permute-start | bytes 393224 | tf_op jit(solution)/shard_map/ppermute | solution.py:141
  31.3 0.0 collective-permute-done.5.s1a
  31.3 0.0 collective-permute-done.6.s3b
  31.3 1.9 %far.1.before_ref = f32[96,2304]{1,0:T(8,128)S(1)} custom-call(f32[512,128]{1,0:T(8,128)S(1)} %collective-permute-done.whole_ref.s0, f32[256,128]{1,0:T(8,128)S(1)} %collective-permute-done.5.s1a, f32[256,128]{1,0:T(8,128)S(1)} %collective-permute-done.3.s1b, f32[256,128]{1,0:T(8,128)S(1)} %collective-permute-done.1.s3a, ...), custom_call_target="tpu_custom_call" | custom-call | flops 5435817984 | bytes 3000000 | tf_op jit(solution)/shard_map/far/pallas_call | solution.py:197
  33.2 2.1 %collective-permute-done.2.s2a = f32[256,128]{1,0:T(8,128)S(1)} collective-permute-done((f32[256,128]{1,0:T(8,128)S(1)}, f32[256,128]{1,0:T(8,128)S(1)}, u32[]{:S(2)}, u32[]{:S(2)}) %collective-permute-start.2) | collective-permute-done | bytes 131104 | tf_op jit(solution)/shard_map/ppermute | solution.py:141
  35.3 0.0 collective-permute-done.4.s2b
  35.3 0.6 %off.1 = f32[512,128]{1,0:T(8,128)S(1)} custom-call(f32[256,128]{1,0:T(8,128)S(1)} %collective-permute-done.2.s2a, f32[256,128]{1,0:T(8,128)S(1)} %collective-permute-done.4.s2b, bf16[288,384]{1,0:T(8,128)(2,1)S(1)} %get-tuple-element.12.order_ref.taps_ref, f32[96,2304]{1,0:T(8,128)S(1)} %far.1.before_ref), custom_call_target="tpu_custom_call" | custom-call | flops 113246208 | bytes 3000000 | tf_op jit(solution)/shard_map/off/pallas_call | solution.py:208
  35.9 2.4 %collective-permute-start.10 = (f32[512,128]{1,0:T(8,128)S(1)}, f32[512,128]{1,0:T(8,128)S(1)}, u32[]{:S(2)}, u32[]{:S(2)}) collective-permute-start(f32[512,128]{1,0:T(8,128)S(1)} %off.1), channel_id=1, source_target_pairs={{1,2},{2,1},{3,4},{4,3},{5,6},{6,5},{7,8},{8,7},{9,10},{10,9},{11,... | collective-permute-start | bytes 786440 | tf_op jit(solution)/shard_map/ppermute | solution.py:229
  38.3 0.7 %rest.1 = (f32[512,128]{1,0:T(8,128)S(1)}, f32[512,128]{1,0:T(8,128)S(1)}) custom-call(f32[256,128]{1,0:T(8,128)S(1)} %collective-permute-done.2.s2a, f32[256,128]{1,0:T(8,128)S(1)} %collective-permute-done.4.s2b, bf16[288,384]{1,0:T(8,128)(2,1)S(1)} %get-tuple-element.12.order_ref.taps_ref, f32[96,2304]{1,0:T(8,128)S(1)} %far.1.before_ref), custom_call_target="tpu_custom_call" | custom-call | flops 226492416 | bytes 3000000 | tf_op jit(solution)/shard_map/rest/pallas_call | solution.py:208
  39.0 0.1 collective-permute-start.11
  39.1 3.5 %collective-permute-done.10 = f32[512,128]{1,0:T(8,128)S(1)} collective-permute-done((f32[512,128]{1,0:T(8,128)S(1)}, f32[512,128]{1,0:T(8,128)S(1)}, u32[]{:S(2)}, u32[]{:S(2)}) %collective-permute-start.10) | collective-permute-done | bytes 262176 | tf_op jit(solution)/shard_map/ppermute | solution.py:229
  42.6 0.0 collective-permute-done.11
  42.6 0.8 %add_add_fusion = f32[512,128]{1,0:T(8,128)} fusion(f32[512,128]{1,0:T(8,128)S(1)} %collective-permute-done.11, f32[512,128]{1,0:T(8,128)S(1)} %get-tuple-element.17, f32[512,128]{1,0:T(8,128)S(1)} %collective-permute-done.10), kind=kLoop, calls=%fused_computation | loop fusion | flops 131072 | bytes 1048576 | tf_op jit(solution)/shard_map/add | solution.py:231
  (1 shorter events, 0.0 us)
Async XLA Ops:
  0.0 13.5 %collective-permute-start = (f32[512,128]{1,0:T(8,128)}, f32[512,128]{1,0:T(8,128)S(1)}, u32[]{:S(2)}, u32[]{:S(2)}) collective-permute-start(f32[512,128]{1,0:T(8,128)} %bitcast.4), channel_id=1, source_target_pairs={{0,128},{32,160},{64,192},{96,224},{128,0},{160,32},{192,64},{224,... | collective-permute-start | bytes 786440 | tf_op jit(solution)/shard_map/ppermute | solution.py:156
  7.7 9.9 %collective-permute-start.7 = (f32[512,128]{1,0:T(8,128)}, f32[512,128]{1,0:T(8,128)S(1)}, u32[]{:S(2)}, u32[]{:S(2)}) collective-permute-start(f32[512,128]{1,0:T(8,128)} %bitcast.5), channel_id=1, source_target_pairs={{0,96},{32,0},{64,32},{96,64},{128,224},{160,128},{192,160},{224,1... | collective-permute-start | bytes 786440 | tf_op jit(solution)/shard_map/ppermute | solution.py:141
  10.2 9.6 %collective-permute-start.8 = (f32[512,128]{1,0:T(8,128)}, f32[512,128]{1,0:T(8,128)S(1)}, u32[]{:S(2)}, u32[]{:S(2)}) collective-permute-start(f32[512,128]{1,0:T(8,128)} %bitcast.6), channel_id=1, source_target_pairs={{0,64},{32,96},{64,0},{96,32},{128,192},{160,224},{192,128},{224,1... | collective-permute-start | bytes 786440 | tf_op jit(solution)/shard_map/ppermute | solution.py:141
  10.7 15.0 %collective-permute-start.9 = (f32[512,128]{1,0:T(8,128)}, f32[512,128]{1,0:T(8,128)S(1)}, u32[]{:S(2)}, u32[]{:S(2)}) collective-permute-start(f32[512,128]{1,0:T(8,128)} %bitcast.7), channel_id=1, source_target_pairs={{0,32},{32,64},{64,96},{96,0},{128,160},{160,192},{192,224},{224,1... | collective-permute-start | bytes 786440 | tf_op jit(solution)/shard_map/ppermute | solution.py:141
  11.3 1.2 %copy-start = (f32[3,3,3,32,256]{4,3,2,1,0:T(8,128)S(1)}, f32[3,3,3,32,256]{4,3,2,1,0:T(8,128)}, u32[]{:S(2)}) copy-start(f32[3,3,3,32,256]{4,3,2,1,0:T(8,128)} %kernel_ref.1) | copy-start | bytes 2654212
  13.4 12.3 %copy-start.1 = (f32[32,1,16,128]{3,2,1,0:T(8,128)S(1)}, f32[32,1,16,128]{3,2,1,0:T(8,128)}, u32[]{:S(2)}) copy-start(f32[32,1,16,128]{3,2,1,0:T(8,128)} %param.2) | copy-start | bytes 786436
  13.5 15.1 %collective-permute-start.1 = (f32[256,128]{1,0:T(8,128)S(1)}, f32[256,128]{1,0:T(8,128)S(1)}, u32[]{:S(2)}, u32[]{:S(2)}) collective-permute-start(f32[256,128]{1,0:T(8,128)S(1)} %get-tuple-element.13), channel_id=1, source_target_pairs={{0,32},{32,64},{64,96},{96,0},{128,160},{160,192},{192,224},{224,1... | collective-permute-start | bytes 393224 | tf_op jit(solution)/shard_map/ppermute | solution.py:141
  16.3 12.3 %collective-permute-start.3 = (f32[256,128]{1,0:T(8,128)S(1)}, f32[256,128]{1,0:T(8,128)S(1)}, u32[]{:S(2)}, u32[]{:S(2)}) collective-permute-start(f32[256,128]{1,0:T(8,128)S(1)} %get-tuple-element.14), channel_id=1, source_target_pairs={{0,96},{32,0},{64,32},{96,64},{128,224},{160,128},{192,160},{224,1... | collective-permute-start | bytes 393224 | tf_op jit(solution)/shard_map/ppermute | solution.py:141
  17.6 13.6 %collective-permute-start.5 = (f32[256,128]{1,0:T(8,128)S(1)}, f32[256,128]{1,0:T(8,128)S(1)}, u32[]{:S(2)}, u32[]{:S(2)}) collective-permute-start(f32[256,128]{1,0:T(8,128)S(1)} %get-tuple-element.13), channel_id=1, source_target_pairs={{0,96},{32,0},{64,32},{96,64},{128,224},{160,128},{192,160},{224,1... | collective-permute-start | bytes 393224 | tf_op jit(solution)/shard_map/ppermute | solution.py:141
  19.8 11.5 %collective-permute-start.6 = (f32[256,128]{1,0:T(8,128)S(1)}, f32[256,128]{1,0:T(8,128)S(1)}, u32[]{:S(2)}, u32[]{:S(2)}) collective-permute-start(f32[256,128]{1,0:T(8,128)S(1)} %get-tuple-element.14), channel_id=1, source_target_pairs={{0,32},{32,64},{64,96},{96,0},{128,160},{160,192},{192,224},{224,1... | collective-permute-start | bytes 393224 | tf_op jit(solution)/shard_map/ppermute | solution.py:141
  28.6 6.7 %collective-permute-start.2 = (f32[256,128]{1,0:T(8,128)S(1)}, f32[256,128]{1,0:T(8,128)S(1)}, u32[]{:S(2)}, u32[]{:S(2)}) collective-permute-start(f32[256,128]{1,0:T(8,128)S(1)} %collective-permute-done.1.s3a), channel_id=1, source_target_pairs={{0,32},{32,64},{64,96},{96,0},{128,160},{160,192},{192,224},{224,1... | collective-permute-start | bytes 393224 | tf_op jit(solution)/shard_map/ppermute | solution.py:141
  28.6 6.7 %collective-permute-start.4 = (f32[256,128]{1,0:T(8,128)S(1)}, f32[256,128]{1,0:T(8,128)S(1)}, u32[]{:S(2)}, u32[]{:S(2)}) collective-permute-start(f32[256,128]{1,0:T(8,128)S(1)} %collective-permute-done.3.s1b), channel_id=1, source_target_pairs={{0,96},{32,0},{64,32},{96,64},{128,224},{160,128},{192,160},{224,1... | collective-permute-start | bytes 393224 | tf_op jit(solution)/shard_map/ppermute | solution.py:141
  35.9 6.7 %collective-permute-start.10 = (f32[512,128]{1,0:T(8,128)S(1)}, f32[512,128]{1,0:T(8,128)S(1)}, u32[]{:S(2)}, u32[]{:S(2)}) collective-permute-start(f32[512,128]{1,0:T(8,128)S(1)} %off.1), channel_id=1, source_target_pairs={{1,2},{2,1},{3,4},{4,3},{5,6},{6,5},{7,8},{8,7},{9,10},{10,9},{11,... | collective-permute-start | bytes 786440 | tf_op jit(solution)/shard_map/ppermute | solution.py:229
  39.0 3.6 %collective-permute-start.11 = (f32[512,128]{1,0:T(8,128)S(1)}, f32[512,128]{1,0:T(8,128)S(1)}, u32[]{:S(2)}, u32[]{:S(2)}) collective-permute-start(f32[512,128]{1,0:T(8,128)S(1)} %get-tuple-element.18), channel_id=1, source_target_pairs={{0,1},{2,3},{4,5},{6,7},{8,9},{10,11},{12,13},{14,15},{16,17},{18,... | collective-permute-start | bytes 786440 | tf_op jit(solution)/shard_map/ppermute | solution.py:230
